TPU v7x, 32 devices: a whole 2x2x4 slice. The times are simulated.
32 devices in a mesh: row: 8 (over y, x, core), col: 4 (over z).
Axes of the slice: x: 2, y: 2, z: 4, core: 2. Of those that a mesh axis runs over, the one named last changes fastest.
Arguments:
- amplitudes: bfloat16 [2, 2048, 2048], P(None, 'row', 'col'), may hold values from -6 to 6
- factor: bfloat16 [2048, 4096], P('row', 'col'), may hold values from -0.125 to 0.125
- kernel: float32 [4096, 4096], P('row', 'col'), may hold values from -6 to 6
Outputs:
- ladder: bfloat16 [2, 2048, 2048], P(None, 'row', 'col')
All inputs are finite; a program needn't handle non-finite values.
Results may differ from a plain program's by a relative error of at most 0.015.
Values may be sent and summed in bfloat16 or wider, within the bound.
No kernel may reach another device: no remote copies, remote signals or barrier semaphores. Data moves between devices by JAX's collectives and lax.ppermute only.
A program may use at most 64 MiB of HBM per device.

v0:
```python
import jax
import jax.numpy as jnp
from jax import lax
from jax.sharding import PartitionSpec as P


def per_device(amplitudes, factor, kernel):
    factor_cols = lax.all_gather(factor, "row", axis=0, tiled=True)
    factor_rows = lax.all_gather(factor, "col", axis=1, tiled=True)
    factor_first = lax.all_to_all(factor_rows, "row", split_axis=1, concat_axis=0, tiled=True)
    factor_part = factor_cols
    projected = jnp.einsum(
        "pak,kq->paq",
        lax.all_gather(amplitudes, "col", axis=2, tiled=True),
        factor_part,
        preferred_element_type=jnp.float32,
    ).astype(jnp.bfloat16)
    factor_part = factor_first
    grid_pairs = jnp.einsum(
        "kp,nkq->npq",
        factor_part,
        lax.all_gather(projected, "row", axis=1, tiled=True),
        preferred_element_type=jnp.float32,
    )
    scaled = (kernel[None] * grid_pairs).astype(jnp.bfloat16)
    factor_part = factor_cols
    half_back = lax.psum_scatter(
        jnp.einsum("bq,npq->bnp", factor_part, scaled, preferred_element_type=jnp.float32).astype(
            jnp.bfloat16
        ),
        "col",
        scatter_dimension=0,
        tiled=True,
    ).astype(jnp.float32)
    half_back = half_back.astype(jnp.bfloat16)
    factor_part = factor_rows
    result = jnp.einsum(
        "ak,bnk->nab",
        factor_part,
        lax.all_gather(half_back, "row", axis=2, tiled=True),
        preferred_element_type=jnp.float32,
    )
    return result.astype(jnp.bfloat16)


def solution(mesh):
    placed = (P(None, "row", "col"), P("row", "col"), P("row", "col"))
    return jax.shard_map(
        per_device, mesh=mesh, in_specs=placed, out_specs=P(None, "row", "col"), check_vma=False
    )
```

profile of v0, /device:TPU:0, one launch (start us, length us, event | category | flops | bytes accessed | tf_op | source)
XLA Modules:
  0.0 378.0 jit_solution(17484808536219745371)
XLA Ops:
  6.5 0.0 all-gather.6.cloned.1.call-start
  6.5 0.7 all-gather.6.cloned.1.call-update
  7.3 0.0 all-gather.8.cloned.1.call-start
  7.3 0.7 all-gather.8.cloned.1.call-update
  8.0 0.0 all-gather.12.cloned.1.call-start
  8.1 0.7 all-gather.12.cloned.1.call-update
  8.7 0.0 all-gather.10.cloned.1.call-start
  8.8 48.8 %all-gather.6.cloned.1.call-done = bf16[2,256,2048]{2,1,0:T(8,128)(2,1)} async-done(((bf16[2,256,512]{2,1,0:T(8,128)(2,1)}), bf16[2,256,2048]{2,1,0:T(8,128)(2,1)}) %all-gather.6.cloned.1.call-update) | async-done | bytes 2097168 | tf_op jit(solution)/shard_map/all_gather | solution.py:14
  57.6 37.4 %all-gather.8.cloned.1.call-done = bf16[2048,1024]{1,0:T(8,128)(2,1)} async-done(((bf16[256,1024]{1,0:T(8,128)(2,1)}), bf16[2048,1024]{1,0:T(8,128)(2,1)}) %all-gather.8.cloned.1.call-update) | async-done | bytes 4194320 | tf_op jit(solution)/shard_map/all_gather | solution.py:8
  94.9 6.1 %fusion.9 = bf16[2,256,1024]{2,1,0:T(8,128)(2,1)} fusion(bf16[2,256,2048]{2,1,0:T(8,128)(2,1)} %all-gather.6.cloned.1.call-done, bf16[2048,1024]{1,0:T(8,128)(2,1)} %all-gather.8.cloned.1.call-done), kind=kOutput, calls=%fused_computation.10 | convolution fusion | flops 2148007936 | bytes 7340032 | tf_op jit(solution)/shard_map/pak,kq->paq/dot_general | solution.py:12
  101.1 0.0 all-gather.10.cloned.1.call-update
  101.1 0.0 reduce-scatter.2.cloned.1.call-start
  101.2 41.3 %all-gather.12.cloned.1.call-done = bf16[256,4096]{1,0:T(8,128)(2,1)} async-done(((bf16[256,1024]{1,0:T(8,128)(2,1)}), bf16[256,4096]{1,0:T(8,128)(2,1)}) %all-gather.12.cloned.1.call-update) | async-done | bytes 2097168 | tf_op jit(solution)/shard_map/all_gather | solution.py:9
  142.5 1.8 copy.9
  144.3 41.3 %all_to_all.19 = bf16[256,8,512]{2,0,1:T(8,128)(2,1)S(1)} all-to-all(bf16[256,8,512]{2,0,1:T(8,128)(2,1)S(1)} %bitcast.50), channel_id=1, replica_groups=mesh['row'=8,'col'=4] {'row'}, dimensions={1} | all-to-all | bytes 4194304 | tf_op jit(solution)/shard_map/all_to_all | solution.py:10
  185.6 29.1 %all-gather.10.cloned.1.call-done = bf16[2,2048,1024]{2,1,0:T(8,128)(2,1)} async-done(((bf16[2,256,1024]{2,1,0:T(8,128)(2,1)}), bf16[2,2048,1024]{2,1,0:T(8,128)(2,1)}) %all-gather.10.cloned.1.call-update) | async-done | bytes 8388624 | tf_op jit(solution)/shard_map/all_gather | solution.py:22
  214.6 14.5 %convert_bitcast_fusion = bf16[2048,2,512]{2,0,1:T(8,128)(2,1)} fusion(bf16[2048,1024]{1,0:T(8,128)(2,1)} %all-gather.8.cloned.1.call-done, bf16[2,2048,1024]{2,1,0:T(8,128)(2,1)} %all-gather.10.cloned.1.call-done, bf16[2048,512,1]{1,0,2:T(8,128)(2,1)S(1)} %bitcast.52, f32[512,1024]{1,0:T(8,128)} %param.5), kind=kOutput, calls=%fused_computation.6 | convolution fusion | flops 8594128896 | bytes 20971520 | tf_op jit(solution)/shard_map/bq,npq->bnp/dot_general | solution.py:28
  229.1 0.0 copy-start
  229.1 0.0 reduce-scatter.2.cloned.1.call-update
  229.1 0.0 all-gather.14.cloned.1.call-start
  229.2 76.9 %reduce-scatter.2.cloned.1.call-done = bf16[512,2,512]{2,0,1:T(8,128)(2,1)} async-done(((bf16[2048,2,512]{2,0,1:T(8,128)(2,1)}), bf16[512,2,512]{2,0,1:T(8,128)(2,1)}) %reduce-scatter.2.cloned.1.call-update) | async-done | bytes 1048592 | tf_op jit(solution)/shard_map/reduce_scatter | solution.py:27
  306.0 0.0 all-gather.14.cloned.1.call-update
  306.1 58.4 %all-gather.14.cloned.1.call-done = bf16[512,2,4096]{2,0,1:T(8,128)(2,1)} async-done(((bf16[512,2,512]{2,0,1:T(8,128)(2,1)}), bf16[512,2,4096]{2,0,1:T(8,128)(2,1)}) %all-gather.14.cloned.1.call-update) | async-done | bytes 8388624 | tf_op jit(solution)/shard_map/all_gather | solution.py:40
  364.4 0.0 copy-done
  364.4 5.7 %fusion.15 = bf16[2,256,512]{1,2,0:T(8,128)(2,1)S(1)} fusion(bf16[512,2,4096]{2,0,1:T(8,128)(2,1)} %all-gather.14.cloned.1.call-done, bf16[256,4096]{1,0:T(8,128)(2,1)S(1)} %copy-done), kind=kOutput, calls=%fused_computation.12 | convolution fusion | flops 2147745792 | bytes 11010048 | tf_op jit(solution)/shard_map/ak,bnk->nab/dot_general | solution.py:37
  370.2 1.0 copy.6
Async XLA Ops:
  6.5 51.1 %all-gather.6.cloned.1.call-start = ((), (), s32[]{:S(2)}) async-start(), calls=%async_computation.2 | async-start | bytes 2621440 | tf_op jit(solution)/shard_map/all_gather | solution.py:14
  7.3 87.7 %all-gather.8.cloned.1.call-start = ((), (), s32[]{:S(2)}) async-start(), calls=%async_computation.3 | async-start | bytes 4718592 | tf_op jit(solution)/shard_map/all_gather | solution.py:8
  8.0 134.5 %all-gather.12.cloned.1.call-start = ((), (), s32[]{:S(2)}) async-start(), calls=%async_computation.5 | async-start | bytes 2621440 | tf_op jit(solution)/shard_map/all_gather | solution.py:9
  8.7 205.9 %all-gather.10.cloned.1.call-start = ((), (), s32[]{:S(2)}) async-start(), calls=%async_computation.4 | async-start | bytes 9437184 | tf_op jit(solution)/shard_map/all_gather | solution.py:22
  101.1 204.9 %reduce-scatter.2.cloned.1.call-start = ((), (), s32[]{:S(2)}) async-start(), calls=%async_computation.6 | async-start | bytes 5242880 | tf_op jit(solution)/shard_map/reduce_scatter | solution.py:27
  229.1 135.4 %copy-start = (bf16[256,4096]{1,0:T(8,128)(2,1)S(1)}, bf16[256,4096]{1,0:T(8,128)(2,1)}, u32[]{:S(2)}) copy-start(bf16[256,4096]{1,0:T(8,128)(2,1)} %all-gather.12.cloned.1.call-done) | copy-start | bytes 6291460
  229.1 135.3 %all-gather.14.cloned.1.call-start = ((), (), s32[]{:S(2)}) async-start(), calls=%async_computation.7 | async-start | bytes 9437184 | tf_op jit(solution)/shard_map/all_gather | solution.py:40
Sparse Core Ops, SparseCore 0:
  8.9 48.6 all-gather.5
  59.5 35.4 all-gather.7
  96.5 45.9 all-gather.11
  144.3 70.3 all-gather.9
  229.2 76.7 reduce-scatter.1
  307.9 56.4 all-gather.13
where the time goes:
time: 378 us
  waiting for transfers between devices  294 us (78%)
  blocking collectives  41.3 us (11%)
  matrix products  26.4 us (7%)
  between operations  13.5 us (4%)
    reduce_scatter x1, waiting for transfers between devices, per_device(): lax.psum_scatter(jnp.einsum('bq,npq->bnp', factor_part, scaled, preferred...  76.9 us
    all_gather x1, waiting for transfers between devices, per_device(): lax.all_gather(half_back, 'row', axis=2, tiled=True)  58.4 us
    all_gather x1, waiting for transfers between devices, per_device(): lax.all_gather(amplitudes, 'col', axis=2, tiled=True)  48.8 us
    all_gather x1, waiting for transfers between devices, per_device(): factor_rows = lax.all_gather(factor, 'col', axis=1, tiled=True)  41.3 us
    all_to_all x1, blocking collectives, per_device(): lax.all_to_all(factor_rows, 'row', split_axis=1, concat_axis=0, tiled=True)  41.3 us
    all_gather x1, waiting for transfers between devices, per_device(): factor_cols = lax.all_gather(factor, 'row', axis=0, tiled=True)  37.4 us
    all_gather x1, waiting for transfers between devices, per_device(): lax.all_gather(projected, 'row', axis=1, tiled=True)  29.1 us
    dot_general x1, matrix products, per_device(): jnp.einsum('bq,npq->bnp', factor_part, scaled, preferred_element_type=jnp...  14.5 us
  transfers between devices with their start and end apart: 6, of which 6 were waited for; matrix products, arithmetic and copies ran while one was open for 2% of the time, Pallas kernels for 0%

commit v1 on v0

v1 whole, which is shorter than its diff:
```python
import functools

import jax
import jax.numpy as jnp
from jax import lax
from jax.experimental import pallas as pl
from jax.experimental.pallas import tpu as pltpu
from jax.sharding import PartitionSpec as P

BF16 = jnp.bfloat16
F32 = jnp.float32
ANY = pl.BlockSpec(memory_space=pltpu.HBM)


def flipped(value, bits):
    total = 0
    for t in range(bits):
        total = total + (((value >> t) & 1) << (bits - 1 - t))
    return total


def params(vmem):
    return pltpu.CompilerParams(vmem_limit_bytes=vmem)


def where_am_i(bits):
    row, col = lax.axis_index("row"), lax.axis_index("col")
    core, chip = lax.rem(row, 2), row // 2
    offset = chip ^ col
    base = jnp.where(core == 0, offset, flipped(offset, bits))
    return core, base


def copy_all(pairs, sems):
    copies = [pltpu.make_async_copy(a, b, sems.at[s]) for s, (a, b) in enumerate(pairs)]
    for copy in copies:
        copy.start()
    return copies


def plane_pairs(own, other, room, core, rows, bits):
    pairs = []
    for j, ref in enumerate(own):
        pairs.append((ref, room.at[pl.ds((2 * j + core) * rows, rows)]))
    for j, ref in enumerate(other):
        pairs.append((ref, room.at[pl.ds((2 * flipped(j, bits) + 1 - core) * rows, rows)]))
    return pairs


def project_kernel(bits, *refs):
    n = 1 << bits
    terms, own, other = refs[:n], refs[n : 2 * n], refs[2 * n : 3 * n]
    out, held, room, total, sems = refs[3 * n :]
    core, base = where_am_i(bits)
    rows, width = own[0].shape
    depth = terms[0].shape[1]
    pairs = [(terms[l], held.at[l]) for l in range(n)] + plane_pairs(own, other, room, core, rows, bits)
    for copy in copy_all(pairs, sems):
        copy.wait()
    tile = min(width, 512)

    @pl.loop(0, width // tile)
    def _(step):
        at = pl.ds(pl.multiple_of(step * tile, tile), tile)
        acc = jnp.zeros((out.shape[0], tile), F32)
        for l in range(n):
            start = pl.multiple_of((base ^ l) * depth, depth)
            acc = acc + jnp.dot(held[l], room[pl.ds(start, depth), at], preferred_element_type=F32)
        total[:, at] = acc.astype(BF16)

    copy = pltpu.make_async_copy(total, out, sems.at[0])
    copy.start()
    copy.wait()


def project(terms, own, other, bits):
    n = len(terms)
    m, depth = terms[0].shape
    rows, width = own[0].shape
    return pl.pallas_call(
        functools.partial(project_kernel, bits),
        out_shape=jax.ShapeDtypeStruct((m, width), BF16),
        in_specs=[ANY] * (3 * n),
        out_specs=ANY,
        scratch_shapes=[
            pltpu.VMEM((n, m, depth), BF16),
            pltpu.VMEM((2 * n * rows, width), BF16),
            pltpu.VMEM((m, width), BF16),
            pltpu.SemaphoreType.DMA((3 * n,)),
        ],
        compiler_params=params(32 << 20),
        cost_estimate=pl.CostEstimate(flops=2 * m * n * depth * width, bytes_accessed=2 * n * (m * depth + 2 * rows * width), transcendentals=0),
        name="project",
    )(*terms, *own, *other)


def grid_kernel(bits, *refs):
    n = 1 << bits
    first, second = refs[:n], refs[n : 2 * n]
    own, other = refs[2 * n : 3 * n], refs[3 * n : 4 * n]
    kernel_own, kernel_other = refs[4 * n : 4 * n + 2]
    outs = refs[4 * n + 2 : 6 * n + 2]
    proj, room, coulomb, scaled, back, sems, out_sems = refs[6 * n + 2 :]
    core, _ = where_am_i(bits)
    rows, width = own[0].shape
    half = kernel_own.shape[0]
    pairs = []
    for j in range(n):
        pairs.append((own[j], room.at[pl.ds(2 * j * rows, rows)]))
        pairs.append((other[flipped(j, bits)], room.at[pl.ds((2 * j + 1) * rows, rows)]))
        pairs.append((first[j], proj.at[pl.ds(2 * j * rows, rows)]))
        pairs.append((second[j], proj.at[pl.ds((2 * j + 1) * rows, rows)]))
    pairs.append((kernel_own, coulomb.at[pl.ds(core * half, half)]))
    pairs.append((kernel_other, coulomb.at[pl.ds((1 - core) * half, half)]))
    for copy in copy_all(pairs, sems):
        copy.wait()
    tile = min(proj.shape[1], 256)

    @pl.loop(0, proj.shape[1] // tile)
    def _(step):
        at = pl.ds(pl.multiple_of(step * tile, tile), tile)
        grid = lax.dot_general(room[...], proj[:, at], (((0,), (0,)), ((), ())), preferred_element_type=F32)
        scaled[:, at] = (coulomb[:, at] * grid).astype(BF16)

    copies = []
    for h in (1, 0):
        for j in range(n - 1, -1, -1):
            at = pl.ds((2 * j + h) * rows, rows)
            back[at, :] = jnp.dot(room[at, :], scaled[...], preferred_element_type=F32).astype(BF16)
            copy = pltpu.make_async_copy(back.at[at], outs[h * n + j], out_sems.at[h * n + j])
            copy.start()
            copies.append(copy)
    for copy in copies:
        copy.wait()


def grid(first, second, own, other, kernel_own, kernel_other, bits):
    n = len(first)
    rows, width = own[0].shape
    cols = first[0].shape[1]
    outs = pl.pallas_call(
        functools.partial(grid_kernel, bits),
        out_shape=[jax.ShapeDtypeStruct((rows, cols), BF16)] * (2 * n),
        in_specs=[ANY] * (4 * n + 2),
        out_specs=[ANY] * (2 * n),
        scratch_shapes=[
            pltpu.VMEM((2 * n * rows, cols), BF16),
            pltpu.VMEM((2 * n * rows, width), BF16),
            pltpu.VMEM((width, cols), F32),
            pltpu.VMEM((width, cols), BF16),
            pltpu.VMEM((2 * n * rows, cols), BF16),
            pltpu.SemaphoreType.DMA((4 * n + 2,)),
            pltpu.SemaphoreType.DMA((2 * n,)),
        ],
        compiler_params=params(48 << 20),
        cost_estimate=pl.CostEstimate(flops=8 * n * rows * width * cols, bytes_accessed=12 * n * rows * cols + 4 * width * cols, transcendentals=0),
        name="grid",
    )(*first, *second, *own, *other, kernel_own, kernel_other)
    return list(outs[:n]), list(outs[n:])


def back_kernel(bits, *refs):
    n = 1 << bits
    q = bits + 1
    parts, own, other = refs[:q], refs[q : q + n], refs[q + n : q + 2 * n]
    outs = refs[q + 2 * n : q + 3 * n]
    given, room, results, sems, out_sems = refs[q + 3 * n :]
    core, base = where_am_i(bits)
    rows, width = own[0].shape
    depth = outs[0].shape[1]
    pairs = [(parts[i], given.at[i]) for i in range(q)] + plane_pairs(own, other, room, core, rows, bits)
    for copy in copy_all(pairs, sems):
        copy.wait()
    left = total([given[i] for i in range(q)])
    copies = []
    for l in range(n - 1, -1, -1):
        right = room[pl.ds(pl.multiple_of((base ^ l) * depth, depth), depth), :]
        results[l] = lax.dot_general(left, right, (((1,), (1,)), ((), ())), preferred_element_type=F32).astype(BF16)
        copy = pltpu.make_async_copy(results.at[l], outs[l], out_sems.at[l])
        copy.start()
        copies.append(copy)
    for copy in copies:
        copy.wait()


def back(parts, own, other, bits):
    n, q = len(own), len(parts)
    rows, width = own[0].shape
    m, depth = parts[0].shape[0], 2 * rows
    outs = pl.pallas_call(
        functools.partial(back_kernel, bits),
        out_shape=[jax.ShapeDtypeStruct((m, depth), BF16)] * n,
        in_specs=[ANY] * (q + 2 * n),
        out_specs=[ANY] * n,
        scratch_shapes=[
            pltpu.VMEM((q, m, width), BF16),
            pltpu.VMEM((2 * n * rows, width), BF16),
            pltpu.VMEM((n, m, depth), BF16),
            pltpu.SemaphoreType.DMA((q + 2 * n,)),
            pltpu.SemaphoreType.DMA((n,)),
        ],
        compiler_params=params(32 << 20),
        cost_estimate=pl.CostEstimate(flops=2 * m * n * depth * width, bytes_accessed=2 * n * (m * depth + 2 * rows * width), transcendentals=0),
        name="back",
    )(*parts, *own, *other)
    return list(outs)


def pick_kernel(bits, *refs):
    n = 1 << bits
    blocks, outs, (room, sems) = refs[:n], refs[n : 2 * n], refs[2 * n :]
    _, base = where_am_i(bits)
    for copy in copy_all([(blocks[l], room.at[l]) for l in range(n)], sems):
        copy.wait()
    for copy in copy_all([(room.at[base ^ j], outs[j]) for j in range(n)], sems):
        copy.wait()


def pick(blocks, bits):
    n = len(blocks)
    return pl.pallas_call(
        functools.partial(pick_kernel, bits),
        out_shape=[jax.ShapeDtypeStruct(blocks[0].shape, BF16)] * n,
        in_specs=[ANY] * n,
        out_specs=[ANY] * n,
        scratch_shapes=[pltpu.VMEM((n, *blocks[0].shape), BF16), pltpu.SemaphoreType.DMA((n,))],
        compiler_params=params(16 << 20),
        cost_estimate=pl.CostEstimate(flops=0, bytes_accessed=4 * n * blocks[0].size, transcendentals=0),
        name="pick",
    )(*blocks)


def total(parts):
    return sum(part.astype(F32) for part in parts).astype(BF16)


def after(value, *others):
    return lax.optimization_barrier((value, *others))[0]


def per_device(rows, cols, amplitudes, factor, kernel):
    chips = rows // 2
    bits = chips.bit_length() - 1
    core = lax.rem(lax.axis_index("row"), 2)

    def bit_of(step, row):
        return step if row % 2 == 0 else bits - 1 - step

    def swap(value):
        return lax.ppermute(value, "row", [(r, r ^ 1) for r in range(rows)])

    def to_plane(mask):
        def send(value):
            return lax.ppermute(value, "row", [(r, r ^ (2 * (mask if r % 2 == 0 else flipped(mask, bits)))) for r in range(rows)])

        return send

    def to_line(step):
        def send(value):
            pairs = []
            for r in range(rows):
                for c in range(cols):
                    pairs.append((r * cols + c, r * cols + (c ^ (1 << bit_of(step, r)))))
            return lax.ppermute(value, ("row", "col"), pairs)

        return send

    plane = [to_plane(1 << t) for t in range(bits)]
    line = [to_line(t) for t in range(bits)]

    def gather(block, sends, gates=()):
        blocks = [block]
        for t, send in enumerate(sends):
            first = after(block, gates[t]) if t < len(gates) else block
            blocks = blocks + [send(b) for b in [first] + blocks[1:]]
        return blocks

    def scatter(blocks, sends, gate=None):
        parts, marks = [], []
        for t in range(len(sends) - 1, -1, -1):
            n = 1 << t
            away = blocks[n:]
            if gate is not None and not marks:
                away = [after(block, gate) for block in away]
            got = [sends[t](block) for block in away]
            marks.append(got[-1])
            parts.append(got[0])
            blocks = [blocks[0]] + [total([blocks[j], got[j]]) for j in range(1, n)]
        return [blocks[0], *parts], marks[0]

    middle = 1 << (bits - 1)
    mine = lax.dynamic_index_in_dim(amplitudes, core, 0, keepdims=False)
    theirs = lax.dynamic_index_in_dim(amplitudes, 1 - core, 0, keepdims=False)

    line_own = gather(factor, line)
    cols_own = gather(factor, plane)
    kernel_other = swap(kernel)
    second = swap(theirs)
    cols_other = [swap(b) for b in cols_own]
    terms0 = gather(mine, line, [line_own[middle], line_own[-1]])
    terms1 = gather(second, line, [terms0[middle], terms0[-1]])

    pieces = pick(line_own, bits)
    first_own = [pieces[0]] + [to_plane(j)(pieces[j]) for j in range(1, chips)]
    first_other = [swap(b) for b in first_own]

    proj0 = gather(project(terms0, cols_own, cols_other, bits), plane)
    proj1 = gather(project(terms1, cols_own, cols_other, bits), plane)

    z0, z1 = grid(proj0, proj1, first_own, first_other, kernel, kernel_other, bits)
    s1, mark = scatter(z1, plane)
    s0, _ = scatter(z0, plane, mark)
    o1 = back(s1, cols_own, cols_other, bits)
    o0 = back(s0, cols_own, cols_other, bits)
    t1, mark = scatter(o1, line)
    t0, _ = scatter(o0, line, mark)

    away = swap(total(t1))
    here = total(t0)
    return jnp.where(core == 0, jnp.stack([here, away]), jnp.stack([away, here]))


def solution(mesh):
    placed = (P(None, "row", "col"), P("row", "col"), P("row", "col"))
    rows, cols = mesh.shape["row"], mesh.shape["col"]
    return jax.shard_map(
        functools.partial(per_device, rows, cols), mesh=mesh, in_specs=placed, out_specs=P(None, "row", "col"), check_vma=False
    )
```

time: 378 us -> 231 us (0.61)
  waiting for transfers between devices: 294 us -> 149 us
  starting transfers between devices: 0.2 us -> 49.7 us
  blocking collectives: 41.3 us -> 0 us
  matrix products: 26.4 us -> 0 us
  Pallas kernels: 0 us -> 26.3 us
  between operations: 13.5 us -> 0.43 us
    all_gather x5 -> x0, waiting for transfers between devices: 215 us -> none  [the longest x1 58.4 us: per_device(): lax.all_gather(half_back, 'row', axis=2, tiled=True)]
    ppermute x0 -> x44, waiting for transfers between devices: none -> 149 us  [the longest x18 75.3 us: send(): lax.ppermute(value, 'row', [(r, r ^ 2 * (mask if r % 2 == 0 else flipped(...]
    reduce_scatter x1 -> x0, waiting for transfers between devices: 76.9 us -> none  [per_device(): lax.psum_scatter(jnp.einsum('bq,npq->bnp', factor_part, scaled, preferred...]
    ppermute x0 -> x44, starting transfers between devices: none -> 49.7 us  [the longest x15 30 us: send(): return lax.ppermute(value, ('row', 'col'), pairs)]
    all_to_all x1 -> x0, blocking collectives: 41.3 us -> none  [per_device(): lax.all_to_all(factor_rows, 'row', split_axis=1, concat_axis=0, tiled=True)]
    dot_general x3 -> x0, matrix products: 26.4 us -> none  [the longest x1 14.5 us: per_device(): jnp.einsum('bq,npq->bnp', factor_part, scaled, preferred_element_type=jnp...]
    pallas_call x0 -> x6, Pallas kernels: none -> 26.3 us  [the longest x1 15.9 us: grid(): pl.pallas_call(functools.partial(grid_kernel, bits), out_shape=[jax.Shape...]
  transfers between devices with their start and end apart: 6 -> 44, of which waited for: 6 -> 17; matrix products, arithmetic and copies ran while one was open for 2% -> 1% of each run, Pallas kernels for 0% -> 4%
where the time goes in v1:
time: 231 us
  waiting for transfers between devices  149 us (65%)
  starting transfers between devices  49.7 us (22%)
  Pallas kernels  26.3 us (11%)
  local copies, waits for them, and re-layouts  4.41 us (2%)
    ppermute x18, waiting for transfers between devices, send(): lax.ppermute(value, 'row', [(r, r ^ 2 * (mask if r % 2 == 0 else flipped(...  75.3 us
    ppermute x15, waiting for transfers between devices, send(): return lax.ppermute(value, ('row', 'col'), pairs)  73.3 us
    ppermute x15, starting transfers between devices, send(): return lax.ppermute(value, ('row', 'col'), pairs)  30 us
    pallas_call x1, Pallas kernels, grid(): pl.pallas_call(functools.partial(grid_kernel, bits), out_shape=[jax.Shape...  15.9 us
    ppermute x18, starting transfers between devices, send(): lax.ppermute(value, 'row', [(r, r ^ 2 * (mask if r % 2 == 0 else flipped(...  15.9 us
    pallas_call x2, Pallas kernels, back(): pl.pallas_call(functools.partial(back_kernel, bits), out_shape=[jax.Shape...  5.04 us
  transfers between devices with their start and end apart: 44, of which 17 were waited for; matrix products, arithmetic and copies ran while one was open for 1% of the time, Pallas kernels for 4%

profile of v1, /device:TPU:0, one launch (start us, length us, event | category | flops | bytes accessed | tf_op | source)
XLA Modules:
  0.0 231.1 jit_solution(12051564326123062090)
XLA Ops:
  0.0 3.0 %collective-permute-start.2 = (bf16[256,1024]{1,0:T(8,128)(2,1)}, bf16[256,1024]{1,0:T(8,128)(2,1)S(1)}, u32[]{:S(2)}, u32[]{:S(2)}) collective-permute-start(bf16[256,1024]{1,0:T(8,128)(2,1)} %refs_3_.3), channel_id=1, source_target_pairs={{0,1},{1,0},{2,3},{3,2},{4,6},{5,7},{6,4},{7,5},{8,9},{9,8},{10,11... | collective-permute-start | bytes 1572872 | tf_op jit(solution)/shard_map/ppermute | solution.py:264
  3.0 1.5 collective-permute-start.6
  4.5 2.6 %collective-permute-start = (bf16[256,1024]{1,0:T(8,128)(2,1)}, bf16[256,1024]{1,0:T(8,128)(2,1)S(1)}, u32[]{:S(2)}, u32[]{:S(2)}) collective-permute-start(bf16[256,1024]{1,0:T(8,128)(2,1)} %refs_3_.3), channel_id=1, source_target_pairs={{0,2},{1,3},{2,0},{3,1},{4,5},{5,4},{6,7},{7,6},{8,10},{9,11},{10,... | collective-permute-start | bytes 1572872 | tf_op jit(solution)/shard_map/ppermute | solution.py:264
  7.1 1.5 collective-permute-start.7
  8.6 17.0 %collective-permute-done.2.refs_1_ = bf16[256,1024]{1,0:T(8,128)(2,1)S(1)} collective-permute-done((bf16[256,1024]{1,0:T(8,128)(2,1)}, bf16[256,1024]{1,0:T(8,128)(2,1)S(1)}, u32[]{:S(2)}, u32[]{:S(2)}) %collective-permute-start.2) | collective-permute-done | bytes 524320 | tf_op jit(solution)/shard_map/ppermute | solution.py:264
  25.7 3.4 %collective-permute-start.3 = (bf16[256,1024]{1,0:T(8,128)(2,1)S(1)}, bf16[256,1024]{1,0:T(8,128)(2,1)}, u32[]{:S(2)}, u32[]{:S(2)}) collective-permute-start(bf16[256,1024]{1,0:T(8,128)(2,1)S(1)} %collective-permute-done.2.refs_1_), channel_id=1, source_target_pairs={{0,2},{1,3},{2,0},{3,1},{4,5},{5,4},{6,7},{7,6},{8,10},{9,11},{10,... | collective-permute-start | bytes 1572872 | tf_op jit(solution)/shard_map/ppermute | solution.py:264
  29.6 1.1 dynamic-slice_bitcast_fusion
  30.8 2.6 %collective-permute-start.1 = (bf16[256,512]{1,0:T(8,128)(2,1)S(1)}, bf16[256,512]{1,0:T(8,128)(2,1)S(1)}, u32[]{:S(2)}, u32[]{:S(2)}) collective-permute-start(bf16[256,512]{1,0:T(8,128)(2,1)S(1)} %get-tuple-element.34.refs_0_), channel_id=1, source_target_pairs={{0,1},{1,0},{2,3},{3,2},{4,6},{5,7},{6,4},{7,5},{8,9},{9,8},{10,11... | collective-permute-start | bytes 786440 | tf_op jit(solution)/shard_map/ppermute | solution.py:264
  33.4 13.9 %collective-permute-done.3.refs_3_ = bf16[256,1024]{1,0:T(8,128)(2,1)} collective-permute-done((bf16[256,1024]{1,0:T(8,128)(2,1)S(1)}, bf16[256,1024]{1,0:T(8,128)(2,1)}, u32[]{:S(2)}, u32[]{:S(2)}) %collective-permute-start.3) | collective-permute-done | bytes 524320 | tf_op jit(solution)/shard_map/ppermute | solution.py:264
  47.3 2.0 collective-permute-start.10
  49.3 3.5 %collective-permute-start.5 = (bf16[256,512]{1,0:T(8,128)(2,1)S(1)}, bf16[256,512]{1,0:T(8,128)(2,1)S(1)}, u32[]{:S(2)}, u32[]{:S(2)}) collective-permute-start(bf16[256,512]{1,0:T(8,128)(2,1)S(1)} %collective-permute-done.1.refs_1_), channel_id=1, source_target_pairs={{0,2},{1,3},{2,0},{3,1},{4,5},{5,4},{6,7},{7,6},{8,10},{9,11},{10,... | collective-permute-start | bytes 786440 | tf_op jit(solution)/shard_map/ppermute | solution.py:264
  52.8 2.8 %collective-permute-done.4.refs_2_ = bf16[256,512]{1,0:T(8,128)(2,1)S(1)} collective-permute-done((bf16[256,512]{1,0:T(8,128)(2,1)S(1)}, bf16[256,512]{1,0:T(8,128)(2,1)S(1)}, u32[]{:S(2)}, u32[]{:S(2)}) %collective-permute-start.4) | collective-permute-done | bytes 262176 | tf_op jit(solution)/shard_map/ppermute | solution.py:264
  55.6 1.0 collective-permute-start.12
  56.6 1.0 copy-done
  57.6 1.5 pick.1
  59.1 1.5 collective-permute-start.23
  60.7 3.1 %collective-permute-start.17 = (bf16[256,512]{1,0:T(8,128)(2,1)S(1)}, bf16[256,512]{1,0:T(8,128)(2,1)S(1)}, u32[]{:S(2)}, u32[]{:S(2)}) collective-permute-start(bf16[256,512]{1,0:T(8,128)(2,1)S(1)} %collective-permute-done.16.refs_0_), channel_id=1, source_target_pairs={{0,1},{1,0},{2,3},{3,2},{4,6},{5,7},{6,4},{7,5},{8,9},{9,8},{10,11... | collective-permute-start | bytes 786440 | tf_op jit(solution)/shard_map/ppermute | solution.py:264
  63.8 1.7 collective-permute-start.18
  65.6 7.5 %collective-permute-done.17.refs_1_ = bf16[256,512]{1,0:T(8,128)(2,1)S(1)} collective-permute-done((bf16[256,512]{1,0:T(8,128)(2,1)S(1)}, bf16[256,512]{1,0:T(8,128)(2,1)S(1)}, u32[]{:S(2)}, u32[]{:S(2)}) %collective-permute-start.17) | collective-permute-done | bytes 262176 | tf_op jit(solution)/shard_map/ppermute | solution.py:264
  73.1 4.4 %collective-permute-start.19 = (bf16[256,512]{1,0:T(8,128)(2,1)S(1)}, bf16[256,512]{1,0:T(8,128)(2,1)S(1)}, u32[]{:S(2)}, u32[]{:S(2)}) collective-permute-start(bf16[256,512]{1,0:T(8,128)(2,1)S(1)} %collective-permute-done.17.refs_1_), channel_id=1, source_target_pairs={{0,2},{1,3},{2,0},{3,1},{4,5},{5,4},{6,7},{7,6},{8,10},{9,11},{10,... | collective-permute-start | bytes 786440 | tf_op jit(solution)/shard_map/ppermute | solution.py:264
  77.5 1.7 collective-permute-start.24
  79.3 1.9 project.2.refs_0_
  81.4 3.3 %collective-permute-done.19.refs_3_ = bf16[256,512]{1,0:T(8,128)(2,1)S(1)} collective-permute-done((bf16[256,512]{1,0:T(8,128)(2,1)S(1)}, bf16[256,512]{1,0:T(8,128)(2,1)S(1)}, u32[]{:S(2)}, u32[]{:S(2)}) %collective-permute-start.19) | collective-permute-done | bytes 262176 | tf_op jit(solution)/shard_map/ppermute | solution.py:264
  84.7 2.4 %collective-permute-start.14 = (bf16[256,1024]{1,0:T(8,128)(2,1)S(1)}, bf16[256,1024]{1,0:T(8,128)(2,1)S(1)}, u32[]{:S(2)}, u32[]{:S(2)}) collective-permute-start(bf16[256,1024]{1,0:T(8,128)(2,1)S(1)} %project.2.refs_0_), channel_id=1, source_target_pairs={{0,16},{4,12},{8,24},{12,4},{16,0},{20,28},{24,8},{28,20},{1,17},{... | collective-permute-start | bytes 1572872 | tf_op jit(solution)/shard_map/ppermute | solution.py:254
  87.1 1.9 project.3.refs_4_
  89.1 11.7 %collective-permute-done.24.refs_10_ = bf16[256,1024]{1,0:T(8,128)(2,1)S(1)} collective-permute-done((bf16[256,1024]{1,0:T(8,128)(2,1)S(1)}, bf16[256,1024]{1,0:T(8,128)(2,1)S(1)}, u32[]{:S(2)}, u32[]{:S(2)}) %collective-permute-start.24) | collective-permute-done | bytes 524320 | tf_op jit(solution)/shard_map/ppermute | solution.py:254
  101.3 10.6 %collective-permute-done.14.refs_2_ = bf16[256,1024]{1,0:T(8,128)(2,1)S(1)} collective-permute-done((bf16[256,1024]{1,0:T(8,128)(2,1)S(1)}, bf16[256,1024]{1,0:T(8,128)(2,1)S(1)}, u32[]{:S(2)}, u32[]{:S(2)}) %collective-permute-start.14) | collective-permute-done | bytes 524320 | tf_op jit(solution)/shard_map/ppermute | solution.py:254
  112.0 0.8 collective-permute-start.21
  112.8 1.3 collective-permute-start.15
  114.1 12.7 %collective-permute-done.20.refs_5_ = bf16[256,1024]{1,0:T(8,128)(2,1)S(1)} collective-permute-done((bf16[256,1024]{1,0:T(8,128)(2,1)S(1)}, bf16[256,1024]{1,0:T(8,128)(2,1)S(1)}, u32[]{:S(2)}, u32[]{:S(2)}) %collective-permute-start.20) | collective-permute-done | bytes 524320 | tf_op jit(solution)/shard_map/ppermute | solution.py:254
  127.6 0.8 copy-done.13
  129.8 6.2 %collective-permute-done.22.refs_7_ = bf16[256,1024]{1,0:T(8,128)(2,1)} collective-permute-done((bf16[256,1024]{1,0:T(8,128)(2,1)S(1)}, bf16[256,1024]{1,0:T(8,128)(2,1)}, u32[]{:S(2)}, u32[]{:S(2)}) %collective-permute-start.22) | collective-permute-done | bytes 524320 | tf_op jit(solution)/shard_map/ppermute | solution.py:254
  136.1 15.9 %grid.1 = (bf16[256,1024]{1,0:T(8,128)(2,1)S(1)}, bf16[256,1024]{1,0:T(8,128)(2,1)S(1)}, bf16[256,1024]{1,0:T(8,128)(2,1)S(1)}, bf16[256,1024]{1,0:T(8,128)(2,1)...) custom-call(bf16[256,1024]{1,0:T(8,128)(2,1)S(1)} %project.2.refs_0_, ...), custom_call_target="tpu_custom_call" | custom-call | flops 8589934592 | bytes 16777216 | tf_op jit(solution)/shard_map/grid/pallas_call | solution.py:141
  152.0 0.8 collective-permute-start.31
  152.9 8.4 %collective-permute-done.31 = bf16[256,1024]{1,0:T(8,128)(2,1)S(1)} collective-permute-done((bf16[256,1024]{1,0:T(8,128)(2,1)S(1)}, bf16[256,1024]{1,0:T(8,128)(2,1)S(1)}, u32[]{:S(2)}, u32[]{:S(2)}) %collective-permute-start.31) | collective-permute-done | bytes 524320 | tf_op jit(solution)/shard_map/ppermute | solution.py:254
  162.0 1.3 collective-permute-start.35
  164.3 10.3 %collective-permute-done.33 = bf16[256,1024]{1,0:T(8,128)(2,1)S(1)} collective-permute-done((bf16[256,1024]{1,0:T(8,128)(2,1)S(1)}, bf16[256,1024]{1,0:T(8,128)(2,1)S(1)}, u32[]{:S(2)}, u32[]{:S(2)}) %collective-permute-start.33) | collective-permute-done | bytes 524320 | tf_op jit(solution)/shard_map/ppermute | solution.py:254
  174.9 11.0 %collective-permute-done.35.refs_1_ = bf16[256,1024]{1,0:T(8,128)(2,1)S(1)} collective-permute-done((bf16[256,1024]{1,0:T(8,128)(2,1)S(1)}, bf16[256,1024]{1,0:T(8,128)(2,1)S(1)}, u32[]{:S(2)}, u32[]{:S(2)}) %collective-permute-start.35) | collective-permute-done | bytes 524320 | tf_op jit(solution)/shard_map/ppermute | solution.py:254
  185.9 2.5 %back.3 = (bf16[256,512]{1,0:T(8,128)(2,1)S(1)}, bf16[256,512]{1,0:T(8,128)(2,1)S(1)}, bf16[256,512]{1,0:T(8,128)(2,1)S(1)}, bf16[256,512]{1,0:T(8,128)(2,1)S(1)}) custom-call(bf16[256,1024]{1,0:T(8,128)(2,1)S(1)} %get-tuple-element.50.refs_0_, bf16[256,1024]{1,0:T(8,128)(2,1)S(1)} %collective-permute-done.35.refs_1_, ...), custom_call_target="tpu_custom_call" | custom-call | flops 1073741824 | bytes 5242880 | tf_op jit(solution)/shard_map/back/pallas_call | solution.py:190
  188.5 4.4 %collective-permute-done.32.refs_1_ = bf16[256,1024]{1,0:T(8,128)(2,1)S(1)} collective-permute-done((bf16[256,1024]{1,0:T(8,128)(2,1)S(1)}, bf16[256,1024]{1,0:T(8,128)(2,1)S(1)}, u32[]{:S(2)}, u32[]{:S(2)}) %collective-permute-start.32) | collective-permute-done | bytes 524320 | tf_op jit(solution)/shard_map/ppermute | solution.py:254
  192.9 2.5 %back.2 = (bf16[256,512]{1,0:T(8,128)(2,1)S(1)}, bf16[256,512]{1,0:T(8,128)(2,1)S(1)}, bf16[256,512]{1,0:T(8,128)(2,1)S(1)}, bf16[256,512]{1,0:T(8,128)(2,1)S(1)}) custom-call(bf16[256,1024]{1,0:T(8,128)(2,1)S(1)} %get-tuple-element.41.refs_0_, bf16[256,1024]{1,0:T(8,128)(2,1)S(1)} %collective-permute-done.32.refs_1_, ...), custom_call_target="tpu_custom_call" | custom-call | flops 1073741824 | bytes 5242880 | tf_op jit(solution)/shard_map/back/pallas_call | solution.py:190
  195.5 3.1 %collective-permute-done.37 = bf16[256,512]{1,0:T(8,128)(2,1)S(1)} collective-permute-done((bf16[256,512]{1,0:T(8,128)(2,1)S(1)}, bf16[256,512]{1,0:T(8,128)(2,1)S(1)}, u32[]{:S(2)}, u32[]{:S(2)}) %collective-permute-start.37) | collective-permute-done | bytes 262176 | tf_op jit(solution)/shard_map/ppermute | solution.py:264
  198.6 2.9 %collective-permute-start.41 = (bf16[256,512]{1,0:T(8,128)(2,1)S(1)}, bf16[256,512]{1,0:T(8,128)(2,1)S(1)}, u32[]{:S(2)}, u32[]{:S(2)}) collective-permute-start(bf16[256,512]{1,0:T(8,128)(2,1)S(1)} %get-tuple-element.59), channel_id=1, source_target_pairs={{0,2},{1,3},{2,0},{3,1},{4,5},{5,4},{6,7},{7,6},{8,10},{9,11},{10,... | collective-permute-start | bytes 786440 | tf_op jit(solution)/shard_map/ppermute | solution.py:264
  202.2 2.0 collective-permute-start.38
  204.1 13.1 %collective-permute-done.39 = bf16[256,512]{1,0:T(8,128)(2,1)S(1)} collective-permute-done((bf16[256,512]{1,0:T(8,128)(2,1)S(1)}, bf16[256,512]{1,0:T(8,128)(2,1)S(1)}, u32[]{:S(2)}, u32[]{:S(2)}) %collective-permute-start.39) | collective-permute-done | bytes 262176 | tf_op jit(solution)/shard_map/ppermute | solution.py:264
  217.3 9.9 %collective-permute-done.41 = bf16[256,512]{1,0:T(8,128)(2,1)S(1)} collective-permute-done((bf16[256,512]{1,0:T(8,128)(2,1)S(1)}, bf16[256,512]{1,0:T(8,128)(2,1)S(1)}, u32[]{:S(2)}, u32[]{:S(2)}) %collective-permute-start.41) | collective-permute-done | bytes 262176 | tf_op jit(solution)/shard_map/ppermute | solution.py:264
  227.5 2.6 %collective-permute-done.38 = bf16[256,512]{1,0:T(8,128)(2,1)S(1)} collective-permute-done((bf16[256,512]{1,0:T(8,128)(2,1)S(1)}, bf16[256,512]{1,0:T(8,128)(2,1)S(1)}, u32[]{:S(2)}, u32[]{:S(2)}) %collective-permute-start.38) | collective-permute-done | bytes 262176 | tf_op jit(solution)/shard_map/ppermute | solution.py:264
  230.2 0.9 maximum_select_fusion
  (86 shorter events, 6.9 us)
Async XLA Ops:
  0.0 79.3 %copy-start.1 = (bf16[256,1024]{1,0:T(8,128)(2,1)S(1)}, bf16[256,1024]{1,0:T(8,128)(2,1)}, u32[]{:S(2)}) copy-start(bf16[256,1024]{1,0:T(8,128)(2,1)} %refs_3_.3) | copy-start | bytes 1572868
  0.0 25.7 %collective-permute-start.2 = (bf16[256,1024]{1,0:T(8,128)(2,1)}, bf16[256,1024]{1,0:T(8,128)(2,1)S(1)}, u32[]{:S(2)}, u32[]{:S(2)}) collective-permute-start(bf16[256,1024]{1,0:T(8,128)(2,1)} %refs_3_.3), channel_id=1, source_target_pairs={{0,1},{1,0},{2,3},{3,2},{4,6},{5,7},{6,4},{7,5},{8,9},{9,8},{10,11... | collective-permute-start | bytes 1572872 | tf_op jit(solution)/shard_map/ppermute | solution.py:264
  3.0 26.0 %collective-permute-start.6 = (bf16[256,1024]{1,0:T(8,128)(2,1)}, bf16[256,1024]{1,0:T(8,128)(2,1)S(1)}, u32[]{:S(2)}, u32[]{:S(2)}) collective-permute-start(bf16[256,1024]{1,0:T(8,128)(2,1)} %refs_3_.3), channel_id=1, source_target_pairs={{0,8},{4,20},{8,0},{12,28},{16,24},{20,4},{24,16},{28,12},{1,9},{5... | collective-permute-start | bytes 1572872 | tf_op jit(solution)/shard_map/ppermute | solution.py:254
  4.5 26.3 %collective-permute-start = (bf16[256,1024]{1,0:T(8,128)(2,1)}, bf16[256,1024]{1,0:T(8,128)(2,1)S(1)}, u32[]{:S(2)}, u32[]{:S(2)}) collective-permute-start(bf16[256,1024]{1,0:T(8,128)(2,1)} %refs_3_.3), channel_id=1, source_target_pairs={{0,2},{1,3},{2,0},{3,1},{4,5},{5,4},{6,7},{7,6},{8,10},{9,11},{10,... | collective-permute-start | bytes 1572872 | tf_op jit(solution)/shard_map/ppermute | solution.py:264
  7.1 26.3 %collective-permute-start.7 = (bf16[256,1024]{1,0:T(8,128)(2,1)}, bf16[256,1024]{1,0:T(8,128)(2,1)S(1)}, u32[]{:S(2)}, u32[]{:S(2)}) collective-permute-start(bf16[256,1024]{1,0:T(8,128)(2,1)} %refs_3_.3), channel_id=1, source_target_pairs={{0,16},{4,12},{8,24},{12,4},{16,0},{20,28},{24,8},{28,20},{1,17},{... | collective-permute-start | bytes 1572872 | tf_op jit(solution)/shard_map/ppermute | solution.py:254
  25.7 21.6 %collective-permute-start.3 = (bf16[256,1024]{1,0:T(8,128)(2,1)S(1)}, bf16[256,1024]{1,0:T(8,128)(2,1)}, u32[]{:S(2)}, u32[]{:S(2)}) collective-permute-start(bf16[256,1024]{1,0:T(8,128)(2,1)S(1)} %collective-permute-done.2.refs_1_), channel_id=1, source_target_pairs={{0,2},{1,3},{2,0},{3,1},{4,5},{5,4},{6,7},{7,6},{8,10},{9,11},{10,... | collective-permute-start | bytes 1572872 | tf_op jit(solution)/shard_map/ppermute | solution.py:264
  29.1 20.2 %collective-permute-start.8 = (bf16[256,1024]{1,0:T(8,128)(2,1)S(1)}, bf16[256,1024]{1,0:T(8,128)(2,1)S(1)}, u32[]{:S(2)}, u32[]{:S(2)}) collective-permute-start(bf16[256,1024]{1,0:T(8,128)(2,1)S(1)} %collective-permute-done.6.refs_5_.refs_4_), channel_id=1, source_target_pairs={{0,16},{4,12},{8,24},{12,4},{16,0},{20,28},{24,8},{28,20},{1,17},{... | collective-permute-start | bytes 1572872 | tf_op jit(solution)/shard_map/ppermute | solution.py:254
  30.7 16.5 %collective-permute-start.16 = (bf16[256,512]{1,0:T(8,128)(2,1)S(1)}, bf16[256,512]{1,0:T(8,128)(2,1)S(1)}, u32[]{:S(2)}, u32[]{:S(2)}) collective-permute-start(bf16[256,512]{1,0:T(8,128)(2,1)S(1)} %get-tuple-element.61), channel_id=1, source_target_pairs={{0,4},{4,0},{8,12},{12,8},{16,20},{20,16},{24,28},{28,24},{1,5},{5... | collective-permute-start | bytes 786440 | tf_op jit(solution)/shard_map/ppermute | solution.py:250
  30.8 16.5 %collective-permute-start.1 = (bf16[256,512]{1,0:T(8,128)(2,1)S(1)}, bf16[256,512]{1,0:T(8,128)(2,1)S(1)}, u32[]{:S(2)}, u32[]{:S(2)}) collective-permute-start(bf16[256,512]{1,0:T(8,128)(2,1)S(1)} %get-tuple-element.34.refs_0_), channel_id=1, source_target_pairs={{0,1},{1,0},{2,3},{3,2},{4,6},{5,7},{6,4},{7,5},{8,9},{9,8},{10,11... | collective-permute-start | bytes 786440 | tf_op jit(solution)/shard_map/ppermute | solution.py:264
  33.4 25.7 %collective-permute-start.9 = (bf16[256,1024]{1,0:T(8,128)(2,1)}, bf16[256,1024]{1,0:T(8,128)(2,1)S(1)}, u32[]{:S(2)}, u32[]{:S(2)}) collective-permute-start(bf16[256,1024]{1,0:T(8,128)(2,1)} %refs_3_.3), channel_id=1, source_target_pairs={{0,4},{4,0},{8,12},{12,8},{16,20},{20,16},{24,28},{28,24},{1,5},{5... | collective-permute-start | bytes 1572872 | tf_op jit(solution)/shard_map/ppermute | solution.py:250
  47.2 13.4 %collective-permute-start.11 = (bf16[256,1024]{1,0:T(8,128)(2,1)S(1)}, bf16[256,1024]{1,0:T(8,128)(2,1)S(1)}, u32[]{:S(2)}, u32[]{:S(2)}) collective-permute-start(bf16[256,1024]{1,0:T(8,128)(2,1)S(1)} %collective-permute-done.7.refs_6_.refs_5_), channel_id=1, source_target_pairs={{0,4},{4,0},{8,12},{12,8},{16,20},{20,16},{24,28},{28,24},{1,5},{5... | collective-permute-start | bytes 1572872 | tf_op jit(solution)/shard_map/ppermute | solution.py:250
  47.3 8.4 %collective-permute-start.4 = (bf16[256,512]{1,0:T(8,128)(2,1)S(1)}, bf16[256,512]{1,0:T(8,128)(2,1)S(1)}, u32[]{:S(2)}, u32[]{:S(2)}) collective-permute-start(bf16[256,512]{1,0:T(8,128)(2,1)S(1)} %get-tuple-element.34.refs_0_), channel_id=1, source_target_pairs={{0,2},{1,3},{2,0},{3,1},{4,5},{5,4},{6,7},{7,6},{8,10},{9,11},{10,... | collective-permute-start | bytes 786440 | tf_op jit(solution)/shard_map/ppermute | solution.py:264
  47.3 16.6 %collective-permute-start.10 = (bf16[256,1024]{1,0:T(8,128)(2,1)S(1)}, bf16[256,1024]{1,0:T(8,128)(2,1)S(1)}, u32[]{:S(2)}, u32[]{:S(2)}) collective-permute-start(bf16[256,1024]{1,0:T(8,128)(2,1)S(1)} %collective-permute-done.6.refs_5_.refs_4_), channel_id=1, source_target_pairs={{0,4},{4,0},{8,12},{12,8},{16,20},{20,16},{24,28},{28,24},{1,5},{5... | collective-permute-start | bytes 1572872 | tf_op jit(solution)/shard_map/ppermute | solution.py:250
  49.3 14.5 %collective-permute-start.5 = (bf16[256,512]{1,0:T(8,128)(2,1)S(1)}, bf16[256,512]{1,0:T(8,128)(2,1)S(1)}, u32[]{:S(2)}, u32[]{:S(2)}) collective-permute-start(bf16[256,512]{1,0:T(8,128)(2,1)S(1)} %collective-permute-done.1.refs_1_), channel_id=1, source_target_pairs={{0,2},{1,3},{2,0},{3,1},{4,5},{5,4},{6,7},{7,6},{8,10},{9,11},{10,... | collective-permute-start | bytes 786440 | tf_op jit(solution)/shard_map/ppermute | solution.py:264
  55.6 21.9 %collective-permute-start.12 = (bf16[256,1024]{1,0:T(8,128)(2,1)S(1)}, bf16[256,1024]{1,0:T(8,128)(2,1)S(1)}, u32[]{:S(2)}, u32[]{:S(2)}) collective-permute-start(bf16[256,1024]{1,0:T(8,128)(2,1)S(1)} %collective-permute-done.8.refs_7_.refs_6_), channel_id=1, source_target_pairs={{0,4},{4,0},{8,12},{12,8},{16,20},{20,16},{24,28},{28,24},{1,5},{5... | collective-permute-start | bytes 1572872 | tf_op jit(solution)/shard_map/ppermute | solution.py:250
  59.1 22.2 %collective-permute-start.23 = (bf16[256,1024]{1,0:T(8,128)(2,1)S(1)}, bf16[256,1024]{1,0:T(8,128)(2,1)S(1)}, u32[]{:S(2)}, u32[]{:S(2)}) collective-permute-start(bf16[256,1024]{1,0:T(8,128)(2,1)S(1)} %get-tuple-element.38), channel_id=1, source_target_pairs={{0,8},{4,20},{8,0},{12,28},{16,24},{20,4},{24,16},{28,12},{1,9},{5... | collective-permute-start | bytes 1572872 | tf_op jit(solution)/shard_map/ppermute | solution.py:254
  60.7 12.4 %collective-permute-start.17 = (bf16[256,512]{1,0:T(8,128)(2,1)S(1)}, bf16[256,512]{1,0:T(8,128)(2,1)S(1)}, u32[]{:S(2)}, u32[]{:S(2)}) collective-permute-start(bf16[256,512]{1,0:T(8,128)(2,1)S(1)} %collective-permute-done.16.refs_0_), channel_id=1, source_target_pairs={{0,1},{1,0},{2,3},{3,2},{4,6},{5,7},{6,4},{7,5},{8,9},{9,8},{10,11... | collective-permute-start | bytes 786440 | tf_op jit(solution)/shard_map/ppermute | solution.py:264
  63.8 63.7 %collective-permute-start.30 = (f32[512,1024]{1,0:T(8,128)S(1)}, f32[512,1024]{1,0:T(8,128)S(1)}, u32[]{:S(2)}, u32[]{:S(2)}) collective-permute-start(f32[512,1024]{1,0:T(8,128)S(1)} %copy-done.4), channel_id=1, source_target_pairs={{0,4},{4,0},{8,12},{12,8},{16,20},{20,16},{24,28},{28,24},{1,5},{5... | collective-permute-start | bytes 6291464 | tf_op jit(solution)/shard_map/ppermute | solution.py:250
  63.8 17.4 %collective-permute-start.18 = (bf16[256,512]{1,0:T(8,128)(2,1)S(1)}, bf16[256,512]{1,0:T(8,128)(2,1)S(1)}, u32[]{:S(2)}, u32[]{:S(2)}) collective-permute-start(bf16[256,512]{1,0:T(8,128)(2,1)S(1)} %collective-permute-done.16.refs_0_), channel_id=1, source_target_pairs={{0,2},{1,3},{2,0},{3,1},{4,5},{5,4},{6,7},{7,6},{8,10},{9,11},{10,... | collective-permute-start | bytes 786440 | tf_op jit(solution)/shard_map/ppermute | solution.py:264
  73.1 11.6 %collective-permute-start.19 = (bf16[256,512]{1,0:T(8,128)(2,1)S(1)}, bf16[256,512]{1,0:T(8,128)(2,1)S(1)}, u32[]{:S(2)}, u32[]{:S(2)}) collective-permute-start(bf16[256,512]{1,0:T(8,128)(2,1)S(1)} %collective-permute-done.17.refs_1_), channel_id=1, source_target_pairs={{0,2},{1,3},{2,0},{3,1},{4,5},{5,4},{6,7},{7,6},{8,10},{9,11},{10,... | collective-permute-start | bytes 786440 | tf_op jit(solution)/shard_map/ppermute | solution.py:264
  77.5 23.2 %collective-permute-start.24 = (bf16[256,1024]{1,0:T(8,128)(2,1)S(1)}, bf16[256,1024]{1,0:T(8,128)(2,1)S(1)}, u32[]{:S(2)}, u32[]{:S(2)}) collective-permute-start(bf16[256,1024]{1,0:T(8,128)(2,1)S(1)} %get-tuple-element.39), channel_id=1, source_target_pairs={{0,16},{4,12},{8,24},{12,4},{16,0},{20,28},{24,8},{28,20},{1,17},{... | collective-permute-start | bytes 1572872 | tf_op jit(solution)/shard_map/ppermute | solution.py:254
  81.2 19.5 %collective-permute-start.25 = (bf16[256,1024]{1,0:T(8,128)(2,1)S(1)}, bf16[256,1024]{1,0:T(8,128)(2,1)S(1)}, u32[]{:S(2)}, u32[]{:S(2)}) collective-permute-start(bf16[256,1024]{1,0:T(8,128)(2,1)S(1)} %get-tuple-element.40), channel_id=1, source_target_pairs={{0,24},{4,28},{8,16},{12,20},{16,8},{20,12},{24,0},{28,4},{1,25},{... | collective-permute-start | bytes 1572872 | tf_op jit(solution)/shard_map/ppermute | solution.py:254
  81.3 19.5 %collective-permute-start.26 = (bf16[256,1024]{1,0:T(8,128)(2,1)S(1)}, bf16[256,1024]{1,0:T(8,128)(2,1)S(1)}, u32[]{:S(2)}, u32[]{:S(2)}) collective-permute-start(bf16[256,1024]{1,0:T(8,128)(2,1)S(1)} %get-tuple-element.37.refs_8_), channel_id=1, source_target_pairs={{0,4},{4,0},{8,12},{12,8},{16,20},{20,16},{24,28},{28,24},{1,5},{5... | collective-permute-start | bytes 1572872 | tf_op jit(solution)/shard_map/ppermute | solution.py:250
  84.7 27.2 %collective-permute-start.14 = (bf16[256,1024]{1,0:T(8,128)(2,1)S(1)}, bf16[256,1024]{1,0:T(8,128)(2,1)S(1)}, u32[]{:S(2)}, u32[]{:S(2)}) collective-permute-start(bf16[256,1024]{1,0:T(8,128)(2,1)S(1)} %project.2.refs_0_), channel_id=1, source_target_pairs={{0,16},{4,12},{8,24},{12,4},{16,0},{20,28},{24,8},{28,20},{1,17},{... | collective-permute-start | bytes 1572872 | tf_op jit(solution)/shard_map/ppermute | solution.py:254
  89.1 47.0 %copy-start.2 = (bf16[256,1024]{1,0:T(8,128)(2,1)}, bf16[256,1024]{1,0:T(8,128)(2,1)S(1)}, u32[]{:S(2)}) copy-start(bf16[256,1024]{1,0:T(8,128)(2,1)S(1)} %project.3.refs_4_) | copy-start | bytes 1572868
  100.7 35.3 %copy-start.7 = (bf16[256,1024]{1,0:T(8,128)(2,1)}, bf16[256,1024]{1,0:T(8,128)(2,1)S(1)}, u32[]{:S(2)}) copy-start(bf16[256,1024]{1,0:T(8,128)(2,1)S(1)} %collective-permute-done.24.refs_10_) | copy-start | bytes 1572868
  100.7 11.2 %collective-permute-start.13 = (bf16[256,1024]{1,0:T(8,128)(2,1)S(1)}, bf16[256,1024]{1,0:T(8,128)(2,1)S(1)}, u32[]{:S(2)}, u32[]{:S(2)}) collective-permute-start(bf16[256,1024]{1,0:T(8,128)(2,1)S(1)} %project.2.refs_0_), channel_id=1, source_target_pairs={{0,8},{4,20},{8,0},{12,28},{16,24},{20,4},{24,16},{28,12},{1,9},{5... | collective-permute-start | bytes 1572872 | tf_op jit(solution)/shard_map/ppermute | solution.py:254
  100.7 35.3 %copy-start.8 = (bf16[256,1024]{1,0:T(8,128)(2,1)}, bf16[256,1024]{1,0:T(8,128)(2,1)S(1)}, u32[]{:S(2)}) copy-start(bf16[256,1024]{1,0:T(8,128)(2,1)S(1)} %collective-permute-done.25.refs_11_) | copy-start | bytes 1572868
  100.7 11.2 %collective-permute-start.27 = (bf16[256,1024]{1,0:T(8,128)(2,1)S(1)}, bf16[256,1024]{1,0:T(8,128)(2,1)S(1)}, u32[]{:S(2)}, u32[]{:S(2)}) collective-permute-start(bf16[256,1024]{1,0:T(8,128)(2,1)S(1)} %collective-permute-done.23.refs_9_), channel_id=1, source_target_pairs={{0,4},{4,0},{8,12},{12,8},{16,20},{20,16},{24,28},{28,24},{1,5},{5... | collective-permute-start | bytes 1572872 | tf_op jit(solution)/shard_map/ppermute | solution.py:250
  100.8 12.0 %collective-permute-start.28 = (bf16[256,1024]{1,0:T(8,128)(2,1)S(1)}, bf16[256,1024]{1,0:T(8,128)(2,1)S(1)}, u32[]{:S(2)}, u32[]{:S(2)}) collective-permute-start(bf16[256,1024]{1,0:T(8,128)(2,1)S(1)} %collective-permute-done.24.refs_10_), channel_id=1, source_target_pairs={{0,4},{4,0},{8,12},{12,8},{16,20},{20,16},{24,28},{28,24},{1,5},{5... | collective-permute-start | bytes 1572872 | tf_op jit(solution)/shard_map/ppermute | solution.py:250
  112.0 14.8 %collective-permute-start.20 = (bf16[256,1024]{1,0:T(8,128)(2,1)S(1)}, bf16[256,1024]{1,0:T(8,128)(2,1)S(1)}, u32[]{:S(2)}, u32[]{:S(2)}) collective-permute-start(bf16[256,1024]{1,0:T(8,128)(2,1)S(1)} %project.3.refs_4_), channel_id=1, source_target_pairs={{0,8},{4,20},{8,0},{12,28},{16,24},{20,4},{24,16},{28,12},{1,9},{5... | collective-permute-start | bytes 1572872 | tf_op jit(solution)/shard_map/ppermute | solution.py:254
  112.0 15.5 %collective-permute-start.29 = (bf16[256,1024]{1,0:T(8,128)(2,1)S(1)}, bf16[256,1024]{1,0:T(8,128)(2,1)S(1)}, u32[]{:S(2)}, u32[]{:S(2)}) collective-permute-start(bf16[256,1024]{1,0:T(8,128)(2,1)S(1)} %collective-permute-done.25.refs_11_), channel_id=1, source_target_pairs={{0,4},{4,0},{8,12},{12,8},{16,20},{20,16},{24,28},{28,24},{1,5},{5... | collective-permute-start | bytes 1572872 | tf_op jit(solution)/shard_map/ppermute | solution.py:250
  112.0 15.5 %collective-permute-start.21 = (bf16[256,1024]{1,0:T(8,128)(2,1)S(1)}, bf16[256,1024]{1,0:T(8,128)(2,1)S(1)}, u32[]{:S(2)}, u32[]{:S(2)}) collective-permute-start(bf16[256,1024]{1,0:T(8,128)(2,1)S(1)} %project.3.refs_4_), channel_id=1, source_target_pairs={{0,16},{4,12},{8,24},{12,4},{16,0},{20,28},{24,8},{28,20},{1,17},{... | collective-permute-start | bytes 1572872 | tf_op jit(solution)/shard_map/ppermute | solution.py:254
  112.8 14.7 %collective-permute-start.15 = (bf16[256,1024]{1,0:T(8,128)(2,1)S(1)}, bf16[256,1024]{1,0:T(8,128)(2,1)S(1)}, u32[]{:S(2)}, u32[]{:S(2)}) collective-permute-start(bf16[256,1024]{1,0:T(8,128)(2,1)S(1)} %collective-permute-done.13.refs_1_), channel_id=1, source_target_pairs={{0,16},{4,12},{8,24},{12,4},{16,0},{20,28},{24,8},{28,20},{1,17},{... | collective-permute-start | bytes 1572872 | tf_op jit(solution)/shard_map/ppermute | solution.py:254
  126.8 9.3 %collective-permute-start.22 = (bf16[256,1024]{1,0:T(8,128)(2,1)S(1)}, bf16[256,1024]{1,0:T(8,128)(2,1)}, u32[]{:S(2)}, u32[]{:S(2)}) collective-permute-start(bf16[256,1024]{1,0:T(8,128)(2,1)S(1)} %collective-permute-done.20.refs_5_), channel_id=1, source_target_pairs={{0,16},{4,12},{8,24},{12,4},{16,0},{20,28},{24,8},{28,20},{1,17},{... | collective-permute-start | bytes 1572872 | tf_op jit(solution)/shard_map/ppermute | solution.py:254
  152.0 9.2 %collective-permute-start.31 = (bf16[256,1024]{1,0:T(8,128)(2,1)S(1)}, bf16[256,1024]{1,0:T(8,128)(2,1)S(1)}, u32[]{:S(2)}, u32[]{:S(2)}) collective-permute-start(bf16[256,1024]{1,0:T(8,128)(2,1)S(1)} %get-tuple-element.43), channel_id=1, source_target_pairs={{0,16},{4,12},{8,24},{12,4},{16,0},{20,28},{24,8},{28,20},{1,17},{... | collective-permute-start | bytes 1572872 | tf_op jit(solution)/shard_map/ppermute | solution.py:254
  161.3 13.4 %collective-permute-start.33 = (bf16[256,1024]{1,0:T(8,128)(2,1)S(1)}, bf16[256,1024]{1,0:T(8,128)(2,1)S(1)}, u32[]{:S(2)}, u32[]{:S(2)}) collective-permute-start(bf16[256,1024]{1,0:T(8,128)(2,1)S(1)} %get-tuple-element.47), channel_id=1, source_target_pairs={{0,16},{4,12},{8,24},{12,4},{16,0},{20,28},{24,8},{28,20},{1,17},{... | collective-permute-start | bytes 1572872 | tf_op jit(solution)/shard_map/ppermute | solution.py:254
  162.0 23.9 %collective-permute-start.35 = (bf16[256,1024]{1,0:T(8,128)(2,1)S(1)}, bf16[256,1024]{1,0:T(8,128)(2,1)S(1)}, u32[]{:S(2)}, u32[]{:S(2)}) collective-permute-start(bf16[256,1024]{1,0:T(8,128)(2,1)S(1)} %get-tuple-element.51), channel_id=1, source_target_pairs={{0,16},{4,12},{8,24},{12,4},{16,0},{20,28},{24,8},{28,20},{1,17},{... | collective-permute-start | bytes 1572872 | tf_op jit(solution)/shard_map/ppermute | solution.py:254
  163.3 29.6 %collective-permute-start.32 = (bf16[256,1024]{1,0:T(8,128)(2,1)S(1)}, bf16[256,1024]{1,0:T(8,128)(2,1)S(1)}, u32[]{:S(2)}, u32[]{:S(2)}) collective-permute-start(bf16[256,1024]{1,0:T(8,128)(2,1)S(1)} %get-tuple-element.44), channel_id=1, source_target_pairs={{0,16},{4,12},{8,24},{12,4},{16,0},{20,28},{24,8},{28,20},{1,17},{... | collective-permute-start | bytes 1572872 | tf_op jit(solution)/shard_map/ppermute | solution.py:254
  164.3 21.6 %collective-permute-start.36 = (bf16[256,1024]{1,0:T(8,128)(2,1)S(1)}, bf16[256,1024]{1,0:T(8,128)(2,1)S(1)}, u32[]{:S(2)}, u32[]{:S(2)}) collective-permute-start(bf16[256,1024]{1,0:T(8,128)(2,1)S(1)} %add_convert_fusion), channel_id=1, source_target_pairs={{0,8},{4,20},{8,0},{12,28},{16,24},{20,4},{24,16},{28,12},{1,9},{5... | collective-permute-start | bytes 1572872 | tf_op jit(solution)/shard_map/ppermute | solution.py:254
  174.9 18.1 %collective-permute-start.34 = (bf16[256,1024]{1,0:T(8,128)(2,1)S(1)}, bf16[256,1024]{1,0:T(8,128)(2,1)S(1)}, u32[]{:S(2)}, u32[]{:S(2)}) collective-permute-start(bf16[256,1024]{1,0:T(8,128)(2,1)S(1)} %add_convert_fusion.1), channel_id=1, source_target_pairs={{0,8},{4,20},{8,0},{12,28},{16,24},{20,4},{24,16},{28,12},{1,9},{5... | collective-permute-start | bytes 1572872 | tf_op jit(solution)/shard_map/ppermute | solution.py:254
  188.4 10.1 %collective-permute-start.37 = (bf16[256,512]{1,0:T(8,128)(2,1)S(1)}, bf16[256,512]{1,0:T(8,128)(2,1)S(1)}, u32[]{:S(2)}, u32[]{:S(2)}) collective-permute-start(bf16[256,512]{1,0:T(8,128)(2,1)S(1)} %get-tuple-element.53), channel_id=1, source_target_pairs={{0,2},{1,3},{2,0},{3,1},{4,5},{5,4},{6,7},{7,6},{8,10},{9,11},{10,... | collective-permute-start | bytes 786440 | tf_op jit(solution)/shard_map/ppermute | solution.py:264
  198.6 18.6 %collective-permute-start.39 = (bf16[256,512]{1,0:T(8,128)(2,1)S(1)}, bf16[256,512]{1,0:T(8,128)(2,1)S(1)}, u32[]{:S(2)}, u32[]{:S(2)}) collective-permute-start(bf16[256,512]{1,0:T(8,128)(2,1)S(1)} %get-tuple-element.57), channel_id=1, source_target_pairs={{0,2},{1,3},{2,0},{3,1},{4,5},{5,4},{6,7},{7,6},{8,10},{9,11},{10,... | collective-permute-start | bytes 786440 | tf_op jit(solution)/shard_map/ppermute | solution.py:264
  198.6 28.7 %collective-permute-start.41 = (bf16[256,512]{1,0:T(8,128)(2,1)S(1)}, bf16[256,512]{1,0:T(8,128)(2,1)S(1)}, u32[]{:S(2)}, u32[]{:S(2)}) collective-permute-start(bf16[256,512]{1,0:T(8,128)(2,1)S(1)} %get-tuple-element.59), channel_id=1, source_target_pairs={{0,2},{1,3},{2,0},{3,1},{4,5},{5,4},{6,7},{7,6},{8,10},{9,11},{10,... | collective-permute-start | bytes 786440 | tf_op jit(solution)/shard_map/ppermute | solution.py:264
  201.6 25.7 %collective-permute-start.42 = (bf16[256,512]{1,0:T(8,128)(2,1)S(1)}, bf16[256,512]{1,0:T(8,128)(2,1)S(1)}, u32[]{:S(2)}, u32[]{:S(2)}) collective-permute-start(bf16[256,512]{1,0:T(8,128)(2,1)S(1)} %add_convert_fusion.3), channel_id=1, source_target_pairs={{0,1},{1,0},{2,3},{3,2},{4,6},{5,7},{6,4},{7,5},{8,9},{9,8},{10,11... | collective-permute-start | bytes 786440 | tf_op jit(solution)/shard_map/ppermute | solution.py:264
  202.2 27.9 %collective-permute-start.38 = (bf16[256,512]{1,0:T(8,128)(2,1)S(1)}, bf16[256,512]{1,0:T(8,128)(2,1)S(1)}, u32[]{:S(2)}, u32[]{:S(2)}) collective-permute-start(bf16[256,512]{1,0:T(8,128)(2,1)S(1)} %get-tuple-element.54), channel_id=1, source_target_pairs={{0,2},{1,3},{2,0},{3,1},{4,5},{5,4},{6,7},{7,6},{8,10},{9,11},{10,... | collective-permute-start | bytes 786440 | tf_op jit(solution)/shard_map/ppermute | solution.py:264
  217.3 12.8 %collective-permute-start.40 = (bf16[256,512]{1,0:T(8,128)(2,1)S(1)}, bf16[256,512]{1,0:T(8,128)(2,1)S(1)}, u32[]{:S(2)}, u32[]{:S(2)}) collective-permute-start(bf16[256,512]{1,0:T(8,128)(2,1)S(1)} %add_convert_fusion.5), channel_id=1, source_target_pairs={{0,1},{1,0},{2,3},{3,2},{4,6},{5,7},{6,4},{7,5},{8,9},{9,8},{10,11... | collective-permute-start | bytes 786440 | tf_op jit(solution)/shard_map/ppermute | solution.py:264
  227.4 2.8 %collective-permute-start.43 = (bf16[256,512]{1,0:T(8,128)(2,1)S(1)}, bf16[256,512]{1,0:T(8,128)(2,1)S(1)}, u32[]{:S(2)}, u32[]{:S(2)}) collective-permute-start(bf16[256,512]{1,0:T(8,128)(2,1)S(1)} %add_convert_fusion.2), channel_id=1, source_target_pairs={{0,4},{4,0},{8,12},{12,8},{16,20},{20,16},{24,28},{28,24},{1,5},{5... | collective-permute-start | bytes 786440 | tf_op jit(solution)/shard_map/ppermute | solution.py:250
  (12 other events, 144.0 us)

commit v2 on v1

v2 whole, which is shorter than its diff:
```python
import functools

import jax
import jax.numpy as jnp
from jax import lax
from jax.experimental import pallas as pl
from jax.experimental.pallas import tpu as pltpu
from jax.sharding import PartitionSpec as P

BF16 = jnp.bfloat16
F32 = jnp.float32
ANY = pl.BlockSpec(memory_space=pl.ANY)
HBM = pl.BlockSpec(memory_space=pltpu.HBM)


def flipped(value, bits):
    total = 0
    for t in range(bits):
        total = total + (((value >> t) & 1) << (bits - 1 - t))
    return total


def params(vmem):
    return pltpu.CompilerParams(vmem_limit_bytes=vmem)


def where_am_i(bits):
    row, col = lax.axis_index("row"), lax.axis_index("col")
    core, chip = lax.rem(row, 2), row // 2
    offset = chip ^ col
    base = jnp.where(core == 0, offset, flipped(offset, bits))
    return core, base


def copy_all(pairs, sems):
    copies = [pltpu.make_async_copy(a, b, sems.at[s]) for s, (a, b) in enumerate(pairs)]
    for copy in copies:
        copy.start()
    return copies


def plane_pairs(own, other, room, core, rows, bits):
    pairs = []
    for j, ref in enumerate(own):
        pairs.append((ref, room.at[pl.ds((2 * j + core) * rows, rows)]))
    for j, ref in enumerate(other):
        pairs.append((ref, room.at[pl.ds((2 * flipped(j, bits) + 1 - core) * rows, rows)]))
    return pairs


def halves(ref, core):
    half = ref.shape[1] // 2
    return [ref.at[:, pl.ds(pl.multiple_of(which * half, half), half)] for which in (core, 1 - core)]


def project_kernel(bits, *refs):
    n = 1 << bits
    terms, own, other = refs[:n], refs[n : 2 * n], refs[2 * n : 3 * n]
    keep, away, held, room, result, sems = refs[3 * n :]
    core, base = where_am_i(bits)
    rows, width = own[0].shape
    depth = terms[0].shape[1]
    pairs = plane_pairs(own, other, room, core, rows, bits) + [(terms[l], held.at[l]) for l in range(n)]
    for copy in copy_all(pairs, sems):
        copy.wait()
    tile = min(width // 2, 512)

    @pl.loop(0, width // tile)
    def _(step):
        at = pl.ds(pl.multiple_of(step * tile, tile), tile)
        acc = jnp.zeros((rows, tile), F32)
        for l in range(n):
            start = pl.multiple_of((base ^ l) * depth, depth)
            acc = acc + jnp.dot(held[l], room[pl.ds(start, depth), at], preferred_element_type=F32)
        result[:, at] = acc.astype(BF16)

    for copy in copy_all(list(zip(halves(result, core), (keep, away))), sems):
        copy.wait()


def project(terms, own, other, bits):
    n = len(terms)
    m, depth = terms[0].shape
    rows, width = own[0].shape
    return pl.pallas_call(
        functools.partial(project_kernel, bits),
        out_shape=[jax.ShapeDtypeStruct((m, width // 2), BF16)] * 2,
        in_specs=[HBM] * (3 * n),
        out_specs=[ANY] * 2,
        scratch_shapes=[
            pltpu.VMEM((n, m, depth), BF16),
            pltpu.VMEM((2 * n * rows, width), BF16),
            pltpu.VMEM((m, width), BF16),
            pltpu.SemaphoreType.DMA((3 * n,)),
        ],
        compiler_params=params(32 << 20),
        cost_estimate=pl.CostEstimate(flops=1, bytes_accessed=1, transcendentals=0),
        name="project",
    )(*terms, *own, *other)


def grid_kernel(bits, *refs):
    n = 1 << bits
    proj_in, own, other = refs[:n], refs[n : 2 * n], refs[2 * n : 3 * n]
    kernel_own, kernel_other = refs[3 * n : 3 * n + 2]
    outs = refs[3 * n + 2 : 4 * n + 2]
    proj, room, coulomb, scaled, result, sems, tile_sems, out_sems = refs[4 * n + 2 :]
    core, _ = where_am_i(bits)
    rows = own[0].shape[0]
    half = kernel_own.shape[0]
    pairs = []
    for j in range(n):
        pairs.append((own[j], room.at[pl.ds(2 * j * rows, rows)]))
        pairs.append((other[flipped(j, bits)], room.at[pl.ds((2 * j + 1) * rows, rows)]))
        pairs.append((proj_in[j], proj.at[pl.ds(2 * j * rows, 2 * rows)]))
    loads = copy_all(pairs, sems)
    late = copy_all([(kernel_own, coulomb.at[pl.ds(core * half, half)]), (kernel_other, coulomb.at[pl.ds((1 - core) * half, half)])], tile_sems)
    for copy in loads:
        copy.wait()
    for copy in late:
        copy.wait()
    tile = min(proj.shape[1], 256)

    @pl.loop(0, proj.shape[1] // tile)
    def _(step):
        at = pl.ds(pl.multiple_of(step * tile, tile), tile)
        grid = lax.dot_general(room[...], proj[:, at], (((0,), (0,)), ((), ())), preferred_element_type=F32)
        scaled[:, at] = (coulomb[:, at] * grid).astype(BF16)

    copies = []
    for j in range(n - 1, -1, -1):
        at = pl.ds(2 * j * rows, 2 * rows)
        result[at, :] = jnp.dot(room[at, :], scaled[...], preferred_element_type=F32).astype(BF16)
        copy = pltpu.make_async_copy(result.at[at], outs[j], out_sems.at[j])
        copy.start()
        copies.append(copy)
    for copy in copies:
        copy.wait()


def grid(proj, own, other, kernel_own, kernel_other, bits):
    n = len(proj)
    rows, width = own[0].shape
    cols = proj[0].shape[1]
    outs = pl.pallas_call(
        functools.partial(grid_kernel, bits),
        out_shape=[jax.ShapeDtypeStruct((2 * rows, cols), BF16)] * n,
        in_specs=[HBM] * (3 * n) + [ANY] * 2,
        out_specs=[ANY] * n,
        scratch_shapes=[
            pltpu.VMEM((2 * n * rows, cols), BF16),
            pltpu.VMEM((2 * n * rows, width), BF16),
            pltpu.VMEM((width, cols), F32),
            pltpu.VMEM((width, cols), BF16),
            pltpu.VMEM((2 * n * rows, cols), BF16),
            pltpu.SemaphoreType.DMA((3 * n,)),
            pltpu.SemaphoreType.DMA((2,)),
            pltpu.SemaphoreType.DMA((n,)),
        ],
        compiler_params=params(40 << 20),
        cost_estimate=pl.CostEstimate(flops=1, bytes_accessed=1, transcendentals=0),
        name="grid",
    )(*proj, *own, *other, kernel_own, kernel_other)
    return list(outs)


def back_kernel(bits, *refs):
    n = 1 << bits
    keep, came, own, other = refs[0], refs[1], refs[2 : 2 + n], refs[2 + n : 2 + 2 * n]
    outs = refs[2 + 2 * n : 2 + 3 * n]
    given, room, results, sems, out_sems = refs[2 + 3 * n :]
    core, base = where_am_i(bits)
    rows, width = own[0].shape
    depth = outs[0].shape[1]
    pairs = plane_pairs(own, other, room, core, rows, bits) + list(zip((keep, came), halves(given, core)))
    for copy in copy_all(pairs, sems):
        copy.wait()
    copies = []
    for l in range(n - 1, -1, -1):
        right = room[pl.ds(pl.multiple_of((base ^ l) * depth, depth), depth), :]
        results[l] = lax.dot_general(given[...], right, (((1,), (1,)), ((), ())), preferred_element_type=F32).astype(BF16)
        copy = pltpu.make_async_copy(results.at[l], outs[l], out_sems.at[l])
        copy.start()
        copies.append(copy)
    for copy in copies:
        copy.wait()


def back(keep, came, own, other, bits):
    n = len(own)
    rows, width = own[0].shape
    m, depth = keep.shape[0], 2 * rows
    outs = pl.pallas_call(
        functools.partial(back_kernel, bits),
        out_shape=[jax.ShapeDtypeStruct((m, depth), BF16)] * n,
        in_specs=[ANY] * 2 + [HBM] * (2 * n),
        out_specs=[ANY] * n,
        scratch_shapes=[
            pltpu.VMEM((m, width), BF16),
            pltpu.VMEM((2 * n * rows, width), BF16),
            pltpu.VMEM((n, m, depth), BF16),
            pltpu.SemaphoreType.DMA((2 + 2 * n,)),
            pltpu.SemaphoreType.DMA((n,)),
        ],
        compiler_params=params(32 << 20),
        cost_estimate=pl.CostEstimate(flops=1, bytes_accessed=1, transcendentals=0),
        name="back",
    )(keep, came, *own, *other)
    return list(outs)


def pick_kernel(bits, *refs):
    n = 1 << bits
    blocks, outs, (room, sems) = refs[:n], refs[n : 2 * n], refs[2 * n :]
    _, base = where_am_i(bits)
    for copy in copy_all([(blocks[l], room.at[l]) for l in range(n)], sems):
        copy.wait()
    for copy in copy_all([(room.at[base ^ j], outs[j]) for j in range(n)], sems):
        copy.wait()


def pick(blocks, bits):
    n = len(blocks)
    return pl.pallas_call(
        functools.partial(pick_kernel, bits),
        out_shape=[jax.ShapeDtypeStruct(blocks[0].shape, BF16)] * n,
        in_specs=[HBM] * n,
        out_specs=[ANY] * n,
        scratch_shapes=[pltpu.VMEM((n, *blocks[0].shape), BF16), pltpu.SemaphoreType.DMA((n,))],
        compiler_params=params(16 << 20),
        cost_estimate=pl.CostEstimate(flops=1, bytes_accessed=1, transcendentals=0),
        name="pick",
    )(*blocks)


def total(parts):
    return sum(part.astype(F32) for part in parts).astype(BF16)


def after(value, *others):
    return lax.optimization_barrier((value, *others))[0]


def per_device(rows, cols, amplitudes, factor, kernel):
    chips = rows // 2
    bits = chips.bit_length() - 1
    core = lax.rem(lax.axis_index("row"), 2)

    def distance(row, mask):
        return mask if row % 2 == 0 else flipped(mask, bits)

    def swap(value):
        return lax.ppermute(value, "row", [(r, r ^ 1) for r in range(rows)])

    def in_plane(mask):
        return lambda value: lax.ppermute(value, "row", [(r, r ^ (2 * distance(r, mask))) for r in range(rows)])

    def in_line(mask):
        pairs = [(r * cols + c, r * cols + (c ^ distance(r, mask))) for r in range(rows) for c in range(cols)]
        return lambda value: lax.ppermute(value, ("row", "col"), pairs)

    plane = [in_plane(1 << t) for t in range(bits)]
    line = [in_line(1 << t) for t in range(bits)]

    def gather(block, sends, gates=(), chained=False):
        blocks = [block]
        for t, send in enumerate(sends):
            first = after(block, *gates[t]) if t < len(gates) else block
            fresh = [send(first)]
            blocks = blocks + fresh + [send(after(b, *fresh) if chained else b) for b in blocks[1:]]
        return blocks

    def scatter(blocks, sends, gates=None):
        parts, marks = [], None
        for t in range(len(sends) - 1, -1, -1):
            n = 1 << t
            away = blocks[n:]
            if gates is not None and marks is None:
                away = [after(block, *gates) for block in away]
            got = [sends[t](block) for block in away]
            marks = got if marks is None else marks
            parts.append(got[0])
            blocks = [blocks[0]] + [total([blocks[j], got[j]]) for j in range(1, n)]
        return [blocks[0], *parts], marks

    def column_halves(value):
        half = value.shape[1] // 2
        return [lax.dynamic_slice_in_dim(value, which * half, half, 1) for which in (core, 1 - core)]

    line_own = gather(factor, line, chained=True)
    cols_own = gather(factor, plane)
    kernel_own, kernel_away = column_halves(kernel)
    kernel_other = swap(kernel_away)
    cols_other = [swap(b) for b in cols_own]
    terms = [gather(amplitudes[0], line, [[line_own[-1]]] * bits)]
    terms.append(gather(amplitudes[1], line, [[terms[0][1]]] + [[terms[0][-1]]] * (bits - 1)))

    pieces = pick(line_own, bits)
    first_own = [pieces[0]] + [in_plane(j)(pieces[j]) for j in range(1, chips)]
    first_other = [swap(b) for b in first_own]

    gates, results, marks = first_own[1:], [], [None, None]
    for pair in range(amplitudes.shape[0]):
        keep, away = project(terms[pair], cols_own, cols_other, bits)
        block = jnp.concatenate([keep, swap(away)])
        proj = gather(block, plane, [gates] * bits)
        gates = proj[1:3]
        backs = grid(proj, first_own, first_other, kernel_own, kernel_other, bits)
        parts, marks[0] = scatter(backs, plane, marks[0])
        rest = amplitudes.shape[1]
        came = swap(total([part[rest:] for part in parts]))
        keep = total([part[:rest] for part in parts])
        outs = back(keep, came, cols_own, cols_other, bits)
        parts, marks[1] = scatter(outs, line, marks[1])
        results.append(total(parts))
    return jnp.stack(results)


def solution(mesh):
    placed = (P(None, "row", "col"), P("row", "col"), P("row", "col"))
    rows, cols = mesh.shape["row"], mesh.shape["col"]
    return jax.shard_map(
        functools.partial(per_device, rows, cols), mesh=mesh, in_specs=placed, out_specs=P(None, "row", "col"), check_vma=False
    )
```

time: 231 us -> 200 us (0.87)
  waiting for transfers between devices: 149 us -> 100 us
  starting transfers between devices: 49.7 us -> 62.6 us
    ppermute x33, waiting for transfers between devices: 149 us -> 97.6 us  [the longest x15 64.1 us: in_line(): return lambda value: lax.ppermute(value, ('row', 'col'), pairs)]
    ppermute x33, starting transfers between devices: 45.9 us -> 54 us  [the longest x15 29 us: in_line(): return lambda value: lax.ppermute(value, ('row', 'col'), pairs)]
    ppermute x11 -> x13, starting transfers between devices: 3.78 us -> 8.51 us  [swap(): return lax.ppermute(value, 'row', [(r, r ^ 1) for r in range(rows)])]
    ppermute x11 -> x13, waiting for transfers between devices: 0.03 us -> 2.69 us  [swap(): return lax.ppermute(value, 'row', [(r, r ^ 1) for r in range(rows)])]
    pallas_call x1 -> x2, Pallas kernels: 15.9 us -> 14.1 us  [grid(): pl.pallas_call(functools.partial(grid_kernel, bits), out_shape=[jax.Shape...]
  transfers between devices with their start and end apart: 44 -> 46, of which waited for: 17 -> 20; matrix products, arithmetic and copies ran while one was open for 1% -> 2% of each run, Pallas kernels for 4% -> 14%
where the time goes in v2:
time: 200 us; the launch traced here: 199 us
  waiting for transfers between devices  100 us (50%)
  starting transfers between devices  62.6 us (31%)
  Pallas kernels  28.1 us (14%)
  local copies, waits for them, and re-layouts  6.38 us (3%)
    ppermute x15, waiting for transfers between devices, in_line(): return lambda value: lax.ppermute(value, ('row', 'col'), pairs)  64.1 us
    ppermute x18, waiting for transfers between devices, in_plane(): lax.ppermute(value, 'row', [(r, r ^ 2 * distance(r, mask)) for r in range...  33.5 us
    ppermute x15, starting transfers between devices, in_line(): return lambda value: lax.ppermute(value, ('row', 'col'), pairs)  29 us
    ppermute x18, starting transfers between devices, in_plane(): lax.ppermute(value, 'row', [(r, r ^ 2 * distance(r, mask)) for r in range...  25 us
    pallas_call x2, Pallas kernels, grid(): pl.pallas_call(functools.partial(grid_kernel, bits), out_shape=[jax.Shape...  14.1 us
    ppermute x13, starting transfers between devices, swap(): return lax.ppermute(value, 'row', [(r, r ^ 1) for r in range(rows)])  8.51 us
    pallas_call x2, Pallas kernels, back(): pl.pallas_call(functools.partial(back_kernel, bits), out_shape=[jax.Shape...  6.97 us
    pallas_call x2, Pallas kernels, project(): pl.pallas_call(functools.partial(project_kernel, bits), out_shape=[jax.Sh...  6.06 us
  transfers between devices with their start and end apart: 46, of which 20 were waited for; matrix products, arithmetic and copies ran while one was open for 2% of the time, Pallas kernels for 14%

profile of v2, /device:TPU:0, one launch (start us, length us, event | category | flops | bytes accessed | tf_op | source)
XLA Modules:
  0.0 199.4 jit_solution(9672873725069113392)
XLA Ops:
  0.0 3.0 %collective-permute-start = (bf16[256,1024]{1,0:T(8,128)(2,1)}, bf16[256,1024]{1,0:T(8,128)(2,1)S(1)}, u32[]{:S(2)}, u32[]{:S(2)}) collective-permute-start(bf16[256,1024]{1,0:T(8,128)(2,1)} %refs_2_.3), channel_id=1, source_target_pairs={{0,1},{1,0},{2,3},{3,2},{4,6},{5,7},{6,4},{7,5},{8,9},{9,8},{10,11... | collective-permute-start | bytes 1572872 | tf_op jit(solution)/shard_map/ppermute | solution.py:260
  3.0 2.6 %collective-permute-start.1 = (bf16[256,1024]{1,0:T(8,128)(2,1)}, bf16[256,1024]{1,0:T(8,128)(2,1)S(1)}, u32[]{:S(2)}, u32[]{:S(2)}) collective-permute-start(bf16[256,1024]{1,0:T(8,128)(2,1)} %refs_2_.3), channel_id=1, source_target_pairs={{0,2},{1,3},{2,0},{3,1},{4,5},{5,4},{6,7},{7,6},{8,10},{9,11},{10,... | collective-permute-start | bytes 1572872 | tf_op jit(solution)/shard_map/ppermute | solution.py:260
  5.6 1.5 collective-permute-start.6
  7.1 1.5 collective-permute-start.7
  8.6 18.1 %collective-permute-done.refs_1_ = bf16[256,1024]{1,0:T(8,128)(2,1)S(1)} collective-permute-done((bf16[256,1024]{1,0:T(8,128)(2,1)}, bf16[256,1024]{1,0:T(8,128)(2,1)S(1)}, u32[]{:S(2)}, u32[]{:S(2)}) %collective-permute-start) | collective-permute-done | bytes 524320 | tf_op jit(solution)/shard_map/ppermute | solution.py:260
  26.8 3.3 %collective-permute-start.2 = (bf16[256,1024]{1,0:T(8,128)(2,1)S(1)}, bf16[256,1024]{1,0:T(8,128)(2,1)S(1)}, u32[]{:S(2)}, u32[]{:S(2)}) collective-permute-start(bf16[256,1024]{1,0:T(8,128)(2,1)S(1)} %collective-permute-done.refs_1_), channel_id=1, source_target_pairs={{0,2},{1,3},{2,0},{3,1},{4,5},{5,4},{6,7},{7,6},{8,10},{9,11},{10,... | collective-permute-start | bytes 1572872 | tf_op jit(solution)/shard_map/ppermute | solution.py:260
  30.0 1.5 collective-permute-start.8
  32.1 1.8 slice_bitcast_fusion.1
  33.9 9.0 %collective-permute-done.2.refs_3_ = bf16[256,1024]{1,0:T(8,128)(2,1)S(1)} collective-permute-done((bf16[256,1024]{1,0:T(8,128)(2,1)S(1)}, bf16[256,1024]{1,0:T(8,128)(2,1)S(1)}, u32[]{:S(2)}, u32[]{:S(2)}) %collective-permute-start.2) | collective-permute-done | bytes 524320 | tf_op jit(solution)/shard_map/ppermute | solution.py:260
  43.7 3.4 %collective-permute-start.4 = (bf16[256,512]{1,0:T(8,128)(2,1)}, bf16[256,512]{1,0:T(8,128)(2,1)}, u32[]{:S(2)}, u32[]{:S(2)}) collective-permute-start(bf16[256,512]{1,0:T(8,128)(2,1)} %get-tuple-element.40.refs_0_), channel_id=1, source_target_pairs={{0,2},{1,3},{2,0},{3,1},{4,5},{5,4},{6,7},{7,6},{8,10},{9,11},{10,... | collective-permute-start | bytes 786440 | tf_op jit(solution)/shard_map/ppermute | solution.py:260
  51.0 1.5 collective-permute-start.14
  52.4 4.6 %collective-permute-done.3.refs_1_ = bf16[256,512]{1,0:T(8,128)(2,1)} collective-permute-done((bf16[256,512]{1,0:T(8,128)(2,1)}, bf16[256,512]{1,0:T(8,128)(2,1)}, u32[]{:S(2)}, u32[]{:S(2)}) %collective-permute-start.3) | collective-permute-done | bytes 262176 | tf_op jit(solution)/shard_map/ppermute | solution.py:260
  57.1 1.6 collective-permute-start.5
  58.7 1.5 collective-permute-start.15
  60.2 1.4 collective-permute-start.16
  61.6 1.7 constant_dynamic-slice_fusion
  63.4 2.7 %collective-permute-start.32 = (bf16[256,512]{1,0:T(8,128)(2,1)S(1)}, bf16[256,512]{1,0:T(8,128)(2,1)S(1)}, u32[]{:S(2)}, u32[]{:S(2)}) collective-permute-start(bf16[256,512]{1,0:T(8,128)(2,1)S(1)} %get-tuple-element.57.refs_0_), channel_id=1, source_target_pairs={{0,1},{1,0},{2,3},{3,2},{4,6},{5,7},{6,4},{7,5},{8,9},{9,8},{10,11... | collective-permute-start | bytes 786440 | tf_op jit(solution)/shard_map/ppermute | solution.py:260
  67.1 3.2 %project.2 = (bf16[256,512]{1,0:T(8,128)(2,1)S(1)}, bf16[256,512]{1,0:T(8,128)(2,1)S(1)}) custom-call(bf16[256,512]{1,0:T(8,128)(2,1)} %get-tuple-element.40.refs_0_, bf16[256,512]{1,0:T(8,128)(2,1)} %collective-permute-done.3.refs_1_, bf16[256,512]{1,0:T(8,128)(2,1)} %collective-permute-done.4.refs_2_, bf16[256,512]{1,0:T(8,128)(2,1)} %collective-permute-done.5.refs_3_, ...), custom_call_target="tpu_custom_call" | custom-call | flops 1 | bytes 1 | tf_op jit(solution)/shard_map/project/pallas_call | solution.py:85
  70.8 1.9 collective-permute-done.32.refs_1_
  73.9 1.9 collective-permute-start.34
  75.8 3.5 %collective-permute-done.15.refs_6_ = bf16[256,1024]{1,0:T(8,128)(2,1)S(1)} collective-permute-done((bf16[256,1024]{1,0:T(8,128)(2,1)}, bf16[256,1024]{1,0:T(8,128)(2,1)S(1)}, u32[]{:S(2)}, u32[]{:S(2)}) %collective-permute-start.15) | collective-permute-done | bytes 524320 | tf_op jit(solution)/shard_map/ppermute | solution.py:256
  79.3 1.5 collective-permute-start.17
  80.8 1.5 collective-permute-start.18
  82.3 3.1 %collective-permute-start.20 = (bf16[256,1024]{1,0:T(8,128)(2,1)S(1)}, bf16[256,1024]{1,0:T(8,128)(2,1)S(1)}, u32[]{:S(2)}, u32[]{:S(2)}) collective-permute-start(bf16[256,1024]{1,0:T(8,128)(2,1)S(1)} %copy-done.3), channel_id=1, source_target_pairs={{0,4},{4,0},{8,12},{12,8},{16,20},{20,16},{24,28},{28,24},{1,5},{5... | collective-permute-start | bytes 1572872 | tf_op jit(solution)/shard_map/ppermute | solution.py:253
  85.5 2.9 %project.3 = (bf16[256,512]{1,0:T(8,128)(2,1)S(1)}, bf16[256,512]{1,0:T(8,128)(2,1)S(1)}) custom-call(bf16[256,512]{1,0:T(8,128)(2,1)S(1)} %get-tuple-element.57.refs_0_, bf16[256,512]{1,0:T(8,128)(2,1)S(1)} %collective-permute-done.32.refs_1_, bf16[256,512]{1,0:T(8,128)(2,1)S(1)} %collective-permute-done.33.refs_2_, ...), custom_call_target="tpu_custom_call" | custom-call | flops 1 | bytes 1 | tf_op jit(solution)/shard_map/project/pallas_call | solution.py:85
  88.4 2.9 %collective-permute-start.35 = (bf16[256,512]{1,0:T(8,128)(2,1)S(1)}, bf16[256,512]{1,0:T(8,128)(2,1)S(1)}, u32[]{:S(2)}, u32[]{:S(2)}) collective-permute-start(bf16[256,512]{1,0:T(8,128)(2,1)S(1)} %get-tuple-element.59), channel_id=1, source_target_pairs={{0,4},{4,0},{8,12},{12,8},{16,20},{20,16},{24,28},{28,24},{1,5},{5... | collective-permute-start | bytes 786440 | tf_op jit(solution)/shard_map/ppermute | solution.py:253
  95.0 1.4 collective-permute-start.19
  97.1 9.7 %collective-permute-done.36.refs_1_ = bf16[512,512]{1,0:T(8,128)(2,1)S(1)} collective-permute-done((bf16[512,512]{1,0:T(8,128)(2,1)S(1)}, bf16[512,512]{1,0:T(8,128)(2,1)S(1)}, u32[]{:S(2)}, u32[]{:S(2)}) %collective-permute-start.36) | collective-permute-done | bytes 524320 | tf_op jit(solution)/shard_map/ppermute | solution.py:256
  106.7 2.0 collective-permute-start.38
  108.7 7.0 %grid.2 = (bf16[512,512]{1,0:T(8,128)(2,1)S(1)}, bf16[512,512]{1,0:T(8,128)(2,1)S(1)}, bf16[512,512]{1,0:T(8,128)(2,1)S(1)}, bf16[512,512]{1,0:T(8,128)(2,1)S(1)}) custom-call(bf16[512,512]{1,0:T(8,128)(2,1)S(1)} %constant_dynamic-update-slice_fusion.refs_0_, bf16[512,512]{1,0:T(8,128)(2,1)S(1)} %collective-permute-done.17.refs_1_, ...), custom_call_target="tpu_custom_call" | custom-call | flops 1 | bytes 1 | tf_op jit(solution)/shard_map/grid/pallas_call | solution.py:145
  116.2 1.6 collective-permute-start.25
  118.6 7.0 %grid.3 = (bf16[512,512]{1,0:T(8,128)(2,1)S(1)}, bf16[512,512]{1,0:T(8,128)(2,1)S(1)}, bf16[512,512]{1,0:T(8,128)(2,1)S(1)}, bf16[512,512]{1,0:T(8,128)(2,1)S(1)}) custom-call(bf16[512,512]{1,0:T(8,128)(2,1)S(1)} %constant_dynamic-update-slice_fusion.2.refs_0_, bf16[512,512]{1,0:T(8,128)(2,1)S(1)} %collective-permute-done.36.refs_1_, ...), custom_call_target="tpu_custom_call" | custom-call | flops 1 | bytes 1 | tf_op jit(solution)/shard_map/grid/pallas_call | solution.py:145
  125.7 5.0 %collective-permute-done.25 = bf16[512,512]{1,0:T(8,128)(2,1)S(1)} collective-permute-done((bf16[512,512]{1,0:T(8,128)(2,1)S(1)}, bf16[512,512]{1,0:T(8,128)(2,1)S(1)}, u32[]{:S(2)}, u32[]{:S(2)}) %collective-permute-start.25) | collective-permute-done | bytes 524320 | tf_op jit(solution)/shard_map/ppermute | solution.py:256
  131.7 1.5 collective-permute-start.27
  133.3 2.0 collective-permute-start.39
  135.3 10.1 %collective-permute-done.40 = bf16[512,512]{1,0:T(8,128)(2,1)S(1)} collective-permute-done((bf16[512,512]{1,0:T(8,128)(2,1)S(1)}, bf16[512,512]{1,0:T(8,128)(2,1)S(1)}, u32[]{:S(2)}, u32[]{:S(2)}) %collective-permute-start.40) | collective-permute-done | bytes 524320 | tf_op jit(solution)/shard_map/ppermute | solution.py:256
  147.0 1.5 collective-permute-done.28.refs_1_
  148.5 3.6 %back.2 = (bf16[256,512]{1,0:T(8,128)(2,1)S(1)}, bf16[256,512]{1,0:T(8,128)(2,1)S(1)}, bf16[256,512]{1,0:T(8,128)(2,1)S(1)}, bf16[256,512]{1,0:T(8,128)(2,1)S(1)}) custom-call(bf16[256,512]{1,0:T(8,128)(2,1)S(1)} %get-tuple-element.76.refs_0_, bf16[256,512]{1,0:T(8,128)(2,1)S(1)} %collective-permute-done.28.refs_1_, bf16[256,1024]{1,0:T(8,128)(2,1)S(1)} %copy-done.1, ...), custom_call_target="tpu_custom_call" | custom-call | flops 1 | bytes 1 | tf_op jit(solution)/shard_map/back/pallas_call | solution.py:193
  152.1 4.5 %collective-permute-done.39 = bf16[512,512]{1,0:T(8,128)(2,1)S(1)} collective-permute-done((bf16[512,512]{1,0:T(8,128)(2,1)S(1)}, bf16[512,512]{1,0:T(8,128)(2,1)S(1)}, u32[]{:S(2)}, u32[]{:S(2)}) %collective-permute-start.39) | collective-permute-done | bytes 524320 | tf_op jit(solution)/shard_map/ppermute | solution.py:256
  157.0 2.9 %collective-permute-start.30 = (bf16[256,512]{1,0:T(8,128)(2,1)S(1)}, bf16[256,512]{1,0:T(8,128)(2,1)S(1)}, u32[]{:S(2)}, u32[]{:S(2)}) collective-permute-start(bf16[256,512]{1,0:T(8,128)(2,1)S(1)} %get-tuple-element.55), channel_id=1, source_target_pairs={{0,2},{1,3},{2,0},{3,1},{4,5},{5,4},{6,7},{7,6},{8,10},{9,11},{10,... | collective-permute-start | bytes 786440 | tf_op jit(solution)/shard_map/ppermute | solution.py:260
  160.0 3.4 %back.3 = (bf16[256,512]{1,0:T(8,128)(2,1)S(1)}, bf16[256,512]{1,0:T(8,128)(2,1)S(1)}, bf16[256,512]{1,0:T(8,128)(2,1)S(1)}, bf16[256,512]{1,0:T(8,128)(2,1)S(1)}) custom-call(bf16[256,512]{1,0:T(8,128)(2,1)S(1)} %get-tuple-element.78.refs_0_, bf16[256,512]{1,0:T(8,128)(2,1)S(1)} %collective-permute-done.42.refs_1_, bf16[256,1024]{1,0:T(8,128)(2,1)S(1)} %copy-done.1, ...), custom_call_target="tpu_custom_call" | custom-call | flops 1 | bytes 1 | tf_op jit(solution)/shard_map/back/pallas_call | solution.py:193
  163.4 3.0 %collective-permute-done.30 = bf16[256,512]{1,0:T(8,128)(2,1)S(1)} collective-permute-done((bf16[256,512]{1,0:T(8,128)(2,1)S(1)}, bf16[256,512]{1,0:T(8,128)(2,1)S(1)}, u32[]{:S(2)}, u32[]{:S(2)}) %collective-permute-start.30) | collective-permute-done | bytes 262176 | tf_op jit(solution)/shard_map/ppermute | solution.py:260
  166.4 5.6 %collective-permute-done.29 = bf16[256,512]{1,0:T(8,128)(2,1)S(1)} collective-permute-done((bf16[256,512]{1,0:T(8,128)(2,1)S(1)}, bf16[256,512]{1,0:T(8,128)(2,1)S(1)}, u32[]{:S(2)}, u32[]{:S(2)}) %collective-permute-start.29) | collective-permute-done | bytes 262176 | tf_op jit(solution)/shard_map/ppermute | solution.py:260
  172.1 3.4 %collective-permute-start.44 = (bf16[256,512]{1,0:T(8,128)(2,1)S(1)}, bf16[256,512]{1,0:T(8,128)(2,1)S(1)}, u32[]{:S(2)}, u32[]{:S(2)}) collective-permute-start(bf16[256,512]{1,0:T(8,128)(2,1)S(1)} %get-tuple-element.72), channel_id=1, source_target_pairs={{0,2},{1,3},{2,0},{3,1},{4,5},{5,4},{6,7},{7,6},{8,10},{9,11},{10,... | collective-permute-start | bytes 786440 | tf_op jit(solution)/shard_map/ppermute | solution.py:260
  175.5 2.0 %collective-permute-start.31 = (bf16[256,512]{1,0:T(8,128)(2,1)S(1)}, bf16[256,512]{1,0:T(8,128)(2,1)S(1)}, u32[]{:S(2)}, u32[]{:S(2)}) collective-permute-start(bf16[256,512]{1,0:T(8,128)(2,1)S(1)} %add_convert_fusion.7), channel_id=1, source_target_pairs={{0,1},{1,0},{2,3},{3,2},{4,6},{5,7},{6,4},{7,5},{8,9},{9,8},{10,11... | collective-permute-start | bytes 786440 | tf_op jit(solution)/shard_map/ppermute | solution.py:260
  177.7 9.6 %collective-permute-done.44 = bf16[256,512]{1,0:T(8,128)(2,1)S(1)} collective-permute-done((bf16[256,512]{1,0:T(8,128)(2,1)S(1)}, bf16[256,512]{1,0:T(8,128)(2,1)S(1)}, u32[]{:S(2)}, u32[]{:S(2)}) %collective-permute-start.44) | collective-permute-done | bytes 262176 | tf_op jit(solution)/shard_map/ppermute | solution.py:260
  187.4 3.0 %collective-permute-done.31 = bf16[256,512]{1,0:T(8,128)(2,1)S(1)} collective-permute-done((bf16[256,512]{1,0:T(8,128)(2,1)S(1)}, bf16[256,512]{1,0:T(8,128)(2,1)S(1)}, u32[]{:S(2)}, u32[]{:S(2)}) %collective-permute-start.31) | collective-permute-done | bytes 262176 | tf_op jit(solution)/shard_map/ppermute | solution.py:260
  190.5 7.9 %collective-permute-done.43 = bf16[256,512]{1,0:T(8,128)(2,1)S(1)} collective-permute-done((bf16[256,512]{1,0:T(8,128)(2,1)S(1)}, bf16[256,512]{1,0:T(8,128)(2,1)S(1)}, u32[]{:S(2)}, u32[]{:S(2)}) %collective-permute-start.43) | collective-permute-done | bytes 262176 | tf_op jit(solution)/shard_map/ppermute | solution.py:260
  (78 shorter events, 18.3 us)
Async XLA Ops:
  0.0 26.7 %collective-permute-start = (bf16[256,1024]{1,0:T(8,128)(2,1)}, bf16[256,1024]{1,0:T(8,128)(2,1)S(1)}, u32[]{:S(2)}, u32[]{:S(2)}) collective-permute-start(bf16[256,1024]{1,0:T(8,128)(2,1)} %refs_2_.3), channel_id=1, source_target_pairs={{0,1},{1,0},{2,3},{3,2},{4,6},{5,7},{6,4},{7,5},{8,9},{9,8},{10,11... | collective-permute-start | bytes 1572872 | tf_op jit(solution)/shard_map/ppermute | solution.py:260
  3.0 23.7 %collective-permute-start.1 = (bf16[256,1024]{1,0:T(8,128)(2,1)}, bf16[256,1024]{1,0:T(8,128)(2,1)S(1)}, u32[]{:S(2)}, u32[]{:S(2)}) collective-permute-start(bf16[256,1024]{1,0:T(8,128)(2,1)} %refs_2_.3), channel_id=1, source_target_pairs={{0,2},{1,3},{2,0},{3,1},{4,5},{5,4},{6,7},{7,6},{8,10},{9,11},{10,... | collective-permute-start | bytes 1572872 | tf_op jit(solution)/shard_map/ppermute | solution.py:260
  5.6 24.4 %collective-permute-start.6 = (bf16[256,1024]{1,0:T(8,128)(2,1)}, bf16[256,1024]{1,0:T(8,128)(2,1)S(1)}, u32[]{:S(2)}, u32[]{:S(2)}) collective-permute-start(bf16[256,1024]{1,0:T(8,128)(2,1)} %refs_2_.3), channel_id=1, source_target_pairs={{0,8},{4,20},{8,0},{12,28},{16,24},{20,4},{24,16},{28,12},{1,9},{5... | collective-permute-start | bytes 1572872 | tf_op jit(solution)/shard_map/ppermute | solution.py:256
  7.1 25.0 %collective-permute-start.7 = (bf16[256,1024]{1,0:T(8,128)(2,1)}, bf16[256,1024]{1,0:T(8,128)(2,1)S(1)}, u32[]{:S(2)}, u32[]{:S(2)}) collective-permute-start(bf16[256,1024]{1,0:T(8,128)(2,1)} %refs_2_.3), channel_id=1, source_target_pairs={{0,16},{4,12},{8,24},{12,4},{16,0},{20,28},{24,8},{28,20},{1,17},{... | collective-permute-start | bytes 1572872 | tf_op jit(solution)/shard_map/ppermute | solution.py:256
  26.8 16.1 %collective-permute-start.2 = (bf16[256,1024]{1,0:T(8,128)(2,1)S(1)}, bf16[256,1024]{1,0:T(8,128)(2,1)S(1)}, u32[]{:S(2)}, u32[]{:S(2)}) collective-permute-start(bf16[256,1024]{1,0:T(8,128)(2,1)S(1)} %collective-permute-done.refs_1_), channel_id=1, source_target_pairs={{0,2},{1,3},{2,0},{3,1},{4,5},{5,4},{6,7},{7,6},{8,10},{9,11},{10,... | collective-permute-start | bytes 1572872 | tf_op jit(solution)/shard_map/ppermute | solution.py:260
  30.0 12.8 %collective-permute-start.8 = (bf16[256,1024]{1,0:T(8,128)(2,1)S(1)}, bf16[256,1024]{1,0:T(8,128)(2,1)S(1)}, u32[]{:S(2)}, u32[]{:S(2)}) collective-permute-start(bf16[256,1024]{1,0:T(8,128)(2,1)S(1)} %collective-permute-done.6.refs_5_.refs_3_), channel_id=1, source_target_pairs={{0,16},{4,12},{8,24},{12,4},{16,0},{20,28},{24,8},{28,20},{1,17},{... | collective-permute-start | bytes 1572872 | tf_op jit(solution)/shard_map/ppermute | solution.py:256
  31.6 12.1 %collective-permute-start.9 = (bf16[256,1024]{1,0:T(8,128)(2,1)}, bf16[256,1024]{1,0:T(8,128)(2,1)S(1)}, u32[]{:S(2)}, u32[]{:S(2)}) collective-permute-start(bf16[256,1024]{1,0:T(8,128)(2,1)} %refs_2_.3), channel_id=1, source_target_pairs={{0,4},{4,0},{8,12},{12,8},{16,20},{20,16},{24,28},{28,24},{1,5},{5... | collective-permute-start | bytes 1572872 | tf_op jit(solution)/shard_map/ppermute | solution.py:253
  31.6 18.4 %collective-permute-start.10 = (bf16[256,1024]{1,0:T(8,128)(2,1)S(1)}, bf16[256,1024]{1,0:T(8,128)(2,1)S(1)}, u32[]{:S(2)}, u32[]{:S(2)}) collective-permute-start(bf16[256,1024]{1,0:T(8,128)(2,1)S(1)} %collective-permute-done.6.refs_5_.refs_3_), channel_id=1, source_target_pairs={{0,4},{4,0},{8,12},{12,8},{16,20},{20,16},{24,28},{28,24},{1,5},{5... | collective-permute-start | bytes 1572872 | tf_op jit(solution)/shard_map/ppermute | solution.py:253
  32.1 26.6 %collective-permute-start.11 = (bf16[256,1024]{1,0:T(8,128)(2,1)S(1)}, bf16[256,1024]{1,0:T(8,128)(2,1)S(1)}, u32[]{:S(2)}, u32[]{:S(2)}) collective-permute-start(bf16[256,1024]{1,0:T(8,128)(2,1)S(1)} %collective-permute-done.7.refs_6_.refs_4_), channel_id=1, source_target_pairs={{0,4},{4,0},{8,12},{12,8},{16,20},{20,16},{24,28},{28,24},{1,5},{5... | collective-permute-start | bytes 1572872 | tf_op jit(solution)/shard_map/ppermute | solution.py:253
  42.9 20.5 %collective-permute-start.12 = (bf16[256,1024]{1,0:T(8,128)(2,1)S(1)}, bf16[256,1024]{1,0:T(8,128)(2,1)}, u32[]{:S(2)}, u32[]{:S(2)}) collective-permute-start(bf16[256,1024]{1,0:T(8,128)(2,1)S(1)} %collective-permute-done.8.refs_7_.refs_5_), channel_id=1, source_target_pairs={{0,4},{4,0},{8,12},{12,8},{16,20},{20,16},{24,28},{28,24},{1,5},{5... | collective-permute-start | bytes 1572872 | tf_op jit(solution)/shard_map/ppermute | solution.py:253
  42.9 14.2 %collective-permute-start.3 = (bf16[256,512]{1,0:T(8,128)(2,1)}, bf16[256,512]{1,0:T(8,128)(2,1)}, u32[]{:S(2)}, u32[]{:S(2)}) collective-permute-start(bf16[256,512]{1,0:T(8,128)(2,1)} %get-tuple-element.40.refs_0_), channel_id=1, source_target_pairs={{0,1},{1,0},{2,3},{3,2},{4,6},{5,7},{6,4},{7,5},{8,9},{9,8},{10,11... | collective-permute-start | bytes 786440 | tf_op jit(solution)/shard_map/ppermute | solution.py:260
  43.7 16.5 %collective-permute-start.4 = (bf16[256,512]{1,0:T(8,128)(2,1)}, bf16[256,512]{1,0:T(8,128)(2,1)}, u32[]{:S(2)}, u32[]{:S(2)}) collective-permute-start(bf16[256,512]{1,0:T(8,128)(2,1)} %get-tuple-element.40.refs_0_), channel_id=1, source_target_pairs={{0,2},{1,3},{2,0},{3,1},{4,5},{5,4},{6,7},{7,6},{8,10},{9,11},{10,... | collective-permute-start | bytes 786440 | tf_op jit(solution)/shard_map/ppermute | solution.py:260
  51.0 19.3 %collective-permute-start.14 = (bf16[256,1024]{1,0:T(8,128)(2,1)}, bf16[256,1024]{1,0:T(8,128)(2,1)}, u32[]{:S(2)}, u32[]{:S(2)}) collective-permute-start(bf16[256,1024]{1,0:T(8,128)(2,1)} %get-tuple-element.43), channel_id=1, source_target_pairs={{0,8},{4,20},{8,0},{12,28},{16,24},{20,4},{24,16},{28,12},{1,9},{5... | collective-permute-start | bytes 1572872 | tf_op jit(solution)/shard_map/ppermute | solution.py:256
  57.1 10.0 %collective-permute-start.5 = (bf16[256,512]{1,0:T(8,128)(2,1)}, bf16[256,512]{1,0:T(8,128)(2,1)}, u32[]{:S(2)}, u32[]{:S(2)}) collective-permute-start(bf16[256,512]{1,0:T(8,128)(2,1)} %collective-permute-done.3.refs_1_), channel_id=1, source_target_pairs={{0,2},{1,3},{2,0},{3,1},{4,5},{5,4},{6,7},{7,6},{8,10},{9,11},{10,... | collective-permute-start | bytes 786440 | tf_op jit(solution)/shard_map/ppermute | solution.py:260
  58.7 20.6 %collective-permute-start.15 = (bf16[256,1024]{1,0:T(8,128)(2,1)}, bf16[256,1024]{1,0:T(8,128)(2,1)S(1)}, u32[]{:S(2)}, u32[]{:S(2)}) collective-permute-start(bf16[256,1024]{1,0:T(8,128)(2,1)} %copy-done.5), channel_id=1, source_target_pairs={{0,16},{4,12},{8,24},{12,4},{16,0},{20,28},{24,8},{28,20},{1,17},{... | collective-permute-start | bytes 1572872 | tf_op jit(solution)/shard_map/ppermute | solution.py:256
  60.2 6.9 %copy-start.1 = (bf16[256,1024]{1,0:T(8,128)(2,1)S(1)}, bf16[256,1024]{1,0:T(8,128)(2,1)}, u32[]{:S(2)}) copy-start(bf16[256,1024]{1,0:T(8,128)(2,1)} %refs_2_.3) | copy-start | bytes 1572868
  60.2 19.1 %collective-permute-start.16 = (bf16[256,1024]{1,0:T(8,128)(2,1)}, bf16[256,1024]{1,0:T(8,128)(2,1)S(1)}, u32[]{:S(2)}, u32[]{:S(2)}) collective-permute-start(bf16[256,1024]{1,0:T(8,128)(2,1)} %copy-done.4), channel_id=1, source_target_pairs={{0,24},{4,28},{8,16},{12,20},{16,8},{20,12},{24,0},{28,4},{1,25},{... | collective-permute-start | bytes 1572872 | tf_op jit(solution)/shard_map/ppermute | solution.py:256
  63.4 9.4 %collective-permute-start.32 = (bf16[256,512]{1,0:T(8,128)(2,1)S(1)}, bf16[256,512]{1,0:T(8,128)(2,1)S(1)}, u32[]{:S(2)}, u32[]{:S(2)}) collective-permute-start(bf16[256,512]{1,0:T(8,128)(2,1)S(1)} %get-tuple-element.57.refs_0_), channel_id=1, source_target_pairs={{0,1},{1,0},{2,3},{3,2},{4,6},{5,7},{6,4},{7,5},{8,9},{9,8},{10,11... | collective-permute-start | bytes 786440 | tf_op jit(solution)/shard_map/ppermute | solution.py:260
  67.1 15.2 %copy-start.3 = (bf16[256,1024]{1,0:T(8,128)(2,1)S(1)}, bf16[256,1024]{1,0:T(8,128)(2,1)}, u32[]{:S(2)}) copy-start(bf16[256,1024]{1,0:T(8,128)(2,1)} %copy-done.2) | copy-start | bytes 1572868
  67.1 27.2 %collective-permute-start.24 = (f32[512,512]{1,0:T(8,128)S(1)}, f32[512,512]{1,0:T(8,128)S(1)}, u32[]{:S(2)}, u32[]{:S(2)}) collective-permute-start(f32[512,512]{1,0:T(8,128)S(1)} %get-tuple-element.73), channel_id=1, source_target_pairs={{0,4},{4,0},{8,12},{12,8},{16,20},{20,16},{24,28},{28,24},{1,5},{5... | collective-permute-start | bytes 3145736 | tf_op jit(solution)/shard_map/ppermute | solution.py:253
  70.3 3.6 %collective-permute-start.13 = (bf16[256,512]{1,0:T(8,128)(2,1)S(1)}, bf16[256,512]{1,0:T(8,128)(2,1)S(1)}, u32[]{:S(2)}, u32[]{:S(2)}) collective-permute-start(bf16[256,512]{1,0:T(8,128)(2,1)S(1)} %get-tuple-element.42), channel_id=1, source_target_pairs={{0,4},{4,0},{8,12},{12,8},{16,20},{20,16},{24,28},{28,24},{1,5},{5... | collective-permute-start | bytes 786440 | tf_op jit(solution)/shard_map/ppermute | solution.py:253
  72.8 9.5 %collective-permute-start.33 = (bf16[256,512]{1,0:T(8,128)(2,1)S(1)}, bf16[256,512]{1,0:T(8,128)(2,1)S(1)}, u32[]{:S(2)}, u32[]{:S(2)}) collective-permute-start(bf16[256,512]{1,0:T(8,128)(2,1)S(1)} %get-tuple-element.57.refs_0_), channel_id=1, source_target_pairs={{0,2},{1,3},{2,0},{3,1},{4,5},{5,4},{6,7},{7,6},{8,10},{9,11},{10,... | collective-permute-start | bytes 786440 | tf_op jit(solution)/shard_map/ppermute | solution.py:260
  73.9 11.6 %collective-permute-start.34 = (bf16[256,512]{1,0:T(8,128)(2,1)S(1)}, bf16[256,512]{1,0:T(8,128)(2,1)S(1)}, u32[]{:S(2)}, u32[]{:S(2)}) collective-permute-start(bf16[256,512]{1,0:T(8,128)(2,1)S(1)} %collective-permute-done.32.refs_1_), channel_id=1, source_target_pairs={{0,2},{1,3},{2,0},{3,1},{4,5},{5,4},{6,7},{7,6},{8,10},{9,11},{10,... | collective-permute-start | bytes 786440 | tf_op jit(solution)/shard_map/ppermute | solution.py:260
  79.3 13.5 %collective-permute-start.17 = (bf16[512,512]{1,0:T(8,128)(2,1)S(1)}, bf16[512,512]{1,0:T(8,128)(2,1)S(1)}, u32[]{:S(2)}, u32[]{:S(2)}) collective-permute-start(bf16[512,512]{1,0:T(8,128)(2,1)S(1)} %constant_dynamic-update-slice_fusion.refs_0_), channel_id=1, source_target_pairs={{0,8},{4,20},{8,0},{12,28},{16,24},{20,4},{24,16},{28,12},{1,9},{5... | collective-permute-start | bytes 1572872 | tf_op jit(solution)/shard_map/ppermute | solution.py:256
  80.8 12.2 %collective-permute-start.18 = (bf16[512,512]{1,0:T(8,128)(2,1)S(1)}, bf16[512,512]{1,0:T(8,128)(2,1)S(1)}, u32[]{:S(2)}, u32[]{:S(2)}) collective-permute-start(bf16[512,512]{1,0:T(8,128)(2,1)S(1)} %constant_dynamic-update-slice_fusion.refs_0_), channel_id=1, source_target_pairs={{0,16},{4,12},{8,24},{12,4},{16,0},{20,28},{24,8},{28,20},{1,17},{... | collective-permute-start | bytes 1572872 | tf_op jit(solution)/shard_map/ppermute | solution.py:256
  82.3 12.7 %collective-permute-start.20 = (bf16[256,1024]{1,0:T(8,128)(2,1)S(1)}, bf16[256,1024]{1,0:T(8,128)(2,1)S(1)}, u32[]{:S(2)}, u32[]{:S(2)}) collective-permute-start(bf16[256,1024]{1,0:T(8,128)(2,1)S(1)} %copy-done.3), channel_id=1, source_target_pairs={{0,4},{4,0},{8,12},{12,8},{16,20},{20,16},{24,28},{28,24},{1,5},{5... | collective-permute-start | bytes 1572872 | tf_op jit(solution)/shard_map/ppermute | solution.py:253
  88.4 4.0 %collective-permute-start.35 = (bf16[256,512]{1,0:T(8,128)(2,1)S(1)}, bf16[256,512]{1,0:T(8,128)(2,1)S(1)}, u32[]{:S(2)}, u32[]{:S(2)}) collective-permute-start(bf16[256,512]{1,0:T(8,128)(2,1)S(1)} %get-tuple-element.59), channel_id=1, source_target_pairs={{0,4},{4,0},{8,12},{12,8},{16,20},{20,16},{24,28},{28,24},{1,5},{5... | collective-permute-start | bytes 786440 | tf_op jit(solution)/shard_map/ppermute | solution.py:253
  92.4 4.1 %collective-permute-start.21 = (bf16[256,1024]{1,0:T(8,128)(2,1)}, bf16[256,1024]{1,0:T(8,128)(2,1)S(1)}, u32[]{:S(2)}, u32[]{:S(2)}) collective-permute-start(bf16[256,1024]{1,0:T(8,128)(2,1)} %collective-permute-done.14.refs_5_), channel_id=1, source_target_pairs={{0,4},{4,0},{8,12},{12,8},{16,20},{20,16},{24,28},{28,24},{1,5},{5... | collective-permute-start | bytes 1572872 | tf_op jit(solution)/shard_map/ppermute | solution.py:253
  92.8 15.9 %collective-permute-start.22 = (bf16[256,1024]{1,0:T(8,128)(2,1)S(1)}, bf16[256,1024]{1,0:T(8,128)(2,1)S(1)}, u32[]{:S(2)}, u32[]{:S(2)}) collective-permute-start(bf16[256,1024]{1,0:T(8,128)(2,1)S(1)} %collective-permute-done.15.refs_6_), channel_id=1, source_target_pairs={{0,4},{4,0},{8,12},{12,8},{16,20},{20,16},{24,28},{28,24},{1,5},{5... | collective-permute-start | bytes 1572872 | tf_op jit(solution)/shard_map/ppermute | solution.py:253
  93.0 13.7 %collective-permute-start.36 = (bf16[512,512]{1,0:T(8,128)(2,1)S(1)}, bf16[512,512]{1,0:T(8,128)(2,1)S(1)}, u32[]{:S(2)}, u32[]{:S(2)}) collective-permute-start(bf16[512,512]{1,0:T(8,128)(2,1)S(1)} %constant_dynamic-update-slice_fusion.2.refs_0_), channel_id=1, source_target_pairs={{0,8},{4,20},{8,0},{12,28},{16,24},{20,4},{24,16},{28,12},{1,9},{5... | collective-permute-start | bytes 1572872 | tf_op jit(solution)/shard_map/ppermute | solution.py:256
  94.3 14.4 %collective-permute-start.23 = (bf16[256,1024]{1,0:T(8,128)(2,1)S(1)}, bf16[256,1024]{1,0:T(8,128)(2,1)S(1)}, u32[]{:S(2)}, u32[]{:S(2)}) collective-permute-start(bf16[256,1024]{1,0:T(8,128)(2,1)S(1)} %collective-permute-done.16.refs_7_), channel_id=1, source_target_pairs={{0,4},{4,0},{8,12},{12,8},{16,20},{20,16},{24,28},{28,24},{1,5},{5... | collective-permute-start | bytes 1572872 | tf_op jit(solution)/shard_map/ppermute | solution.py:253
  95.0 13.7 %collective-permute-start.19 = (bf16[512,512]{1,0:T(8,128)(2,1)S(1)}, bf16[512,512]{1,0:T(8,128)(2,1)S(1)}, u32[]{:S(2)}, u32[]{:S(2)}) collective-permute-start(bf16[512,512]{1,0:T(8,128)(2,1)S(1)} %collective-permute-done.17.refs_1_), channel_id=1, source_target_pairs={{0,16},{4,12},{8,24},{12,4},{16,0},{20,28},{24,8},{28,20},{1,17},{... | collective-permute-start | bytes 1572872 | tf_op jit(solution)/shard_map/ppermute | solution.py:256
  96.5 21.4 %collective-permute-start.37 = (bf16[512,512]{1,0:T(8,128)(2,1)S(1)}, bf16[512,512]{1,0:T(8,128)(2,1)S(1)}, u32[]{:S(2)}, u32[]{:S(2)}) collective-permute-start(bf16[512,512]{1,0:T(8,128)(2,1)S(1)} %constant_dynamic-update-slice_fusion.2.refs_0_), channel_id=1, source_target_pairs={{0,16},{4,12},{8,24},{12,4},{16,0},{20,28},{24,8},{28,20},{1,17},{... | collective-permute-start | bytes 1572872 | tf_op jit(solution)/shard_map/ppermute | solution.py:256
  106.7 11.9 %collective-permute-start.38 = (bf16[512,512]{1,0:T(8,128)(2,1)S(1)}, bf16[512,512]{1,0:T(8,128)(2,1)S(1)}, u32[]{:S(2)}, u32[]{:S(2)}) collective-permute-start(bf16[512,512]{1,0:T(8,128)(2,1)S(1)} %collective-permute-done.36.refs_1_), channel_id=1, source_target_pairs={{0,16},{4,12},{8,24},{12,4},{16,0},{20,28},{24,8},{28,20},{1,17},{... | collective-permute-start | bytes 1572872 | tf_op jit(solution)/shard_map/ppermute | solution.py:256
  115.8 9.9 %collective-permute-start.26 = (bf16[512,512]{1,0:T(8,128)(2,1)S(1)}, bf16[512,512]{1,0:T(8,128)(2,1)S(1)}, u32[]{:S(2)}, u32[]{:S(2)}) collective-permute-start(bf16[512,512]{1,0:T(8,128)(2,1)S(1)} %get-tuple-element.51), channel_id=1, source_target_pairs={{0,16},{4,12},{8,24},{12,4},{16,0},{20,28},{24,8},{28,20},{1,17},{... | collective-permute-start | bytes 1572872 | tf_op jit(solution)/shard_map/ppermute | solution.py:256
  116.2 14.4 %collective-permute-start.25 = (bf16[512,512]{1,0:T(8,128)(2,1)S(1)}, bf16[512,512]{1,0:T(8,128)(2,1)S(1)}, u32[]{:S(2)}, u32[]{:S(2)}) collective-permute-start(bf16[512,512]{1,0:T(8,128)(2,1)S(1)} %get-tuple-element.49), channel_id=1, source_target_pairs={{0,16},{4,12},{8,24},{12,4},{16,0},{20,28},{24,8},{28,20},{1,17},{... | collective-permute-start | bytes 1572872 | tf_op jit(solution)/shard_map/ppermute | solution.py:256
  130.6 14.7 %collective-permute-start.40 = (bf16[512,512]{1,0:T(8,128)(2,1)S(1)}, bf16[512,512]{1,0:T(8,128)(2,1)S(1)}, u32[]{:S(2)}, u32[]{:S(2)}) collective-permute-start(bf16[512,512]{1,0:T(8,128)(2,1)S(1)} %get-tuple-element.66), channel_id=1, source_target_pairs={{0,16},{4,12},{8,24},{12,4},{16,0},{20,28},{24,8},{28,20},{1,17},{... | collective-permute-start | bytes 1572872 | tf_op jit(solution)/shard_map/ppermute | solution.py:256
  131.7 15.0 %collective-permute-start.27 = (bf16[512,512]{1,0:T(8,128)(2,1)S(1)}, bf16[512,512]{1,0:T(8,128)(2,1)S(1)}, u32[]{:S(2)}, u32[]{:S(2)}) collective-permute-start(bf16[512,512]{1,0:T(8,128)(2,1)S(1)} %add_convert_fusion.1), channel_id=1, source_target_pairs={{0,8},{4,20},{8,0},{12,28},{16,24},{20,4},{24,16},{28,12},{1,9},{5... | collective-permute-start | bytes 1572872 | tf_op jit(solution)/shard_map/ppermute | solution.py:256
  133.3 23.3 %collective-permute-start.39 = (bf16[512,512]{1,0:T(8,128)(2,1)S(1)}, bf16[512,512]{1,0:T(8,128)(2,1)S(1)}, u32[]{:S(2)}, u32[]{:S(2)}) collective-permute-start(bf16[512,512]{1,0:T(8,128)(2,1)S(1)} %get-tuple-element.63), channel_id=1, source_target_pairs={{0,16},{4,12},{8,24},{12,4},{16,0},{20,28},{24,8},{28,20},{1,17},{... | collective-permute-start | bytes 1572872 | tf_op jit(solution)/shard_map/ppermute | solution.py:256
  145.5 11.1 %collective-permute-start.41 = (bf16[512,512]{1,0:T(8,128)(2,1)S(1)}, bf16[512,512]{1,0:T(8,128)(2,1)S(1)}, u32[]{:S(2)}, u32[]{:S(2)}) collective-permute-start(bf16[512,512]{1,0:T(8,128)(2,1)S(1)} %add_convert_fusion), channel_id=1, source_target_pairs={{0,8},{4,20},{8,0},{12,28},{16,24},{20,4},{24,16},{28,12},{1,9},{5... | collective-permute-start | bytes 1572872 | tf_op jit(solution)/shard_map/ppermute | solution.py:256
  146.9 1.6 collective-permute-start.28
  156.8 3.2 %collective-permute-start.42 = (bf16[256,512]{1,0:T(8,128)(2,1)S(1)}, bf16[256,512]{1,0:T(8,128)(2,1)S(1)}, u32[]{:S(2)}, u32[]{:S(2)}) collective-permute-start(bf16[256,512]{1,0:T(8,128)(2,1)S(1)} %get-tuple-element.77), channel_id=1, source_target_pairs={{0,4},{4,0},{8,12},{12,8},{16,20},{20,16},{24,28},{28,24},{1,5},{5... | collective-permute-start | bytes 786440 | tf_op jit(solution)/shard_map/ppermute | solution.py:253
  157.0 9.4 %collective-permute-start.30 = (bf16[256,512]{1,0:T(8,128)(2,1)S(1)}, bf16[256,512]{1,0:T(8,128)(2,1)S(1)}, u32[]{:S(2)}, u32[]{:S(2)}) collective-permute-start(bf16[256,512]{1,0:T(8,128)(2,1)S(1)} %get-tuple-element.55), channel_id=1, source_target_pairs={{0,2},{1,3},{2,0},{3,1},{4,5},{5,4},{6,7},{7,6},{8,10},{9,11},{10,... | collective-permute-start | bytes 786440 | tf_op jit(solution)/shard_map/ppermute | solution.py:260
  159.9 12.1 %collective-permute-start.29 = (bf16[256,512]{1,0:T(8,128)(2,1)S(1)}, bf16[256,512]{1,0:T(8,128)(2,1)S(1)}, u32[]{:S(2)}, u32[]{:S(2)}) collective-permute-start(bf16[256,512]{1,0:T(8,128)(2,1)S(1)} %get-tuple-element.53), channel_id=1, source_target_pairs={{0,2},{1,3},{2,0},{3,1},{4,5},{5,4},{6,7},{7,6},{8,10},{9,11},{10,... | collective-permute-start | bytes 786440 | tf_op jit(solution)/shard_map/ppermute | solution.py:260
  172.1 15.2 %collective-permute-start.44 = (bf16[256,512]{1,0:T(8,128)(2,1)S(1)}, bf16[256,512]{1,0:T(8,128)(2,1)S(1)}, u32[]{:S(2)}, u32[]{:S(2)}) collective-permute-start(bf16[256,512]{1,0:T(8,128)(2,1)S(1)} %get-tuple-element.72), channel_id=1, source_target_pairs={{0,2},{1,3},{2,0},{3,1},{4,5},{5,4},{6,7},{7,6},{8,10},{9,11},{10,... | collective-permute-start | bytes 786440 | tf_op jit(solution)/shard_map/ppermute | solution.py:260
  175.5 14.9 %collective-permute-start.31 = (bf16[256,512]{1,0:T(8,128)(2,1)S(1)}, bf16[256,512]{1,0:T(8,128)(2,1)S(1)}, u32[]{:S(2)}, u32[]{:S(2)}) collective-permute-start(bf16[256,512]{1,0:T(8,128)(2,1)S(1)} %add_convert_fusion.7), channel_id=1, source_target_pairs={{0,1},{1,0},{2,3},{3,2},{4,6},{5,7},{6,4},{7,5},{8,9},{9,8},{10,11... | collective-permute-start | bytes 786440 | tf_op jit(solution)/shard_map/ppermute | solution.py:260
  177.5 21.0 %collective-permute-start.43 = (bf16[256,512]{1,0:T(8,128)(2,1)S(1)}, bf16[256,512]{1,0:T(8,128)(2,1)S(1)}, u32[]{:S(2)}, u32[]{:S(2)}) collective-permute-start(bf16[256,512]{1,0:T(8,128)(2,1)S(1)} %get-tuple-element.69), channel_id=1, source_target_pairs={{0,2},{1,3},{2,0},{3,1},{4,5},{5,4},{6,7},{7,6},{8,10},{9,11},{10,... | collective-permute-start | bytes 786440 | tf_op jit(solution)/shard_map/ppermute | solution.py:260
  187.3 11.1 %collective-permute-start.45 = (bf16[256,512]{1,0:T(8,128)(2,1)S(1)}, bf16[256,512]{1,0:T(8,128)(2,1)S(1)}, u32[]{:S(2)}, u32[]{:S(2)}) collective-permute-start(bf16[256,512]{1,0:T(8,128)(2,1)S(1)} %add_convert_fusion.3), channel_id=1, source_target_pairs={{0,1},{1,0},{2,3},{3,2},{4,6},{5,7},{6,4},{7,5},{8,9},{9,8},{10,11... | collective-permute-start | bytes 786440 | tf_op jit(solution)/shard_map/ppermute | solution.py:260
  (4 other events, 3.7 us)

commit v3 on v2

--- a/solution.py
+++ b/solution.py
@@ -60,19 +60,15 @@
     core, base = where_am_i(bits)
     rows, width = own[0].shape
     depth = terms[0].shape[1]
-    pairs = plane_pairs(own, other, room, core, rows, bits) + [(terms[l], held.at[l]) for l in range(n)]
-    for copy in copy_all(pairs, sems):
-        copy.wait()
-    tile = min(width // 2, 512)
-
-    @pl.loop(0, width // tile)
-    def _(step):
-        at = pl.ds(pl.multiple_of(step * tile, tile), tile)
-        acc = jnp.zeros((rows, tile), F32)
-        for l in range(n):
-            start = pl.multiple_of((base ^ l) * depth, depth)
-            acc = acc + jnp.dot(held[l], room[pl.ds(start, depth), at], preferred_element_type=F32)
-        result[:, at] = acc.astype(BF16)
+    loads = copy_all([(terms[l], held.at[l]) for l in range(n)] + plane_pairs(own, other, room, core, rows, bits), sems)
+    for copy in loads[:n]:
+        copy.wait()
+    acc = jnp.zeros((rows, width), F32)
+    for j in range(n):
+        loads[n + j].wait()
+        loads[2 * n + flipped(j, bits)].wait()
+        acc = acc + jnp.dot(held[base ^ j], room[pl.ds(j * depth, depth), :], preferred_element_type=F32)
+    result[...] = acc.astype(BF16)
 
     for copy in copy_all(list(zip(halves(result, core), (keep, away))), sems):
         copy.wait()
@@ -104,7 +100,7 @@
     proj_in, own, other = refs[:n], refs[n : 2 * n], refs[2 * n : 3 * n]
     kernel_own, kernel_other = refs[3 * n : 3 * n + 2]
     outs = refs[3 * n + 2 : 4 * n + 2]
-    proj, room, coulomb, scaled, result, sems, tile_sems, out_sems = refs[4 * n + 2 :]
+    proj, room, coulomb, total_ref, scaled, result, sems, tile_sems, out_sems = refs[4 * n + 2 :]
     core, _ = where_am_i(bits)
     rows = own[0].shape[0]
     half = kernel_own.shape[0]
@@ -115,17 +111,15 @@
         pairs.append((proj_in[j], proj.at[pl.ds(2 * j * rows, 2 * rows)]))
     loads = copy_all(pairs, sems)
     late = copy_all([(kernel_own, coulomb.at[pl.ds(core * half, half)]), (kernel_other, coulomb.at[pl.ds((1 - core) * half, half)])], tile_sems)
-    for copy in loads:
-        copy.wait()
+    for j in range(n):
+        at = pl.ds(2 * j * rows, 2 * rows)
+        for copy in loads[3 * j : 3 * j + 3]:
+            copy.wait()
+        term = lax.dot_general(room[at, :], proj[at, :], (((0,), (0,)), ((), ())), preferred_element_type=F32)
+        total_ref[...] = term if j == 0 else total_ref[...] + term
     for copy in late:
         copy.wait()
-    tile = min(proj.shape[1], 256)
-
-    @pl.loop(0, proj.shape[1] // tile)
-    def _(step):
-        at = pl.ds(pl.multiple_of(step * tile, tile), tile)
-        grid = lax.dot_general(room[...], proj[:, at], (((0,), (0,)), ((), ())), preferred_element_type=F32)
-        scaled[:, at] = (coulomb[:, at] * grid).astype(BF16)
+    scaled[...] = (coulomb[...] * total_ref[...]).astype(BF16)
 
     copies = []
     for j in range(n - 1, -1, -1):
@@ -150,6 +144,7 @@
         scratch_shapes=[
             pltpu.VMEM((2 * n * rows, cols), BF16),
             pltpu.VMEM((2 * n * rows, width), BF16),
+            pltpu.VMEM((width, cols), F32),
             pltpu.VMEM((width, cols), F32),
             pltpu.VMEM((width, cols), BF16),
             pltpu.VMEM((2 * n * rows, cols), BF16),
@@ -276,7 +271,7 @@
             n = 1 << t
             away = blocks[n:]
             if gates is not None and marks is None:
-                away = [after(block, *gates) for block in away]
+                away = [after(block, *gates[:1]) for j, block in enumerate(away)]
             got = [sends[t](block) for block in away]
             marks = got if marks is None else marks
             parts.append(got[0])
@@ -293,13 +288,13 @@
     kernel_other = swap(kernel_away)
     cols_other = [swap(b) for b in cols_own]
     terms = [gather(amplitudes[0], line, [[line_own[-1]]] * bits)]
-    terms.append(gather(amplitudes[1], line, [[terms[0][1]]] + [[terms[0][-1]]] * (bits - 1)))
+    terms.append(gather(amplitudes[1], line, [[terms[0][1]]] * bits))
 
     pieces = pick(line_own, bits)
     first_own = [pieces[0]] + [in_plane(j)(pieces[j]) for j in range(1, chips)]
     first_other = [swap(b) for b in first_own]
 
-    gates, results, marks = first_own[1:], [], [None, None]
+    gates, results, marks, outs = first_own[1:], [], [None, None], ()
     for pair in range(amplitudes.shape[0]):
         keep, away = project(terms[pair], cols_own, cols_other, bits)
         block = jnp.concatenate([keep, swap(away)])
@@ -307,6 +302,7 @@
         gates = proj[1:3]
         backs = grid(proj, first_own, first_other, kernel_own, kernel_other, bits)
         parts, marks[0] = scatter(backs, plane, marks[0])
+        parts = [after(part, *outs) if outs else part for part in parts]
         rest = amplitudes.shape[1]
         came = swap(total([part[rest:] for part in parts]))
         keep = total([part[:rest] for part in parts])

time: 200 us -> 192 us (0.960)
  waiting for transfers between devices: 100 us -> 85.5 us
  starting transfers between devices: 62.6 us -> 70.9 us
  Pallas kernels: 28.1 us -> 25.5 us
    ppermute x15, waiting for transfers between devices: 64.1 us -> 51.9 us  [in_line(): return lambda value: lax.ppermute(value, ('row', 'col'), pairs)]
    ppermute x15, starting transfers between devices: 29 us -> 38.4 us  [in_line(): return lambda value: lax.ppermute(value, ('row', 'col'), pairs)]
    ppermute x13, starting transfers between devices: 8.51 us -> 5.83 us  [swap(): return lax.ppermute(value, 'row', [(r, r ^ 1) for r in range(rows)])]
    ppermute x18, waiting for transfers between devices: 33.5 us -> 30.9 us  [in_plane(): lax.ppermute(value, 'row', [(r, r ^ 2 * distance(r, mask)) for r in range...]
  transfers between devices with their start and end apart: 46 -> 46, of which waited for: 20 -> 22; matrix products, arithmetic and copies ran while one was open for 2% -> 2% of each run, Pallas kernels for 14% -> 13%
where the time goes in v3:
time: 192 us; the launch traced here: 190 us
  waiting for transfers between devices  85.5 us (45%)
  starting transfers between devices  70.9 us (37%)
  Pallas kernels  25.5 us (13%)
  local copies, waits for them, and re-layouts  6.38 us (3%)
    ppermute x15, waiting for transfers between devices, in_line(): return lambda value: lax.ppermute(value, ('row', 'col'), pairs)  51.9 us
    ppermute x15, starting transfers between devices, in_line(): return lambda value: lax.ppermute(value, ('row', 'col'), pairs)  38.4 us
    ppermute x18, waiting for transfers between devices, in_plane(): lax.ppermute(value, 'row', [(r, r ^ 2 * distance(r, mask)) for r in range...  30.9 us
    ppermute x18, starting transfers between devices, in_plane(): lax.ppermute(value, 'row', [(r, r ^ 2 * distance(r, mask)) for r in range...  26.7 us
    pallas_call x2, Pallas kernels, grid(): pl.pallas_call(functools.partial(grid_kernel, bits), out_shape=[jax.Shape...  12.9 us
    pallas_call x2, Pallas kernels, back(): pl.pallas_call(functools.partial(back_kernel, bits), out_shape=[jax.Shape...  6.79 us
    ppermute x13, starting transfers between devices, swap(): return lax.ppermute(value, 'row', [(r, r ^ 1) for r in range(rows)])  5.83 us
    pallas_call x2, Pallas kernels, project(): pl.pallas_call(functools.partial(project_kernel, bits), out_shape=[jax.Sh...  4.8 us
  transfers between devices with their start and end apart: 46, of which 22 were waited for; matrix products, arithmetic and copies ran while one was open for 2% of the time, Pallas kernels for 13%

profile of v3, /device:TPU:0, one launch (start us, length us, event | category | flops | bytes accessed | tf_op | source)
XLA Modules:
  0.0 190.3 jit_solution(8213420939259785483)
XLA Ops:
  0.0 3.0 %collective-permute-start = (bf16[256,1024]{1,0:T(8,128)(2,1)}, bf16[256,1024]{1,0:T(8,128)(2,1)S(1)}, u32[]{:S(2)}, u32[]{:S(2)}) collective-permute-start(bf16[256,1024]{1,0:T(8,128)(2,1)} %refs_2_.3), channel_id=1, source_target_pairs={{0,1},{1,0},{2,3},{3,2},{4,6},{5,7},{6,4},{7,5},{8,9},{9,8},{10,11... | collective-permute-start | bytes 1572872 | tf_op jit(solution)/shard_map/ppermute | solution.py:255
  3.0 2.6 %collective-permute-start.1 = (bf16[256,1024]{1,0:T(8,128)(2,1)}, bf16[256,1024]{1,0:T(8,128)(2,1)S(1)}, u32[]{:S(2)}, u32[]{:S(2)}) collective-permute-start(bf16[256,1024]{1,0:T(8,128)(2,1)} %refs_2_.3), channel_id=1, source_target_pairs={{0,2},{1,3},{2,0},{3,1},{4,5},{5,4},{6,7},{7,6},{8,10},{9,11},{10,... | collective-permute-start | bytes 1572872 | tf_op jit(solution)/shard_map/ppermute | solution.py:255
  7.1 1.5 collective-permute-start.7
  8.6 18.1 %collective-permute-done.refs_1_ = bf16[256,1024]{1,0:T(8,128)(2,1)S(1)} collective-permute-done((bf16[256,1024]{1,0:T(8,128)(2,1)}, bf16[256,1024]{1,0:T(8,128)(2,1)S(1)}, u32[]{:S(2)}, u32[]{:S(2)}) %collective-permute-start) | collective-permute-done | bytes 524320 | tf_op jit(solution)/shard_map/ppermute | solution.py:255
  26.8 3.3 %collective-permute-start.2 = (bf16[256,1024]{1,0:T(8,128)(2,1)S(1)}, bf16[256,1024]{1,0:T(8,128)(2,1)S(1)}, u32[]{:S(2)}, u32[]{:S(2)}) collective-permute-start(bf16[256,1024]{1,0:T(8,128)(2,1)S(1)} %collective-permute-done.refs_1_), channel_id=1, source_target_pairs={{0,2},{1,3},{2,0},{3,1},{4,5},{5,4},{6,7},{7,6},{8,10},{9,11},{10,... | collective-permute-start | bytes 1572872 | tf_op jit(solution)/shard_map/ppermute | solution.py:255
  30.0 1.5 collective-permute-start.8
  32.1 1.8 slice_bitcast_fusion.1
  33.9 9.0 %collective-permute-done.2.refs_3_ = bf16[256,1024]{1,0:T(8,128)(2,1)S(1)} collective-permute-done((bf16[256,1024]{1,0:T(8,128)(2,1)S(1)}, bf16[256,1024]{1,0:T(8,128)(2,1)S(1)}, u32[]{:S(2)}, u32[]{:S(2)}) %collective-permute-start.2) | collective-permute-done | bytes 524320 | tf_op jit(solution)/shard_map/ppermute | solution.py:255
  43.7 3.4 %collective-permute-start.4 = (bf16[256,512]{1,0:T(8,128)(2,1)}, bf16[256,512]{1,0:T(8,128)(2,1)}, u32[]{:S(2)}, u32[]{:S(2)}) collective-permute-start(bf16[256,512]{1,0:T(8,128)(2,1)} %get-tuple-element.42.refs_0_), channel_id=1, source_target_pairs={{0,2},{1,3},{2,0},{3,1},{4,5},{5,4},{6,7},{7,6},{8,10},{9,11},{10,... | collective-permute-start | bytes 786440 | tf_op jit(solution)/shard_map/ppermute | solution.py:255
  52.4 4.6 %collective-permute-done.3.refs_1_ = bf16[256,512]{1,0:T(8,128)(2,1)} collective-permute-done((bf16[256,512]{1,0:T(8,128)(2,1)}, bf16[256,512]{1,0:T(8,128)(2,1)}, u32[]{:S(2)}, u32[]{:S(2)}) %collective-permute-start.3) | collective-permute-done | bytes 262176 | tf_op jit(solution)/shard_map/ppermute | solution.py:255
  57.1 1.6 collective-permute-start.5
  58.7 1.5 collective-permute-start.15
  61.6 1.7 constant_dynamic-slice_fusion
  63.4 2.7 %collective-permute-start.32 = (bf16[256,512]{1,0:T(8,128)(2,1)S(1)}, bf16[256,512]{1,0:T(8,128)(2,1)S(1)}, u32[]{:S(2)}, u32[]{:S(2)}) collective-permute-start(bf16[256,512]{1,0:T(8,128)(2,1)S(1)} %get-tuple-element.58.refs_0_), channel_id=1, source_target_pairs={{0,1},{1,0},{2,3},{3,2},{4,6},{5,7},{6,4},{7,5},{8,9},{9,8},{10,11... | collective-permute-start | bytes 786440 | tf_op jit(solution)/shard_map/ppermute | solution.py:255
  67.1 2.8 %project.2 = (bf16[256,512]{1,0:T(8,128)(2,1)S(1)}, bf16[256,512]{1,0:T(8,128)(2,1)S(1)}) custom-call(bf16[256,512]{1,0:T(8,128)(2,1)} %get-tuple-element.42.refs_0_, bf16[256,512]{1,0:T(8,128)(2,1)} %collective-permute-done.3.refs_1_, bf16[256,512]{1,0:T(8,128)(2,1)} %collective-permute-done.4.refs_2_, bf16[256,512]{1,0:T(8,128)(2,1)} %collective-permute-done.5.refs_3_, ...), custom_call_target="tpu_custom_call" | custom-call | flops 1 | bytes 1 | tf_op jit(solution)/shard_map/project/pallas_call | solution.py:81
  70.5 2.3 %collective-permute-done.32.refs_1_ = bf16[256,512]{1,0:T(8,128)(2,1)S(1)} collective-permute-done((bf16[256,512]{1,0:T(8,128)(2,1)S(1)}, bf16[256,512]{1,0:T(8,128)(2,1)S(1)}, u32[]{:S(2)}, u32[]{:S(2)}) %collective-permute-start.32) | collective-permute-done | bytes 262176 | tf_op jit(solution)/shard_map/ppermute | solution.py:255
  73.9 1.9 %collective-permute-start.34 = (bf16[256,512]{1,0:T(8,128)(2,1)S(1)}, bf16[256,512]{1,0:T(8,128)(2,1)S(1)}, u32[]{:S(2)}, u32[]{:S(2)}) collective-permute-start(bf16[256,512]{1,0:T(8,128)(2,1)S(1)} %collective-permute-done.32.refs_1_), channel_id=1, source_target_pairs={{0,2},{1,3},{2,0},{3,1},{4,5},{5,4},{6,7},{7,6},{8,10},{9,11},{10,... | collective-permute-start | bytes 786440 | tf_op jit(solution)/shard_map/ppermute | solution.py:255
  75.8 3.5 %collective-permute-done.15.refs_6_ = bf16[256,1024]{1,0:T(8,128)(2,1)S(1)} collective-permute-done((bf16[256,1024]{1,0:T(8,128)(2,1)}, bf16[256,1024]{1,0:T(8,128)(2,1)S(1)}, u32[]{:S(2)}, u32[]{:S(2)}) %collective-permute-start.15) | collective-permute-done | bytes 524320 | tf_op jit(solution)/shard_map/ppermute | solution.py:251
  79.3 1.5 collective-permute-start.17
  80.8 1.5 collective-permute-start.18
  82.3 1.9 %collective-permute-start.20 = (bf16[256,1024]{1,0:T(8,128)(2,1)S(1)}, bf16[256,1024]{1,0:T(8,128)(2,1)S(1)}, u32[]{:S(2)}, u32[]{:S(2)}) collective-permute-start(bf16[256,1024]{1,0:T(8,128)(2,1)S(1)} %copy-done.3), channel_id=1, source_target_pairs={{0,4},{4,0},{8,12},{12,8},{16,20},{20,16},{24,28},{28,24},{1,5},{5... | collective-permute-start | bytes 1572872 | tf_op jit(solution)/shard_map/ppermute | solution.py:248
  84.2 1.7 collective-permute-done.34.refs_3_
  85.9 2.0 %project.3 = (bf16[256,512]{1,0:T(8,128)(2,1)S(1)}, bf16[256,512]{1,0:T(8,128)(2,1)S(1)}) custom-call(bf16[256,512]{1,0:T(8,128)(2,1)S(1)} %get-tuple-element.58.refs_0_, bf16[256,512]{1,0:T(8,128)(2,1)S(1)} %collective-permute-done.32.refs_1_, bf16[256,512]{1,0:T(8,128)(2,1)S(1)} %collective-permute-done.33.refs_2_, ...), custom_call_target="tpu_custom_call" | custom-call | flops 1 | bytes 1 | tf_op jit(solution)/shard_map/project/pallas_call | solution.py:81
  87.9 2.1 %collective-permute-start.35 = (bf16[256,512]{1,0:T(8,128)(2,1)S(1)}, bf16[256,512]{1,0:T(8,128)(2,1)S(1)}, u32[]{:S(2)}, u32[]{:S(2)}) collective-permute-start(bf16[256,512]{1,0:T(8,128)(2,1)S(1)} %get-tuple-element.60), channel_id=1, source_target_pairs={{0,4},{4,0},{8,12},{12,8},{16,20},{20,16},{24,28},{28,24},{1,5},{5... | collective-permute-start | bytes 786440 | tf_op jit(solution)/shard_map/ppermute | solution.py:248
  92.6 1.5 collective-permute-start.36
  96.4 10.0 %collective-permute-done.36.refs_1_ = bf16[512,512]{1,0:T(8,128)(2,1)S(1)} collective-permute-done((bf16[512,512]{1,0:T(8,128)(2,1)S(1)}, bf16[512,512]{1,0:T(8,128)(2,1)S(1)}, u32[]{:S(2)}, u32[]{:S(2)}) %collective-permute-start.36) | collective-permute-done | bytes 524320 | tf_op jit(solution)/shard_map/ppermute | solution.py:251
  106.4 1.5 collective-permute-start.38
  107.9 6.4 %grid.2 = (bf16[512,512]{1,0:T(8,128)(2,1)S(1)}, bf16[512,512]{1,0:T(8,128)(2,1)S(1)}, bf16[512,512]{1,0:T(8,128)(2,1)S(1)}, bf16[512,512]{1,0:T(8,128)(2,1)S(1)}) custom-call(bf16[512,512]{1,0:T(8,128)(2,1)S(1)} %constant_dynamic-update-slice_fusion.refs_0_, bf16[512,512]{1,0:T(8,128)(2,1)S(1)} %collective-permute-done.17.refs_1_, ...), custom_call_target="tpu_custom_call" | custom-call | flops 1 | bytes 1 | tf_op jit(solution)/shard_map/grid/pallas_call | solution.py:139
  116.4 1.8 collective-permute-done.38.refs_3_
  118.2 6.5 %grid.3 = (bf16[512,512]{1,0:T(8,128)(2,1)S(1)}, bf16[512,512]{1,0:T(8,128)(2,1)S(1)}, bf16[512,512]{1,0:T(8,128)(2,1)S(1)}, bf16[512,512]{1,0:T(8,128)(2,1)S(1)}) custom-call(bf16[512,512]{1,0:T(8,128)(2,1)S(1)} %constant_dynamic-update-slice_fusion.2.refs_0_, bf16[512,512]{1,0:T(8,128)(2,1)S(1)} %collective-permute-done.36.refs_1_, ...), custom_call_target="tpu_custom_call" | custom-call | flops 1 | bytes 1 | tf_op jit(solution)/shard_map/grid/pallas_call | solution.py:139
  124.7 1.6 collective-permute-start.40
  126.3 3.1 %collective-permute-done.26 = bf16[512,512]{1,0:T(8,128)(2,1)S(1)} collective-permute-done((bf16[512,512]{1,0:T(8,128)(2,1)S(1)}, bf16[512,512]{1,0:T(8,128)(2,1)S(1)}, u32[]{:S(2)}, u32[]{:S(2)}) %collective-permute-start.26) | collective-permute-done | bytes 524320 | tf_op jit(solution)/shard_map/ppermute | solution.py:251
  129.6 2.2 %collective-permute-start.27 = (bf16[512,512]{1,0:T(8,128)(2,1)S(1)}, bf16[512,512]{1,0:T(8,128)(2,1)S(1)}, u32[]{:S(2)}, u32[]{:S(2)}) collective-permute-start(bf16[512,512]{1,0:T(8,128)(2,1)S(1)} %add_convert_fusion.1), channel_id=1, source_target_pairs={{0,8},{4,20},{8,0},{12,28},{16,24},{20,4},{24,16},{28,12},{1,9},{5... | collective-permute-start | bytes 1572872 | tf_op jit(solution)/shard_map/ppermute | solution.py:251
  132.6 4.6 %collective-permute-done.40 = bf16[512,512]{1,0:T(8,128)(2,1)S(1)} collective-permute-done((bf16[512,512]{1,0:T(8,128)(2,1)S(1)}, bf16[512,512]{1,0:T(8,128)(2,1)S(1)}, u32[]{:S(2)}, u32[]{:S(2)}) %collective-permute-start.40) | collective-permute-done | bytes 524320 | tf_op jit(solution)/shard_map/ppermute | solution.py:251
  137.3 2.9 %collective-permute-start.41 = (bf16[512,512]{1,0:T(8,128)(2,1)S(1)}, bf16[512,512]{1,0:T(8,128)(2,1)S(1)}, u32[]{:S(2)}, u32[]{:S(2)}) collective-permute-start(bf16[512,512]{1,0:T(8,128)(2,1)S(1)} %add_convert_fusion), channel_id=1, source_target_pairs={{0,8},{4,20},{8,0},{12,28},{16,24},{20,4},{24,16},{28,12},{1,9},{5... | collective-permute-start | bytes 1572872 | tf_op jit(solution)/shard_map/ppermute | solution.py:251
  140.2 4.4 %collective-permute-done.27 = bf16[512,512]{1,0:T(8,128)(2,1)S(1)} collective-permute-done((bf16[512,512]{1,0:T(8,128)(2,1)S(1)}, bf16[512,512]{1,0:T(8,128)(2,1)S(1)}, u32[]{:S(2)}, u32[]{:S(2)}) %collective-permute-start.27) | collective-permute-done | bytes 524320 | tf_op jit(solution)/shard_map/ppermute | solution.py:251
  144.9 1.5 collective-permute-done.28.refs_1_
  146.4 3.4 %back.2 = (bf16[256,512]{1,0:T(8,128)(2,1)S(1)}, bf16[256,512]{1,0:T(8,128)(2,1)S(1)}, bf16[256,512]{1,0:T(8,128)(2,1)S(1)}, bf16[256,512]{1,0:T(8,128)(2,1)S(1)}) custom-call(bf16[256,512]{1,0:T(8,128)(2,1)S(1)} %get-tuple-element.82.refs_0_, bf16[256,512]{1,0:T(8,128)(2,1)S(1)} %collective-permute-done.28.refs_1_, bf16[256,1024]{1,0:T(8,128)(2,1)S(1)} %copy-done.1, ...), custom_call_target="tpu_custom_call" | custom-call | flops 1 | bytes 1 | tf_op jit(solution)/shard_map/back/pallas_call | solution.py:188
  149.8 2.5 %collective-permute-done.41 = bf16[512,512]{1,0:T(8,128)(2,1)S(1)} collective-permute-done((bf16[512,512]{1,0:T(8,128)(2,1)S(1)}, bf16[512,512]{1,0:T(8,128)(2,1)S(1)}, u32[]{:S(2)}, u32[]{:S(2)}) %collective-permute-start.41) | collective-permute-done | bytes 524320 | tf_op jit(solution)/shard_map/ppermute | solution.py:251
  152.6 2.1 %collective-permute-start.29 = (bf16[256,512]{1,0:T(8,128)(2,1)S(1)}, bf16[256,512]{1,0:T(8,128)(2,1)S(1)}, u32[]{:S(2)}, u32[]{:S(2)}) collective-permute-start(bf16[256,512]{1,0:T(8,128)(2,1)S(1)} %get-tuple-element.55), channel_id=1, source_target_pairs={{0,2},{1,3},{2,0},{3,1},{4,5},{5,4},{6,7},{7,6},{8,10},{9,11},{10,... | collective-permute-start | bytes 786440 | tf_op jit(solution)/shard_map/ppermute | solution.py:255
  155.6 3.4 %back.3 = (bf16[256,512]{1,0:T(8,128)(2,1)S(1)}, bf16[256,512]{1,0:T(8,128)(2,1)S(1)}, bf16[256,512]{1,0:T(8,128)(2,1)S(1)}, bf16[256,512]{1,0:T(8,128)(2,1)S(1)}) custom-call(bf16[256,512]{1,0:T(8,128)(2,1)S(1)} %get-tuple-element.80.refs_0_, bf16[256,512]{1,0:T(8,128)(2,1)S(1)} %collective-permute-done.42.refs_1_, bf16[256,1024]{1,0:T(8,128)(2,1)S(1)} %copy-done.1, ...), custom_call_target="tpu_custom_call" | custom-call | flops 1 | bytes 1 | tf_op jit(solution)/shard_map/back/pallas_call | solution.py:188
  159.0 2.1 %collective-permute-done.29 = bf16[256,512]{1,0:T(8,128)(2,1)S(1)} collective-permute-done((bf16[256,512]{1,0:T(8,128)(2,1)S(1)}, bf16[256,512]{1,0:T(8,128)(2,1)S(1)}, u32[]{:S(2)}, u32[]{:S(2)}) %collective-permute-start.29) | collective-permute-done | bytes 262176 | tf_op jit(solution)/shard_map/ppermute | solution.py:255
  161.2 3.4 %collective-permute-start.44 = (bf16[256,512]{1,0:T(8,128)(2,1)S(1)}, bf16[256,512]{1,0:T(8,128)(2,1)S(1)}, u32[]{:S(2)}, u32[]{:S(2)}) collective-permute-start(bf16[256,512]{1,0:T(8,128)(2,1)S(1)} %get-tuple-element.76), channel_id=1, source_target_pairs={{0,2},{1,3},{2,0},{3,1},{4,5},{5,4},{6,7},{7,6},{8,10},{9,11},{10,... | collective-permute-start | bytes 786440 | tf_op jit(solution)/shard_map/ppermute | solution.py:255
  164.5 2.2 %collective-permute-done.30 = bf16[256,512]{1,0:T(8,128)(2,1)S(1)} collective-permute-done((bf16[256,512]{1,0:T(8,128)(2,1)S(1)}, bf16[256,512]{1,0:T(8,128)(2,1)S(1)}, u32[]{:S(2)}, u32[]{:S(2)}) %collective-permute-start.30) | collective-permute-done | bytes 262176 | tf_op jit(solution)/shard_map/ppermute | solution.py:255
  166.8 4.5 %collective-permute-start.31 = (bf16[256,512]{1,0:T(8,128)(2,1)S(1)}, bf16[256,512]{1,0:T(8,128)(2,1)S(1)}, u32[]{:S(2)}, u32[]{:S(2)}) collective-permute-start(bf16[256,512]{1,0:T(8,128)(2,1)S(1)} %add_convert_fusion.7), channel_id=1, source_target_pairs={{0,1},{1,0},{2,3},{3,2},{4,6},{5,7},{6,4},{7,5},{8,9},{9,8},{10,11... | collective-permute-start | bytes 786440 | tf_op jit(solution)/shard_map/ppermute | solution.py:255
  172.9 5.7 %collective-permute-start.45 = (bf16[256,512]{1,0:T(8,128)(2,1)S(1)}, bf16[256,512]{1,0:T(8,128)(2,1)S(1)}, u32[]{:S(2)}, u32[]{:S(2)}) collective-permute-start(bf16[256,512]{1,0:T(8,128)(2,1)S(1)} %add_convert_fusion.3), channel_id=1, source_target_pairs={{0,1},{1,0},{2,3},{3,2},{4,6},{5,7},{6,4},{7,5},{8,9},{9,8},{10,11... | collective-permute-start | bytes 786440 | tf_op jit(solution)/shard_map/ppermute | solution.py:255
  178.5 5.6 %collective-permute-done.31 = bf16[256,512]{1,0:T(8,128)(2,1)S(1)} collective-permute-done((bf16[256,512]{1,0:T(8,128)(2,1)S(1)}, bf16[256,512]{1,0:T(8,128)(2,1)S(1)}, u32[]{:S(2)}, u32[]{:S(2)}) %collective-permute-start.31) | collective-permute-done | bytes 262176 | tf_op jit(solution)/shard_map/ppermute | solution.py:255
  184.4 5.0 %collective-permute-done.45 = bf16[256,512]{1,0:T(8,128)(2,1)S(1)} collective-permute-done((bf16[256,512]{1,0:T(8,128)(2,1)S(1)}, bf16[256,512]{1,0:T(8,128)(2,1)S(1)}, u32[]{:S(2)}, u32[]{:S(2)}) %collective-permute-start.45) | collective-permute-done | bytes 262176 | tf_op jit(solution)/shard_map/ppermute | solution.py:255
  (78 shorter events, 24.7 us)
Async XLA Ops:
  0.0 26.7 %collective-permute-start = (bf16[256,1024]{1,0:T(8,128)(2,1)}, bf16[256,1024]{1,0:T(8,128)(2,1)S(1)}, u32[]{:S(2)}, u32[]{:S(2)}) collective-permute-start(bf16[256,1024]{1,0:T(8,128)(2,1)} %refs_2_.3), channel_id=1, source_target_pairs={{0,1},{1,0},{2,3},{3,2},{4,6},{5,7},{6,4},{7,5},{8,9},{9,8},{10,11... | collective-permute-start | bytes 1572872 | tf_op jit(solution)/shard_map/ppermute | solution.py:255
  3.0 23.7 %collective-permute-start.1 = (bf16[256,1024]{1,0:T(8,128)(2,1)}, bf16[256,1024]{1,0:T(8,128)(2,1)S(1)}, u32[]{:S(2)}, u32[]{:S(2)}) collective-permute-start(bf16[256,1024]{1,0:T(8,128)(2,1)} %refs_2_.3), channel_id=1, source_target_pairs={{0,2},{1,3},{2,0},{3,1},{4,5},{5,4},{6,7},{7,6},{8,10},{9,11},{10,... | collective-permute-start | bytes 1572872 | tf_op jit(solution)/shard_map/ppermute | solution.py:255
  5.6 24.4 %collective-permute-start.6 = (bf16[256,1024]{1,0:T(8,128)(2,1)}, bf16[256,1024]{1,0:T(8,128)(2,1)S(1)}, u32[]{:S(2)}, u32[]{:S(2)}) collective-permute-start(bf16[256,1024]{1,0:T(8,128)(2,1)} %refs_2_.3), channel_id=1, source_target_pairs={{0,8},{4,20},{8,0},{12,28},{16,24},{20,4},{24,16},{28,12},{1,9},{5... | collective-permute-start | bytes 1572872 | tf_op jit(solution)/shard_map/ppermute | solution.py:251
  7.1 25.0 %collective-permute-start.7 = (bf16[256,1024]{1,0:T(8,128)(2,1)}, bf16[256,1024]{1,0:T(8,128)(2,1)S(1)}, u32[]{:S(2)}, u32[]{:S(2)}) collective-permute-start(bf16[256,1024]{1,0:T(8,128)(2,1)} %refs_2_.3), channel_id=1, source_target_pairs={{0,16},{4,12},{8,24},{12,4},{16,0},{20,28},{24,8},{28,20},{1,17},{... | collective-permute-start | bytes 1572872 | tf_op jit(solution)/shard_map/ppermute | solution.py:251
  26.8 16.1 %collective-permute-start.2 = (bf16[256,1024]{1,0:T(8,128)(2,1)S(1)}, bf16[256,1024]{1,0:T(8,128)(2,1)S(1)}, u32[]{:S(2)}, u32[]{:S(2)}) collective-permute-start(bf16[256,1024]{1,0:T(8,128)(2,1)S(1)} %collective-permute-done.refs_1_), channel_id=1, source_target_pairs={{0,2},{1,3},{2,0},{3,1},{4,5},{5,4},{6,7},{7,6},{8,10},{9,11},{10,... | collective-permute-start | bytes 1572872 | tf_op jit(solution)/shard_map/ppermute | solution.py:255
  30.0 12.8 %collective-permute-start.8 = (bf16[256,1024]{1,0:T(8,128)(2,1)S(1)}, bf16[256,1024]{1,0:T(8,128)(2,1)S(1)}, u32[]{:S(2)}, u32[]{:S(2)}) collective-permute-start(bf16[256,1024]{1,0:T(8,128)(2,1)S(1)} %collective-permute-done.6.refs_5_.refs_3_), channel_id=1, source_target_pairs={{0,16},{4,12},{8,24},{12,4},{16,0},{20,28},{24,8},{28,20},{1,17},{... | collective-permute-start | bytes 1572872 | tf_op jit(solution)/shard_map/ppermute | solution.py:251
  31.6 12.1 %collective-permute-start.9 = (bf16[256,1024]{1,0:T(8,128)(2,1)}, bf16[256,1024]{1,0:T(8,128)(2,1)S(1)}, u32[]{:S(2)}, u32[]{:S(2)}) collective-permute-start(bf16[256,1024]{1,0:T(8,128)(2,1)} %refs_2_.3), channel_id=1, source_target_pairs={{0,4},{4,0},{8,12},{12,8},{16,20},{20,16},{24,28},{28,24},{1,5},{5... | collective-permute-start | bytes 1572872 | tf_op jit(solution)/shard_map/ppermute | solution.py:248
  31.6 18.4 %collective-permute-start.10 = (bf16[256,1024]{1,0:T(8,128)(2,1)S(1)}, bf16[256,1024]{1,0:T(8,128)(2,1)S(1)}, u32[]{:S(2)}, u32[]{:S(2)}) collective-permute-start(bf16[256,1024]{1,0:T(8,128)(2,1)S(1)} %collective-permute-done.6.refs_5_.refs_3_), channel_id=1, source_target_pairs={{0,4},{4,0},{8,12},{12,8},{16,20},{20,16},{24,28},{28,24},{1,5},{5... | collective-permute-start | bytes 1572872 | tf_op jit(solution)/shard_map/ppermute | solution.py:248
  32.1 26.6 %collective-permute-start.11 = (bf16[256,1024]{1,0:T(8,128)(2,1)S(1)}, bf16[256,1024]{1,0:T(8,128)(2,1)S(1)}, u32[]{:S(2)}, u32[]{:S(2)}) collective-permute-start(bf16[256,1024]{1,0:T(8,128)(2,1)S(1)} %collective-permute-done.7.refs_6_.refs_4_), channel_id=1, source_target_pairs={{0,4},{4,0},{8,12},{12,8},{16,20},{20,16},{24,28},{28,24},{1,5},{5... | collective-permute-start | bytes 1572872 | tf_op jit(solution)/shard_map/ppermute | solution.py:248
  42.9 20.5 %collective-permute-start.12 = (bf16[256,1024]{1,0:T(8,128)(2,1)S(1)}, bf16[256,1024]{1,0:T(8,128)(2,1)}, u32[]{:S(2)}, u32[]{:S(2)}) collective-permute-start(bf16[256,1024]{1,0:T(8,128)(2,1)S(1)} %collective-permute-done.8.refs_7_.refs_5_), channel_id=1, source_target_pairs={{0,4},{4,0},{8,12},{12,8},{16,20},{20,16},{24,28},{28,24},{1,5},{5... | collective-permute-start | bytes 1572872 | tf_op jit(solution)/shard_map/ppermute | solution.py:248
  42.9 14.2 %collective-permute-start.3 = (bf16[256,512]{1,0:T(8,128)(2,1)}, bf16[256,512]{1,0:T(8,128)(2,1)}, u32[]{:S(2)}, u32[]{:S(2)}) collective-permute-start(bf16[256,512]{1,0:T(8,128)(2,1)} %get-tuple-element.42.refs_0_), channel_id=1, source_target_pairs={{0,1},{1,0},{2,3},{3,2},{4,6},{5,7},{6,4},{7,5},{8,9},{9,8},{10,11... | collective-permute-start | bytes 786440 | tf_op jit(solution)/shard_map/ppermute | solution.py:255
  43.7 16.5 %collective-permute-start.4 = (bf16[256,512]{1,0:T(8,128)(2,1)}, bf16[256,512]{1,0:T(8,128)(2,1)}, u32[]{:S(2)}, u32[]{:S(2)}) collective-permute-start(bf16[256,512]{1,0:T(8,128)(2,1)} %get-tuple-element.42.refs_0_), channel_id=1, source_target_pairs={{0,2},{1,3},{2,0},{3,1},{4,5},{5,4},{6,7},{7,6},{8,10},{9,11},{10,... | collective-permute-start | bytes 786440 | tf_op jit(solution)/shard_map/ppermute | solution.py:255
  51.0 19.0 %collective-permute-start.14 = (bf16[256,1024]{1,0:T(8,128)(2,1)}, bf16[256,1024]{1,0:T(8,128)(2,1)}, u32[]{:S(2)}, u32[]{:S(2)}) collective-permute-start(bf16[256,1024]{1,0:T(8,128)(2,1)} %get-tuple-element.45), channel_id=1, source_target_pairs={{0,8},{4,20},{8,0},{12,28},{16,24},{20,4},{24,16},{28,12},{1,9},{5... | collective-permute-start | bytes 1572872 | tf_op jit(solution)/shard_map/ppermute | solution.py:251
  57.1 10.0 %collective-permute-start.5 = (bf16[256,512]{1,0:T(8,128)(2,1)}, bf16[256,512]{1,0:T(8,128)(2,1)}, u32[]{:S(2)}, u32[]{:S(2)}) collective-permute-start(bf16[256,512]{1,0:T(8,128)(2,1)} %collective-permute-done.3.refs_1_), channel_id=1, source_target_pairs={{0,2},{1,3},{2,0},{3,1},{4,5},{5,4},{6,7},{7,6},{8,10},{9,11},{10,... | collective-permute-start | bytes 786440 | tf_op jit(solution)/shard_map/ppermute | solution.py:255
  58.7 20.6 %collective-permute-start.15 = (bf16[256,1024]{1,0:T(8,128)(2,1)}, bf16[256,1024]{1,0:T(8,128)(2,1)S(1)}, u32[]{:S(2)}, u32[]{:S(2)}) collective-permute-start(bf16[256,1024]{1,0:T(8,128)(2,1)} %copy-done.5), channel_id=1, source_target_pairs={{0,16},{4,12},{8,24},{12,4},{16,0},{20,28},{24,8},{28,20},{1,17},{... | collective-permute-start | bytes 1572872 | tf_op jit(solution)/shard_map/ppermute | solution.py:251
  60.2 6.9 %copy-start.1 = (bf16[256,1024]{1,0:T(8,128)(2,1)S(1)}, bf16[256,1024]{1,0:T(8,128)(2,1)}, u32[]{:S(2)}) copy-start(bf16[256,1024]{1,0:T(8,128)(2,1)} %refs_2_.3) | copy-start | bytes 1572868
  60.2 19.1 %collective-permute-start.16 = (bf16[256,1024]{1,0:T(8,128)(2,1)}, bf16[256,1024]{1,0:T(8,128)(2,1)S(1)}, u32[]{:S(2)}, u32[]{:S(2)}) collective-permute-start(bf16[256,1024]{1,0:T(8,128)(2,1)} %copy-done.4), channel_id=1, source_target_pairs={{0,24},{4,28},{8,16},{12,20},{16,8},{20,12},{24,0},{28,4},{1,25},{... | collective-permute-start | bytes 1572872 | tf_op jit(solution)/shard_map/ppermute | solution.py:251
  63.4 9.4 %collective-permute-start.32 = (bf16[256,512]{1,0:T(8,128)(2,1)S(1)}, bf16[256,512]{1,0:T(8,128)(2,1)S(1)}, u32[]{:S(2)}, u32[]{:S(2)}) collective-permute-start(bf16[256,512]{1,0:T(8,128)(2,1)S(1)} %get-tuple-element.58.refs_0_), channel_id=1, source_target_pairs={{0,1},{1,0},{2,3},{3,2},{4,6},{5,7},{6,4},{7,5},{8,9},{9,8},{10,11... | collective-permute-start | bytes 786440 | tf_op jit(solution)/shard_map/ppermute | solution.py:255
  67.1 15.2 %copy-start.3 = (bf16[256,1024]{1,0:T(8,128)(2,1)S(1)}, bf16[256,1024]{1,0:T(8,128)(2,1)}, u32[]{:S(2)}) copy-start(bf16[256,1024]{1,0:T(8,128)(2,1)} %copy-done.2) | copy-start | bytes 1572868
  67.1 27.0 %collective-permute-start.24 = (f32[512,512]{1,0:T(8,128)S(1)}, f32[512,512]{1,0:T(8,128)S(1)}, u32[]{:S(2)}, u32[]{:S(2)}) collective-permute-start(f32[512,512]{1,0:T(8,128)S(1)} %get-tuple-element.77), channel_id=1, source_target_pairs={{0,4},{4,0},{8,12},{12,8},{16,20},{20,16},{24,28},{28,24},{1,5},{5... | collective-permute-start | bytes 3145736 | tf_op jit(solution)/shard_map/ppermute | solution.py:248
  70.0 3.9 %collective-permute-start.13 = (bf16[256,512]{1,0:T(8,128)(2,1)S(1)}, bf16[256,512]{1,0:T(8,128)(2,1)S(1)}, u32[]{:S(2)}, u32[]{:S(2)}) collective-permute-start(bf16[256,512]{1,0:T(8,128)(2,1)S(1)} %get-tuple-element.44), channel_id=1, source_target_pairs={{0,4},{4,0},{8,12},{12,8},{16,20},{20,16},{24,28},{28,24},{1,5},{5... | collective-permute-start | bytes 786440 | tf_op jit(solution)/shard_map/ppermute | solution.py:248
  72.8 9.5 %collective-permute-start.33 = (bf16[256,512]{1,0:T(8,128)(2,1)S(1)}, bf16[256,512]{1,0:T(8,128)(2,1)S(1)}, u32[]{:S(2)}, u32[]{:S(2)}) collective-permute-start(bf16[256,512]{1,0:T(8,128)(2,1)S(1)} %get-tuple-element.58.refs_0_), channel_id=1, source_target_pairs={{0,2},{1,3},{2,0},{3,1},{4,5},{5,4},{6,7},{7,6},{8,10},{9,11},{10,... | collective-permute-start | bytes 786440 | tf_op jit(solution)/shard_map/ppermute | solution.py:255
  73.9 12.0 %collective-permute-start.34 = (bf16[256,512]{1,0:T(8,128)(2,1)S(1)}, bf16[256,512]{1,0:T(8,128)(2,1)S(1)}, u32[]{:S(2)}, u32[]{:S(2)}) collective-permute-start(bf16[256,512]{1,0:T(8,128)(2,1)S(1)} %collective-permute-done.32.refs_1_), channel_id=1, source_target_pairs={{0,2},{1,3},{2,0},{3,1},{4,5},{5,4},{6,7},{7,6},{8,10},{9,11},{10,... | collective-permute-start | bytes 786440 | tf_op jit(solution)/shard_map/ppermute | solution.py:255
  79.3 13.3 %collective-permute-start.17 = (bf16[512,512]{1,0:T(8,128)(2,1)S(1)}, bf16[512,512]{1,0:T(8,128)(2,1)S(1)}, u32[]{:S(2)}, u32[]{:S(2)}) collective-permute-start(bf16[512,512]{1,0:T(8,128)(2,1)S(1)} %constant_dynamic-update-slice_fusion.refs_0_), channel_id=1, source_target_pairs={{0,8},{4,20},{8,0},{12,28},{16,24},{20,4},{24,16},{28,12},{1,9},{5... | collective-permute-start | bytes 1572872 | tf_op jit(solution)/shard_map/ppermute | solution.py:251
  80.8 11.8 %collective-permute-start.18 = (bf16[512,512]{1,0:T(8,128)(2,1)S(1)}, bf16[512,512]{1,0:T(8,128)(2,1)S(1)}, u32[]{:S(2)}, u32[]{:S(2)}) collective-permute-start(bf16[512,512]{1,0:T(8,128)(2,1)S(1)} %constant_dynamic-update-slice_fusion.refs_0_), channel_id=1, source_target_pairs={{0,16},{4,12},{8,24},{12,4},{16,0},{20,28},{24,8},{28,20},{1,17},{... | collective-permute-start | bytes 1572872 | tf_op jit(solution)/shard_map/ppermute | solution.py:251
  82.3 12.0 %collective-permute-start.20 = (bf16[256,1024]{1,0:T(8,128)(2,1)S(1)}, bf16[256,1024]{1,0:T(8,128)(2,1)S(1)}, u32[]{:S(2)}, u32[]{:S(2)}) collective-permute-start(bf16[256,1024]{1,0:T(8,128)(2,1)S(1)} %copy-done.3), channel_id=1, source_target_pairs={{0,4},{4,0},{8,12},{12,8},{16,20},{20,16},{24,28},{28,24},{1,5},{5... | collective-permute-start | bytes 1572872 | tf_op jit(solution)/shard_map/ppermute | solution.py:248
  87.9 3.3 %collective-permute-start.35 = (bf16[256,512]{1,0:T(8,128)(2,1)S(1)}, bf16[256,512]{1,0:T(8,128)(2,1)S(1)}, u32[]{:S(2)}, u32[]{:S(2)}) collective-permute-start(bf16[256,512]{1,0:T(8,128)(2,1)S(1)} %get-tuple-element.60), channel_id=1, source_target_pairs={{0,4},{4,0},{8,12},{12,8},{16,20},{20,16},{24,28},{28,24},{1,5},{5... | collective-permute-start | bytes 786440 | tf_op jit(solution)/shard_map/ppermute | solution.py:248
  91.1 4.6 %collective-permute-start.21 = (bf16[256,1024]{1,0:T(8,128)(2,1)}, bf16[256,1024]{1,0:T(8,128)(2,1)S(1)}, u32[]{:S(2)}, u32[]{:S(2)}) collective-permute-start(bf16[256,1024]{1,0:T(8,128)(2,1)} %collective-permute-done.14.refs_5_), channel_id=1, source_target_pairs={{0,4},{4,0},{8,12},{12,8},{16,20},{20,16},{24,28},{28,24},{1,5},{5... | collective-permute-start | bytes 1572872 | tf_op jit(solution)/shard_map/ppermute | solution.py:248
  92.6 15.3 %collective-permute-start.22 = (bf16[256,1024]{1,0:T(8,128)(2,1)S(1)}, bf16[256,1024]{1,0:T(8,128)(2,1)S(1)}, u32[]{:S(2)}, u32[]{:S(2)}) collective-permute-start(bf16[256,1024]{1,0:T(8,128)(2,1)S(1)} %collective-permute-done.15.refs_6_), channel_id=1, source_target_pairs={{0,4},{4,0},{8,12},{12,8},{16,20},{20,16},{24,28},{28,24},{1,5},{5... | collective-permute-start | bytes 1572872 | tf_op jit(solution)/shard_map/ppermute | solution.py:248
  92.6 13.8 %collective-permute-start.36 = (bf16[512,512]{1,0:T(8,128)(2,1)S(1)}, bf16[512,512]{1,0:T(8,128)(2,1)S(1)}, u32[]{:S(2)}, u32[]{:S(2)}) collective-permute-start(bf16[512,512]{1,0:T(8,128)(2,1)S(1)} %constant_dynamic-update-slice_fusion.2.refs_0_), channel_id=1, source_target_pairs={{0,8},{4,20},{8,0},{12,28},{16,24},{20,4},{24,16},{28,12},{1,9},{5... | collective-permute-start | bytes 1572872 | tf_op jit(solution)/shard_map/ppermute | solution.py:251
  94.1 13.8 %collective-permute-start.23 = (bf16[256,1024]{1,0:T(8,128)(2,1)S(1)}, bf16[256,1024]{1,0:T(8,128)(2,1)S(1)}, u32[]{:S(2)}, u32[]{:S(2)}) collective-permute-start(bf16[256,1024]{1,0:T(8,128)(2,1)S(1)} %collective-permute-done.16.refs_7_), channel_id=1, source_target_pairs={{0,4},{4,0},{8,12},{12,8},{16,20},{20,16},{24,28},{28,24},{1,5},{5... | collective-permute-start | bytes 1572872 | tf_op jit(solution)/shard_map/ppermute | solution.py:248
  94.4 13.5 %collective-permute-start.19 = (bf16[512,512]{1,0:T(8,128)(2,1)S(1)}, bf16[512,512]{1,0:T(8,128)(2,1)S(1)}, u32[]{:S(2)}, u32[]{:S(2)}) collective-permute-start(bf16[512,512]{1,0:T(8,128)(2,1)S(1)} %collective-permute-done.17.refs_1_), channel_id=1, source_target_pairs={{0,16},{4,12},{8,24},{12,4},{16,0},{20,28},{24,8},{28,20},{1,17},{... | collective-permute-start | bytes 1572872 | tf_op jit(solution)/shard_map/ppermute | solution.py:251
  95.7 20.7 %collective-permute-start.37 = (bf16[512,512]{1,0:T(8,128)(2,1)S(1)}, bf16[512,512]{1,0:T(8,128)(2,1)S(1)}, u32[]{:S(2)}, u32[]{:S(2)}) collective-permute-start(bf16[512,512]{1,0:T(8,128)(2,1)S(1)} %constant_dynamic-update-slice_fusion.2.refs_0_), channel_id=1, source_target_pairs={{0,16},{4,12},{8,24},{12,4},{16,0},{20,28},{24,8},{28,20},{1,17},{... | collective-permute-start | bytes 1572872 | tf_op jit(solution)/shard_map/ppermute | solution.py:251
  106.4 11.8 %collective-permute-start.38 = (bf16[512,512]{1,0:T(8,128)(2,1)S(1)}, bf16[512,512]{1,0:T(8,128)(2,1)S(1)}, u32[]{:S(2)}, u32[]{:S(2)}) collective-permute-start(bf16[512,512]{1,0:T(8,128)(2,1)S(1)} %collective-permute-done.36.refs_1_), channel_id=1, source_target_pairs={{0,16},{4,12},{8,24},{12,4},{16,0},{20,28},{24,8},{28,20},{1,17},{... | collective-permute-start | bytes 1572872 | tf_op jit(solution)/shard_map/ppermute | solution.py:251
  114.3 10.4 %collective-permute-start.25 = (bf16[512,512]{1,0:T(8,128)(2,1)S(1)}, bf16[512,512]{1,0:T(8,128)(2,1)S(1)}, u32[]{:S(2)}, u32[]{:S(2)}) collective-permute-start(bf16[512,512]{1,0:T(8,128)(2,1)S(1)} %get-tuple-element.51), channel_id=1, source_target_pairs={{0,16},{4,12},{8,24},{12,4},{16,0},{20,28},{24,8},{28,20},{1,17},{... | collective-permute-start | bytes 1572872 | tf_op jit(solution)/shard_map/ppermute | solution.py:251
  114.9 14.5 %collective-permute-start.26 = (bf16[512,512]{1,0:T(8,128)(2,1)S(1)}, bf16[512,512]{1,0:T(8,128)(2,1)S(1)}, u32[]{:S(2)}, u32[]{:S(2)}) collective-permute-start(bf16[512,512]{1,0:T(8,128)(2,1)S(1)} %get-tuple-element.53), channel_id=1, source_target_pairs={{0,16},{4,12},{8,24},{12,4},{16,0},{20,28},{24,8},{28,20},{1,17},{... | collective-permute-start | bytes 1572872 | tf_op jit(solution)/shard_map/ppermute | solution.py:251
  124.7 12.5 %collective-permute-start.40 = (bf16[512,512]{1,0:T(8,128)(2,1)S(1)}, bf16[512,512]{1,0:T(8,128)(2,1)S(1)}, u32[]{:S(2)}, u32[]{:S(2)}) collective-permute-start(bf16[512,512]{1,0:T(8,128)(2,1)S(1)} %get-tuple-element.69), channel_id=1, source_target_pairs={{0,16},{4,12},{8,24},{12,4},{16,0},{20,28},{24,8},{28,20},{1,17},{... | collective-permute-start | bytes 1572872 | tf_op jit(solution)/shard_map/ppermute | solution.py:251
  129.6 15.1 %collective-permute-start.27 = (bf16[512,512]{1,0:T(8,128)(2,1)S(1)}, bf16[512,512]{1,0:T(8,128)(2,1)S(1)}, u32[]{:S(2)}, u32[]{:S(2)}) collective-permute-start(bf16[512,512]{1,0:T(8,128)(2,1)S(1)} %add_convert_fusion.1), channel_id=1, source_target_pairs={{0,8},{4,20},{8,0},{12,28},{16,24},{20,4},{24,16},{28,12},{1,9},{5... | collective-permute-start | bytes 1572872 | tf_op jit(solution)/shard_map/ppermute | solution.py:251
  131.8 18.1 %collective-permute-start.39 = (bf16[512,512]{1,0:T(8,128)(2,1)S(1)}, bf16[512,512]{1,0:T(8,128)(2,1)S(1)}, u32[]{:S(2)}, u32[]{:S(2)}) collective-permute-start(bf16[512,512]{1,0:T(8,128)(2,1)S(1)} %get-tuple-element.65), channel_id=1, source_target_pairs={{0,16},{4,12},{8,24},{12,4},{16,0},{20,28},{24,8},{28,20},{1,17},{... | collective-permute-start | bytes 1572872 | tf_op jit(solution)/shard_map/ppermute | solution.py:251
  137.3 15.0 %collective-permute-start.41 = (bf16[512,512]{1,0:T(8,128)(2,1)S(1)}, bf16[512,512]{1,0:T(8,128)(2,1)S(1)}, u32[]{:S(2)}, u32[]{:S(2)}) collective-permute-start(bf16[512,512]{1,0:T(8,128)(2,1)S(1)} %add_convert_fusion), channel_id=1, source_target_pairs={{0,8},{4,20},{8,0},{12,28},{16,24},{20,4},{24,16},{28,12},{1,9},{5... | collective-permute-start | bytes 1572872 | tf_op jit(solution)/shard_map/ppermute | solution.py:251
  144.8 1.6 collective-permute-start.28
  152.6 3.1 %collective-permute-start.42 = (bf16[256,512]{1,0:T(8,128)(2,1)S(1)}, bf16[256,512]{1,0:T(8,128)(2,1)S(1)}, u32[]{:S(2)}, u32[]{:S(2)}) collective-permute-start(bf16[256,512]{1,0:T(8,128)(2,1)S(1)} %get-tuple-element.79), channel_id=1, source_target_pairs={{0,4},{4,0},{8,12},{12,8},{16,20},{20,16},{24,28},{28,24},{1,5},{5... | collective-permute-start | bytes 786440 | tf_op jit(solution)/shard_map/ppermute | solution.py:248
  152.6 8.5 %collective-permute-start.29 = (bf16[256,512]{1,0:T(8,128)(2,1)S(1)}, bf16[256,512]{1,0:T(8,128)(2,1)S(1)}, u32[]{:S(2)}, u32[]{:S(2)}) collective-permute-start(bf16[256,512]{1,0:T(8,128)(2,1)S(1)} %get-tuple-element.55), channel_id=1, source_target_pairs={{0,2},{1,3},{2,0},{3,1},{4,5},{5,4},{6,7},{7,6},{8,10},{9,11},{10,... | collective-permute-start | bytes 786440 | tf_op jit(solution)/shard_map/ppermute | solution.py:255
  154.7 12.1 %collective-permute-start.30 = (bf16[256,512]{1,0:T(8,128)(2,1)S(1)}, bf16[256,512]{1,0:T(8,128)(2,1)S(1)}, u32[]{:S(2)}, u32[]{:S(2)}) collective-permute-start(bf16[256,512]{1,0:T(8,128)(2,1)S(1)} %get-tuple-element.57), channel_id=1, source_target_pairs={{0,2},{1,3},{2,0},{3,1},{4,5},{5,4},{6,7},{7,6},{8,10},{9,11},{10,... | collective-permute-start | bytes 786440 | tf_op jit(solution)/shard_map/ppermute | solution.py:255
  161.2 11.6 %collective-permute-start.44 = (bf16[256,512]{1,0:T(8,128)(2,1)S(1)}, bf16[256,512]{1,0:T(8,128)(2,1)S(1)}, u32[]{:S(2)}, u32[]{:S(2)}) collective-permute-start(bf16[256,512]{1,0:T(8,128)(2,1)S(1)} %get-tuple-element.76), channel_id=1, source_target_pairs={{0,2},{1,3},{2,0},{3,1},{4,5},{5,4},{6,7},{7,6},{8,10},{9,11},{10,... | collective-permute-start | bytes 786440 | tf_op jit(solution)/shard_map/ppermute | solution.py:255
  166.8 17.3 %collective-permute-start.31 = (bf16[256,512]{1,0:T(8,128)(2,1)S(1)}, bf16[256,512]{1,0:T(8,128)(2,1)S(1)}, u32[]{:S(2)}, u32[]{:S(2)}) collective-permute-start(bf16[256,512]{1,0:T(8,128)(2,1)S(1)} %add_convert_fusion.7), channel_id=1, source_target_pairs={{0,1},{1,0},{2,3},{3,2},{4,6},{5,7},{6,4},{7,5},{8,9},{9,8},{10,11... | collective-permute-start | bytes 786440 | tf_op jit(solution)/shard_map/ppermute | solution.py:255
  171.4 13.0 %collective-permute-start.43 = (bf16[256,512]{1,0:T(8,128)(2,1)S(1)}, bf16[256,512]{1,0:T(8,128)(2,1)S(1)}, u32[]{:S(2)}, u32[]{:S(2)}) collective-permute-start(bf16[256,512]{1,0:T(8,128)(2,1)S(1)} %get-tuple-element.73), channel_id=1, source_target_pairs={{0,2},{1,3},{2,0},{3,1},{4,5},{5,4},{6,7},{7,6},{8,10},{9,11},{10,... | collective-permute-start | bytes 786440 | tf_op jit(solution)/shard_map/ppermute | solution.py:255
  172.9 16.5 %collective-permute-start.45 = (bf16[256,512]{1,0:T(8,128)(2,1)S(1)}, bf16[256,512]{1,0:T(8,128)(2,1)S(1)}, u32[]{:S(2)}, u32[]{:S(2)}) collective-permute-start(bf16[256,512]{1,0:T(8,128)(2,1)S(1)} %add_convert_fusion.3), channel_id=1, source_target_pairs={{0,1},{1,0},{2,3},{3,2},{4,6},{5,7},{6,4},{7,5},{8,9},{9,8},{10,11... | collective-permute-start | bytes 786440 | tf_op jit(solution)/shard_map/ppermute | solution.py:255
  (4 other events, 3.7 us)

commit v4 on v3

--- a/solution.py
+++ b/solution.py
@@ -167,17 +167,15 @@
     core, base = where_am_i(bits)
     rows, width = own[0].shape
     depth = outs[0].shape[1]
-    pairs = plane_pairs(own, other, room, core, rows, bits) + list(zip((keep, came), halves(given, core)))
-    for copy in copy_all(pairs, sems):
-        copy.wait()
-    copies = []
-    for l in range(n - 1, -1, -1):
-        right = room[pl.ds(pl.multiple_of((base ^ l) * depth, depth), depth), :]
-        results[l] = lax.dot_general(given[...], right, (((1,), (1,)), ((), ())), preferred_element_type=F32).astype(BF16)
-        copy = pltpu.make_async_copy(results.at[l], outs[l], out_sems.at[l])
-        copy.start()
-        copies.append(copy)
-    for copy in copies:
+    loads = copy_all(list(zip((keep, came), halves(given, core))) + plane_pairs(own, other, room, core, rows, bits), sems)
+    for copy in loads[:2]:
+        copy.wait()
+    for j in range(n):
+        loads[2 + j].wait()
+        loads[2 + n + flipped(j, bits)].wait()
+        right = room[pl.ds(j * depth, depth), :]
+        results[base ^ j] = lax.dot_general(given[...], right, (((1,), (1,)), ((), ())), preferred_element_type=F32).astype(BF16)
+    for copy in copy_all([(results.at[l], outs[l]) for l in range(n)], out_sems):
         copy.wait()
 
 
@@ -285,14 +283,14 @@
     line_own = gather(factor, line, chained=True)
     cols_own = gather(factor, plane)
     kernel_own, kernel_away = column_halves(kernel)
-    kernel_other = swap(kernel_away)
+    kernel_other = swap(after(kernel_away, line_own[1]))
     cols_other = [swap(b) for b in cols_own]
     terms = [gather(amplitudes[0], line, [[line_own[-1]]] * bits)]
     terms.append(gather(amplitudes[1], line, [[terms[0][1]]] * bits))
 
     pieces = pick(line_own, bits)
     first_own = [pieces[0]] + [in_plane(j)(pieces[j]) for j in range(1, chips)]
-    first_other = [swap(b) for b in first_own]
+    first_other = [swap(after(b, terms[1][-1])) for b in first_own]
 
     gates, results, marks, outs = first_own[1:], [], [None, None], ()
     for pair in range(amplitudes.shape[0]):

time: 192 us -> 191 us (level)
  waiting for transfers between devices: 85.5 us -> 111 us
  starting transfers between devices: 70.9 us -> 46.8 us
  Pallas kernels: 25.5 us -> 23.4 us
    ppermute x15, waiting for transfers between devices: 51.9 us -> 74.1 us  [in_line(): return lambda value: lax.ppermute(value, ('row', 'col'), pairs)]
    ppermute x15, starting transfers between devices: 38.4 us -> 22.7 us  [in_line(): return lambda value: lax.ppermute(value, ('row', 'col'), pairs)]
    ppermute x18, starting transfers between devices: 26.7 us -> 21.7 us  [in_plane(): lax.ppermute(value, 'row', [(r, r ^ 2 * distance(r, mask)) for r in range...]
    ppermute x13, starting transfers between devices: 5.83 us -> 2.3 us  [swap(): return lax.ppermute(value, 'row', [(r, r ^ 1) for r in range(rows)])]
    ppermute x18, waiting for transfers between devices: 30.9 us -> 33.2 us  [in_plane(): lax.ppermute(value, 'row', [(r, r ^ 2 * distance(r, mask)) for r in range...]
    pallas_call x2, Pallas kernels: 6.79 us -> 4.79 us  [back(): pl.pallas_call(functools.partial(back_kernel, bits), out_shape=[jax.Shape...]
  transfers between devices with their start and end apart: 46 -> 46, of which waited for: 22 -> 23; matrix products, arithmetic and copies ran while one was open for 2% -> 2% of each run, Pallas kernels for 13% -> 12%
where the time goes in v4:
time: 191 us
  waiting for transfers between devices  111 us (58%)
  starting transfers between devices  46.8 us (25%)
  Pallas kernels  23.4 us (12%)
  local copies, waits for them, and re-layouts  7.11 us (4%)
    ppermute x15, waiting for transfers between devices, in_line(): return lambda value: lax.ppermute(value, ('row', 'col'), pairs)  74.1 us
    ppermute x18, waiting for transfers between devices, in_plane(): lax.ppermute(value, 'row', [(r, r ^ 2 * distance(r, mask)) for r in range...  33.2 us
    ppermute x15, starting transfers between devices, in_line(): return lambda value: lax.ppermute(value, ('row', 'col'), pairs)  22.7 us
    ppermute x18, starting transfers between devices, in_plane(): lax.ppermute(value, 'row', [(r, r ^ 2 * distance(r, mask)) for r in range...  21.7 us
    pallas_call x2, Pallas kernels, grid(): pl.pallas_call(functools.partial(grid_kernel, bits), out_shape=[jax.Shape...  12.9 us
    pallas_call x2, Pallas kernels, back(): pl.pallas_call(functools.partial(back_kernel, bits), out_shape=[jax.Shape...  4.79 us
    pallas_call x2, Pallas kernels, project(): pl.pallas_call(functools.partial(project_kernel, bits), out_shape=[jax.Sh...  4.74 us
    ppermute x13, waiting for transfers between devices, swap(): return lax.ppermute(value, 'row', [(r, r ^ 1) for r in range(rows)])  4.2 us
  transfers between devices with their start and end apart: 46, of which 23 were waited for; matrix products, arithmetic and copies ran while one was open for 2% of the time, Pallas kernels for 12%

profile of v4, /device:TPU:0, one launch (start us, length us, event | category | flops | bytes accessed | tf_op | source)
XLA Modules:
  0.0 190.9 jit_solution(9854166940725844589)
XLA Ops:
  0.0 3.0 %collective-permute-start = (bf16[256,1024]{1,0:T(8,128)(2,1)}, bf16[256,1024]{1,0:T(8,128)(2,1)S(1)}, u32[]{:S(2)}, u32[]{:S(2)}) collective-permute-start(bf16[256,1024]{1,0:T(8,128)(2,1)} %refs_2_.3), channel_id=1, source_target_pairs={{0,1},{1,0},{2,3},{3,2},{4,6},{5,7},{6,4},{7,5},{8,9},{9,8},{10,11... | collective-permute-start | bytes 1572872 | tf_op jit(solution)/shard_map/ppermute | solution.py:253
  3.0 2.6 %collective-permute-start.1 = (bf16[256,1024]{1,0:T(8,128)(2,1)}, bf16[256,1024]{1,0:T(8,128)(2,1)S(1)}, u32[]{:S(2)}, u32[]{:S(2)}) collective-permute-start(bf16[256,1024]{1,0:T(8,128)(2,1)} %refs_2_.3), channel_id=1, source_target_pairs={{0,2},{1,3},{2,0},{3,1},{4,5},{5,4},{6,7},{7,6},{8,10},{9,11},{10,... | collective-permute-start | bytes 1572872 | tf_op jit(solution)/shard_map/ppermute | solution.py:253
  5.6 1.5 collective-permute-start.6
  7.1 1.5 collective-permute-start.7
  8.6 18.1 %collective-permute-done.refs_1_ = bf16[256,1024]{1,0:T(8,128)(2,1)S(1)} collective-permute-done((bf16[256,1024]{1,0:T(8,128)(2,1)}, bf16[256,1024]{1,0:T(8,128)(2,1)S(1)}, u32[]{:S(2)}, u32[]{:S(2)}) %collective-permute-start) | collective-permute-done | bytes 524320 | tf_op jit(solution)/shard_map/ppermute | solution.py:253
  26.8 3.3 %collective-permute-start.2 = (bf16[256,1024]{1,0:T(8,128)(2,1)S(1)}, bf16[256,1024]{1,0:T(8,128)(2,1)S(1)}, u32[]{:S(2)}, u32[]{:S(2)}) collective-permute-start(bf16[256,1024]{1,0:T(8,128)(2,1)S(1)} %collective-permute-done.refs_1_), channel_id=1, source_target_pairs={{0,2},{1,3},{2,0},{3,1},{4,5},{5,4},{6,7},{7,6},{8,10},{9,11},{10,... | collective-permute-start | bytes 1572872 | tf_op jit(solution)/shard_map/ppermute | solution.py:253
  30.0 1.5 collective-permute-start.8
  32.1 1.8 slice_bitcast_fusion.1
  33.8 9.0 %collective-permute-done.2.refs_3_ = bf16[256,1024]{1,0:T(8,128)(2,1)S(1)} collective-permute-done((bf16[256,1024]{1,0:T(8,128)(2,1)S(1)}, bf16[256,1024]{1,0:T(8,128)(2,1)S(1)}, u32[]{:S(2)}, u32[]{:S(2)}) %collective-permute-start.2) | collective-permute-done | bytes 524320 | tf_op jit(solution)/shard_map/ppermute | solution.py:253
  48.2 1.5 collective-permute-start.14
  49.7 3.4 %collective-permute-start.4 = (bf16[256,512]{1,0:T(8,128)(2,1)}, bf16[256,512]{1,0:T(8,128)(2,1)}, u32[]{:S(2)}, u32[]{:S(2)}) collective-permute-start(bf16[256,512]{1,0:T(8,128)(2,1)} %get-tuple-element.47.refs_0_), channel_id=1, source_target_pairs={{0,2},{1,3},{2,0},{3,1},{4,5},{5,4},{6,7},{7,6},{8,10},{9,11},{10,... | collective-permute-start | bytes 786440 | tf_op jit(solution)/shard_map/ppermute | solution.py:253
  53.1 1.3 collective-permute-start.5
  54.4 1.8 constant_dynamic-slice_fusion
  56.2 1.8 collective-permute-start.15
  58.0 2.3 %collective-permute-done.4.refs_2_ = bf16[256,512]{1,0:T(8,128)(2,1)} collective-permute-done((bf16[256,512]{1,0:T(8,128)(2,1)}, bf16[256,512]{1,0:T(8,128)(2,1)}, u32[]{:S(2)}, u32[]{:S(2)}) %collective-permute-start.4) | collective-permute-done | bytes 262176 | tf_op jit(solution)/shard_map/ppermute | solution.py:253
  60.3 1.4 collective-permute-start.16
  62.9 7.0 %collective-permute-done.5.refs_3_ = bf16[256,512]{1,0:T(8,128)(2,1)} collective-permute-done((bf16[256,512]{1,0:T(8,128)(2,1)}, bf16[256,512]{1,0:T(8,128)(2,1)}, u32[]{:S(2)}, u32[]{:S(2)}) %collective-permute-start.5) | collective-permute-done | bytes 262176 | tf_op jit(solution)/shard_map/ppermute | solution.py:253
  69.8 2.8 %project.2 = (bf16[256,512]{1,0:T(8,128)(2,1)S(1)}, bf16[256,512]{1,0:T(8,128)(2,1)S(1)}) custom-call(bf16[256,512]{1,0:T(8,128)(2,1)} %get-tuple-element.47.refs_0_, bf16[256,512]{1,0:T(8,128)(2,1)} %collective-permute-done.3.refs_1_, bf16[256,512]{1,0:T(8,128)(2,1)} %collective-permute-done.4.refs_2_, bf16[256,512]{1,0:T(8,128)(2,1)} %collective-permute-done.5.refs_3_, ...), custom_call_target="tpu_custom_call" | custom-call | flops 1 | bytes 1 | tf_op jit(solution)/shard_map/project/pallas_call | solution.py:81
  73.2 1.2 collective-permute-done.13
  74.4 1.8 collective-permute-start.34
  76.7 1.5 collective-permute-start.17
  78.2 1.7 collective-permute-start.18
  79.9 3.4 %collective-permute-done.21.refs_3_ = bf16[256,512]{1,0:T(8,128)(2,1)S(1)} collective-permute-done((bf16[256,512]{1,0:T(8,128)(2,1)S(1)}, bf16[256,512]{1,0:T(8,128)(2,1)S(1)}, u32[]{:S(2)}, u32[]{:S(2)}) %collective-permute-start.21) | collective-permute-done | bytes 262176 | tf_op jit(solution)/shard_map/ppermute | solution.py:253
  83.3 5.1 %collective-permute-done.34.refs_2_ = bf16[256,512]{1,0:T(8,128)(2,1)S(1)} collective-permute-done((bf16[256,512]{1,0:T(8,128)(2,1)S(1)}, bf16[256,512]{1,0:T(8,128)(2,1)S(1)}, u32[]{:S(2)}, u32[]{:S(2)}) %collective-permute-start.34) | collective-permute-done | bytes 262176 | tf_op jit(solution)/shard_map/ppermute | solution.py:253
  88.4 2.0 %project.3 = (bf16[256,512]{1,0:T(8,128)(2,1)S(1)}, bf16[256,512]{1,0:T(8,128)(2,1)S(1)}) custom-call(bf16[256,512]{1,0:T(8,128)(2,1)S(1)} %get-tuple-element.55.refs_0_, bf16[256,512]{1,0:T(8,128)(2,1)S(1)} %collective-permute-done.20.refs_1_, bf16[256,512]{1,0:T(8,128)(2,1)S(1)} %collective-permute-done.34.refs_2_, ...), custom_call_target="tpu_custom_call" | custom-call | flops 1 | bytes 1 | tf_op jit(solution)/shard_map/project/pallas_call | solution.py:81
  90.4 1.5 collective-permute-done.35
  94.7 1.2 collective-permute-start.37
  95.8 11.2 %collective-permute-done.36.refs_1_ = bf16[512,512]{1,0:T(8,128)(2,1)S(1)} collective-permute-done((bf16[512,512]{1,0:T(8,128)(2,1)S(1)}, bf16[512,512]{1,0:T(8,128)(2,1)S(1)}, u32[]{:S(2)}, u32[]{:S(2)}) %collective-permute-start.36) | collective-permute-done | bytes 524320 | tf_op jit(solution)/shard_map/ppermute | solution.py:249
  107.0 1.5 collective-permute-start.38
  108.5 6.4 %grid.2 = (bf16[512,512]{1,0:T(8,128)(2,1)S(1)}, bf16[512,512]{1,0:T(8,128)(2,1)S(1)}, bf16[512,512]{1,0:T(8,128)(2,1)S(1)}, bf16[512,512]{1,0:T(8,128)(2,1)S(1)}) custom-call(bf16[512,512]{1,0:T(8,128)(2,1)S(1)} %constant_dynamic-update-slice_fusion.refs_0_, bf16[512,512]{1,0:T(8,128)(2,1)S(1)} %collective-permute-done.17.refs_1_, ...), custom_call_target="tpu_custom_call" | custom-call | flops 1 | bytes 1 | tf_op jit(solution)/shard_map/grid/pallas_call | solution.py:139
  115.5 1.5 collective-permute-start.28
  117.7 6.5 %grid.3 = (bf16[512,512]{1,0:T(8,128)(2,1)S(1)}, bf16[512,512]{1,0:T(8,128)(2,1)S(1)}, bf16[512,512]{1,0:T(8,128)(2,1)S(1)}, bf16[512,512]{1,0:T(8,128)(2,1)S(1)}) custom-call(bf16[512,512]{1,0:T(8,128)(2,1)S(1)} %constant_dynamic-update-slice_fusion.2.refs_0_, bf16[512,512]{1,0:T(8,128)(2,1)S(1)} %collective-permute-done.36.refs_1_, ...), custom_call_target="tpu_custom_call" | custom-call | flops 1 | bytes 1 | tf_op jit(solution)/shard_map/grid/pallas_call | solution.py:139
  124.3 1.4 collective-permute-start.40
  125.7 4.0 %collective-permute-done.28 = bf16[512,512]{1,0:T(8,128)(2,1)S(1)} collective-permute-done((bf16[512,512]{1,0:T(8,128)(2,1)S(1)}, bf16[512,512]{1,0:T(8,128)(2,1)S(1)}, u32[]{:S(2)}, u32[]{:S(2)}) %collective-permute-start.28) | collective-permute-done | bytes 524320 | tf_op jit(solution)/shard_map/ppermute | solution.py:249
  130.1 1.1 collective-permute-start.39
  131.2 6.8 %collective-permute-done.40 = bf16[512,512]{1,0:T(8,128)(2,1)S(1)} collective-permute-done((bf16[512,512]{1,0:T(8,128)(2,1)S(1)}, bf16[512,512]{1,0:T(8,128)(2,1)S(1)}, u32[]{:S(2)}, u32[]{:S(2)}) %collective-permute-start.40) | collective-permute-done | bytes 524320 | tf_op jit(solution)/shard_map/ppermute | solution.py:249
  138.2 6.6 %collective-permute-done.29 = bf16[512,512]{1,0:T(8,128)(2,1)S(1)} collective-permute-done((bf16[512,512]{1,0:T(8,128)(2,1)S(1)}, bf16[512,512]{1,0:T(8,128)(2,1)S(1)}, u32[]{:S(2)}, u32[]{:S(2)}) %collective-permute-start.29) | collective-permute-done | bytes 524320 | tf_op jit(solution)/shard_map/ppermute | solution.py:249
  145.1 1.5 collective-permute-done.30.refs_1_
  146.6 2.4 %back.2 = (bf16[256,512]{1,0:T(8,128)(2,1)S(1)}, bf16[256,512]{1,0:T(8,128)(2,1)S(1)}, bf16[256,512]{1,0:T(8,128)(2,1)S(1)}, bf16[256,512]{1,0:T(8,128)(2,1)S(1)}) custom-call(bf16[256,512]{1,0:T(8,128)(2,1)S(1)} %get-tuple-element.92.refs_0_, bf16[256,512]{1,0:T(8,128)(2,1)S(1)} %collective-permute-done.30.refs_1_, bf16[256,1024]{1,0:T(8,128)(2,1)S(1)} %copy-done.1, ...), custom_call_target="tpu_custom_call" | custom-call | flops 1 | bytes 1 | tf_op jit(solution)/shard_map/back/pallas_call | solution.py:186
  149.2 3.1 %collective-permute-done.41 = bf16[512,512]{1,0:T(8,128)(2,1)S(1)} collective-permute-done((bf16[512,512]{1,0:T(8,128)(2,1)S(1)}, bf16[512,512]{1,0:T(8,128)(2,1)S(1)}, u32[]{:S(2)}, u32[]{:S(2)}) %collective-permute-start.41) | collective-permute-done | bytes 524320 | tf_op jit(solution)/shard_map/ppermute | solution.py:249
  152.7 2.9 %collective-permute-start.32 = (bf16[256,512]{1,0:T(8,128)(2,1)S(1)}, bf16[256,512]{1,0:T(8,128)(2,1)S(1)}, u32[]{:S(2)}, u32[]{:S(2)}) collective-permute-start(bf16[256,512]{1,0:T(8,128)(2,1)S(1)} %get-tuple-element.68), channel_id=1, source_target_pairs={{0,2},{1,3},{2,0},{3,1},{4,5},{5,4},{6,7},{7,6},{8,10},{9,11},{10,... | collective-permute-start | bytes 786440 | tf_op jit(solution)/shard_map/ppermute | solution.py:253
  155.6 2.4 %back.3 = (bf16[256,512]{1,0:T(8,128)(2,1)S(1)}, bf16[256,512]{1,0:T(8,128)(2,1)S(1)}, bf16[256,512]{1,0:T(8,128)(2,1)S(1)}, bf16[256,512]{1,0:T(8,128)(2,1)S(1)}) custom-call(bf16[256,512]{1,0:T(8,128)(2,1)S(1)} %get-tuple-element.90.refs_0_, bf16[256,512]{1,0:T(8,128)(2,1)S(1)} %collective-permute-done.42.refs_1_, bf16[256,1024]{1,0:T(8,128)(2,1)S(1)} %copy-done.1, ...), custom_call_target="tpu_custom_call" | custom-call | flops 1 | bytes 1 | tf_op jit(solution)/shard_map/back/pallas_call | solution.py:186
  158.0 4.8 %collective-permute-done.31 = bf16[256,512]{1,0:T(8,128)(2,1)S(1)} collective-permute-done((bf16[256,512]{1,0:T(8,128)(2,1)S(1)}, bf16[256,512]{1,0:T(8,128)(2,1)S(1)}, u32[]{:S(2)}, u32[]{:S(2)}) %collective-permute-start.31) | collective-permute-done | bytes 262176 | tf_op jit(solution)/shard_map/ppermute | solution.py:253
  162.7 5.6 %collective-permute-done.32 = bf16[256,512]{1,0:T(8,128)(2,1)S(1)} collective-permute-done((bf16[256,512]{1,0:T(8,128)(2,1)S(1)}, bf16[256,512]{1,0:T(8,128)(2,1)S(1)}, u32[]{:S(2)}, u32[]{:S(2)}) %collective-permute-start.32) | collective-permute-done | bytes 262176 | tf_op jit(solution)/shard_map/ppermute | solution.py:253
  168.5 2.3 %collective-permute-start.43 = (bf16[256,512]{1,0:T(8,128)(2,1)S(1)}, bf16[256,512]{1,0:T(8,128)(2,1)S(1)}, u32[]{:S(2)}, u32[]{:S(2)}) collective-permute-start(bf16[256,512]{1,0:T(8,128)(2,1)S(1)} %get-tuple-element.83), channel_id=1, source_target_pairs={{0,2},{1,3},{2,0},{3,1},{4,5},{5,4},{6,7},{7,6},{8,10},{9,11},{10,... | collective-permute-start | bytes 786440 | tf_op jit(solution)/shard_map/ppermute | solution.py:253
  170.8 7.9 %collective-permute-done.44 = bf16[256,512]{1,0:T(8,128)(2,1)S(1)} collective-permute-done((bf16[256,512]{1,0:T(8,128)(2,1)S(1)}, bf16[256,512]{1,0:T(8,128)(2,1)S(1)}, u32[]{:S(2)}, u32[]{:S(2)}) %collective-permute-start.44) | collective-permute-done | bytes 262176 | tf_op jit(solution)/shard_map/ppermute | solution.py:253
  178.9 3.4 %collective-permute-done.33 = bf16[256,512]{1,0:T(8,128)(2,1)S(1)} collective-permute-done((bf16[256,512]{1,0:T(8,128)(2,1)S(1)}, bf16[256,512]{1,0:T(8,128)(2,1)S(1)}, u32[]{:S(2)}, u32[]{:S(2)}) %collective-permute-start.33) | collective-permute-done | bytes 262176 | tf_op jit(solution)/shard_map/ppermute | solution.py:253
  182.4 7.5 %collective-permute-done.43 = bf16[256,512]{1,0:T(8,128)(2,1)S(1)} collective-permute-done((bf16[256,512]{1,0:T(8,128)(2,1)S(1)}, bf16[256,512]{1,0:T(8,128)(2,1)S(1)}, u32[]{:S(2)}, u32[]{:S(2)}) %collective-permute-start.43) | collective-permute-done | bytes 262176 | tf_op jit(solution)/shard_map/ppermute | solution.py:253
  (82 shorter events, 14.9 us)
Async XLA Ops:
  0.0 26.7 %collective-permute-start = (bf16[256,1024]{1,0:T(8,128)(2,1)}, bf16[256,1024]{1,0:T(8,128)(2,1)S(1)}, u32[]{:S(2)}, u32[]{:S(2)}) collective-permute-start(bf16[256,1024]{1,0:T(8,128)(2,1)} %refs_2_.3), channel_id=1, source_target_pairs={{0,1},{1,0},{2,3},{3,2},{4,6},{5,7},{6,4},{7,5},{8,9},{9,8},{10,11... | collective-permute-start | bytes 1572872 | tf_op jit(solution)/shard_map/ppermute | solution.py:253
  3.0 23.7 %collective-permute-start.1 = (bf16[256,1024]{1,0:T(8,128)(2,1)}, bf16[256,1024]{1,0:T(8,128)(2,1)S(1)}, u32[]{:S(2)}, u32[]{:S(2)}) collective-permute-start(bf16[256,1024]{1,0:T(8,128)(2,1)} %refs_2_.3), channel_id=1, source_target_pairs={{0,2},{1,3},{2,0},{3,1},{4,5},{5,4},{6,7},{7,6},{8,10},{9,11},{10,... | collective-permute-start | bytes 1572872 | tf_op jit(solution)/shard_map/ppermute | solution.py:253
  5.6 24.4 %collective-permute-start.6 = (bf16[256,1024]{1,0:T(8,128)(2,1)}, bf16[256,1024]{1,0:T(8,128)(2,1)S(1)}, u32[]{:S(2)}, u32[]{:S(2)}) collective-permute-start(bf16[256,1024]{1,0:T(8,128)(2,1)} %refs_2_.3), channel_id=1, source_target_pairs={{0,8},{4,20},{8,0},{12,28},{16,24},{20,4},{24,16},{28,12},{1,9},{5... | collective-permute-start | bytes 1572872 | tf_op jit(solution)/shard_map/ppermute | solution.py:249
  7.1 25.0 %collective-permute-start.7 = (bf16[256,1024]{1,0:T(8,128)(2,1)}, bf16[256,1024]{1,0:T(8,128)(2,1)S(1)}, u32[]{:S(2)}, u32[]{:S(2)}) collective-permute-start(bf16[256,1024]{1,0:T(8,128)(2,1)} %refs_2_.3), channel_id=1, source_target_pairs={{0,16},{4,12},{8,24},{12,4},{16,0},{20,28},{24,8},{28,20},{1,17},{... | collective-permute-start | bytes 1572872 | tf_op jit(solution)/shard_map/ppermute | solution.py:249
  26.8 16.1 %collective-permute-start.2 = (bf16[256,1024]{1,0:T(8,128)(2,1)S(1)}, bf16[256,1024]{1,0:T(8,128)(2,1)S(1)}, u32[]{:S(2)}, u32[]{:S(2)}) collective-permute-start(bf16[256,1024]{1,0:T(8,128)(2,1)S(1)} %collective-permute-done.refs_1_), channel_id=1, source_target_pairs={{0,2},{1,3},{2,0},{3,1},{4,5},{5,4},{6,7},{7,6},{8,10},{9,11},{10,... | collective-permute-start | bytes 1572872 | tf_op jit(solution)/shard_map/ppermute | solution.py:253
  30.0 12.8 %collective-permute-start.8 = (bf16[256,1024]{1,0:T(8,128)(2,1)S(1)}, bf16[256,1024]{1,0:T(8,128)(2,1)S(1)}, u32[]{:S(2)}, u32[]{:S(2)}) collective-permute-start(bf16[256,1024]{1,0:T(8,128)(2,1)S(1)} %collective-permute-done.6.refs_5_.refs_3_), channel_id=1, source_target_pairs={{0,16},{4,12},{8,24},{12,4},{16,0},{20,28},{24,8},{28,20},{1,17},{... | collective-permute-start | bytes 1572872 | tf_op jit(solution)/shard_map/ppermute | solution.py:249
  31.6 16.6 %collective-permute-start.9 = (bf16[256,1024]{1,0:T(8,128)(2,1)}, bf16[256,1024]{1,0:T(8,128)(2,1)S(1)}, u32[]{:S(2)}, u32[]{:S(2)}) collective-permute-start(bf16[256,1024]{1,0:T(8,128)(2,1)} %refs_2_.3), channel_id=1, source_target_pairs={{0,4},{4,0},{8,12},{12,8},{16,20},{20,16},{24,28},{28,24},{1,5},{5... | collective-permute-start | bytes 1572872 | tf_op jit(solution)/shard_map/ppermute | solution.py:246
  31.6 18.1 %collective-permute-start.10 = (bf16[256,1024]{1,0:T(8,128)(2,1)S(1)}, bf16[256,1024]{1,0:T(8,128)(2,1)S(1)}, u32[]{:S(2)}, u32[]{:S(2)}) collective-permute-start(bf16[256,1024]{1,0:T(8,128)(2,1)S(1)} %collective-permute-done.6.refs_5_.refs_3_), channel_id=1, source_target_pairs={{0,4},{4,0},{8,12},{12,8},{16,20},{20,16},{24,28},{28,24},{1,5},{5... | collective-permute-start | bytes 1572872 | tf_op jit(solution)/shard_map/ppermute | solution.py:246
  32.1 24.1 %collective-permute-start.11 = (bf16[256,1024]{1,0:T(8,128)(2,1)S(1)}, bf16[256,1024]{1,0:T(8,128)(2,1)S(1)}, u32[]{:S(2)}, u32[]{:S(2)}) collective-permute-start(bf16[256,1024]{1,0:T(8,128)(2,1)S(1)} %collective-permute-done.7.refs_6_.refs_4_), channel_id=1, source_target_pairs={{0,4},{4,0},{8,12},{12,8},{16,20},{20,16},{24,28},{28,24},{1,5},{5... | collective-permute-start | bytes 1572872 | tf_op jit(solution)/shard_map/ppermute | solution.py:246
  42.9 18.9 %collective-permute-start.12 = (bf16[256,1024]{1,0:T(8,128)(2,1)S(1)}, bf16[256,1024]{1,0:T(8,128)(2,1)}, u32[]{:S(2)}, u32[]{:S(2)}) collective-permute-start(bf16[256,1024]{1,0:T(8,128)(2,1)S(1)} %collective-permute-done.8.refs_7_.refs_5_), channel_id=1, source_target_pairs={{0,4},{4,0},{8,12},{12,8},{16,20},{20,16},{24,28},{28,24},{1,5},{5... | collective-permute-start | bytes 1572872 | tf_op jit(solution)/shard_map/ppermute | solution.py:246
  42.9 10.2 %collective-permute-start.3 = (bf16[256,512]{1,0:T(8,128)(2,1)}, bf16[256,512]{1,0:T(8,128)(2,1)}, u32[]{:S(2)}, u32[]{:S(2)}) collective-permute-start(bf16[256,512]{1,0:T(8,128)(2,1)} %get-tuple-element.47.refs_0_), channel_id=1, source_target_pairs={{0,1},{1,0},{2,3},{3,2},{4,6},{5,7},{6,4},{7,5},{8,9},{9,8},{10,11... | collective-permute-start | bytes 786440 | tf_op jit(solution)/shard_map/ppermute | solution.py:253
  48.2 24.4 %collective-permute-start.14 = (bf16[256,1024]{1,0:T(8,128)(2,1)}, bf16[256,1024]{1,0:T(8,128)(2,1)}, u32[]{:S(2)}, u32[]{:S(2)}) collective-permute-start(bf16[256,1024]{1,0:T(8,128)(2,1)} %get-tuple-element.50), channel_id=1, source_target_pairs={{0,8},{4,20},{8,0},{12,28},{16,24},{20,4},{24,16},{28,12},{1,9},{5... | collective-permute-start | bytes 1572872 | tf_op jit(solution)/shard_map/ppermute | solution.py:249
  49.7 10.7 %collective-permute-start.4 = (bf16[256,512]{1,0:T(8,128)(2,1)}, bf16[256,512]{1,0:T(8,128)(2,1)}, u32[]{:S(2)}, u32[]{:S(2)}) collective-permute-start(bf16[256,512]{1,0:T(8,128)(2,1)} %get-tuple-element.47.refs_0_), channel_id=1, source_target_pairs={{0,2},{1,3},{2,0},{3,1},{4,5},{5,4},{6,7},{7,6},{8,10},{9,11},{10,... | collective-permute-start | bytes 786440 | tf_op jit(solution)/shard_map/ppermute | solution.py:253
  53.1 16.8 %collective-permute-start.5 = (bf16[256,512]{1,0:T(8,128)(2,1)}, bf16[256,512]{1,0:T(8,128)(2,1)}, u32[]{:S(2)}, u32[]{:S(2)}) collective-permute-start(bf16[256,512]{1,0:T(8,128)(2,1)} %collective-permute-done.3.refs_1_), channel_id=1, source_target_pairs={{0,2},{1,3},{2,0},{3,1},{4,5},{5,4},{6,7},{7,6},{8,10},{9,11},{10,... | collective-permute-start | bytes 786440 | tf_op jit(solution)/shard_map/ppermute | solution.py:253
  54.4 15.4 %copy-start.1 = (bf16[256,1024]{1,0:T(8,128)(2,1)S(1)}, bf16[256,1024]{1,0:T(8,128)(2,1)}, u32[]{:S(2)}) copy-start(bf16[256,1024]{1,0:T(8,128)(2,1)} %refs_2_.3) | copy-start | bytes 1572868
  56.2 20.5 %collective-permute-start.15 = (bf16[256,1024]{1,0:T(8,128)(2,1)S(1)}, bf16[256,1024]{1,0:T(8,128)(2,1)S(1)}, u32[]{:S(2)}, u32[]{:S(2)}) collective-permute-start(bf16[256,1024]{1,0:T(8,128)(2,1)S(1)} %copy-done.7), channel_id=1, source_target_pairs={{0,16},{4,12},{8,24},{12,4},{16,0},{20,28},{24,8},{28,20},{1,17},{... | collective-permute-start | bytes 1572872 | tf_op jit(solution)/shard_map/ppermute | solution.py:249
  60.3 16.4 %collective-permute-start.16 = (bf16[256,1024]{1,0:T(8,128)(2,1)S(1)}, bf16[256,1024]{1,0:T(8,128)(2,1)S(1)}, u32[]{:S(2)}, u32[]{:S(2)}) collective-permute-start(bf16[256,1024]{1,0:T(8,128)(2,1)S(1)} %copy-done.5), channel_id=1, source_target_pairs={{0,24},{4,28},{8,16},{12,20},{16,8},{20,12},{24,0},{28,4},{1,25},{... | collective-permute-start | bytes 1572872 | tf_op jit(solution)/shard_map/ppermute | solution.py:249
  61.8 11.4 %collective-permute-start.20 = (bf16[256,512]{1,0:T(8,128)(2,1)S(1)}, bf16[256,512]{1,0:T(8,128)(2,1)S(1)}, u32[]{:S(2)}, u32[]{:S(2)}) collective-permute-start(bf16[256,512]{1,0:T(8,128)(2,1)S(1)} %get-tuple-element.55.refs_0_), channel_id=1, source_target_pairs={{0,1},{1,0},{2,3},{3,2},{4,6},{5,7},{6,4},{7,5},{8,9},{9,8},{10,11... | collective-permute-start | bytes 786440 | tf_op jit(solution)/shard_map/ppermute | solution.py:253
  69.8 23.6 %collective-permute-start.26 = (f32[512,512]{1,0:T(8,128)S(1)}, f32[512,512]{1,0:T(8,128)S(1)}, u32[]{:S(2)}, u32[]{:S(2)}) collective-permute-start(f32[512,512]{1,0:T(8,128)S(1)} %get-tuple-element.60), channel_id=1, source_target_pairs={{0,4},{4,0},{8,12},{12,8},{16,20},{20,16},{24,28},{28,24},{1,5},{5... | collective-permute-start | bytes 3145736 | tf_op jit(solution)/shard_map/ppermute | solution.py:246
  72.6 1.7 collective-permute-start.13
  73.2 10.1 %collective-permute-start.21 = (bf16[256,512]{1,0:T(8,128)(2,1)S(1)}, bf16[256,512]{1,0:T(8,128)(2,1)S(1)}, u32[]{:S(2)}, u32[]{:S(2)}) collective-permute-start(bf16[256,512]{1,0:T(8,128)(2,1)S(1)} %collective-permute-done.20.refs_1_), channel_id=1, source_target_pairs={{0,2},{1,3},{2,0},{3,1},{4,5},{5,4},{6,7},{7,6},{8,10},{9,11},{10,... | collective-permute-start | bytes 786440 | tf_op jit(solution)/shard_map/ppermute | solution.py:253
  74.4 14.0 %collective-permute-start.34 = (bf16[256,512]{1,0:T(8,128)(2,1)S(1)}, bf16[256,512]{1,0:T(8,128)(2,1)S(1)}, u32[]{:S(2)}, u32[]{:S(2)}) collective-permute-start(bf16[256,512]{1,0:T(8,128)(2,1)S(1)} %get-tuple-element.55.refs_0_), channel_id=1, source_target_pairs={{0,2},{1,3},{2,0},{3,1},{4,5},{5,4},{6,7},{7,6},{8,10},{9,11},{10,... | collective-permute-start | bytes 786440 | tf_op jit(solution)/shard_map/ppermute | solution.py:253
  76.2 17.3 %copy-start.3 = (bf16[256,1024]{1,0:T(8,128)(2,1)S(1)}, bf16[256,1024]{1,0:T(8,128)(2,1)}, u32[]{:S(2)}) copy-start(bf16[256,1024]{1,0:T(8,128)(2,1)} %copy-done.2) | copy-start | bytes 1572868
  76.7 15.4 %collective-permute-start.17 = (bf16[512,512]{1,0:T(8,128)(2,1)S(1)}, bf16[512,512]{1,0:T(8,128)(2,1)S(1)}, u32[]{:S(2)}, u32[]{:S(2)}) collective-permute-start(bf16[512,512]{1,0:T(8,128)(2,1)S(1)} %constant_dynamic-update-slice_fusion.refs_0_), channel_id=1, source_target_pairs={{0,8},{4,20},{8,0},{12,28},{16,24},{20,4},{24,16},{28,12},{1,9},{5... | collective-permute-start | bytes 1572872 | tf_op jit(solution)/shard_map/ppermute | solution.py:249
  78.2 14.3 %collective-permute-start.18 = (bf16[512,512]{1,0:T(8,128)(2,1)S(1)}, bf16[512,512]{1,0:T(8,128)(2,1)S(1)}, u32[]{:S(2)}, u32[]{:S(2)}) collective-permute-start(bf16[512,512]{1,0:T(8,128)(2,1)S(1)} %constant_dynamic-update-slice_fusion.refs_0_), channel_id=1, source_target_pairs={{0,16},{4,12},{8,24},{12,4},{16,0},{20,28},{24,8},{28,20},{1,17},{... | collective-permute-start | bytes 1572872 | tf_op jit(solution)/shard_map/ppermute | solution.py:249
  83.3 10.5 %collective-permute-start.23 = (bf16[256,1024]{1,0:T(8,128)(2,1)}, bf16[256,1024]{1,0:T(8,128)(2,1)S(1)}, u32[]{:S(2)}, u32[]{:S(2)}) collective-permute-start(bf16[256,1024]{1,0:T(8,128)(2,1)} %collective-permute-done.14.refs_5_), channel_id=1, source_target_pairs={{0,4},{4,0},{8,12},{12,8},{16,20},{20,16},{24,28},{28,24},{1,5},{5... | collective-permute-start | bytes 1572872 | tf_op jit(solution)/shard_map/ppermute | solution.py:246
  90.3 1.6 collective-permute-start.35
  91.9 2.7 %collective-permute-start.24 = (bf16[256,1024]{1,0:T(8,128)(2,1)S(1)}, bf16[256,1024]{1,0:T(8,128)(2,1)S(1)}, u32[]{:S(2)}, u32[]{:S(2)}) collective-permute-start(bf16[256,1024]{1,0:T(8,128)(2,1)S(1)} %collective-permute-done.15.refs_6_), channel_id=1, source_target_pairs={{0,4},{4,0},{8,12},{12,8},{16,20},{20,16},{24,28},{28,24},{1,5},{5... | collective-permute-start | bytes 1572872 | tf_op jit(solution)/shard_map/ppermute | solution.py:246
  92.1 16.4 %collective-permute-start.25 = (bf16[256,1024]{1,0:T(8,128)(2,1)S(1)}, bf16[256,1024]{1,0:T(8,128)(2,1)S(1)}, u32[]{:S(2)}, u32[]{:S(2)}) collective-permute-start(bf16[256,1024]{1,0:T(8,128)(2,1)S(1)} %collective-permute-done.16.refs_7_), channel_id=1, source_target_pairs={{0,4},{4,0},{8,12},{12,8},{16,20},{20,16},{24,28},{28,24},{1,5},{5... | collective-permute-start | bytes 1572872 | tf_op jit(solution)/shard_map/ppermute | solution.py:246
  92.5 14.5 %collective-permute-start.36 = (bf16[512,512]{1,0:T(8,128)(2,1)S(1)}, bf16[512,512]{1,0:T(8,128)(2,1)S(1)}, u32[]{:S(2)}, u32[]{:S(2)}) collective-permute-start(bf16[512,512]{1,0:T(8,128)(2,1)S(1)} %constant_dynamic-update-slice_fusion.2.refs_0_), channel_id=1, source_target_pairs={{0,8},{4,20},{8,0},{12,28},{16,24},{20,4},{24,16},{28,12},{1,9},{5... | collective-permute-start | bytes 1572872 | tf_op jit(solution)/shard_map/ppermute | solution.py:249
  93.4 15.1 %collective-permute-start.22 = (bf16[256,1024]{1,0:T(8,128)(2,1)S(1)}, bf16[256,1024]{1,0:T(8,128)(2,1)S(1)}, u32[]{:S(2)}, u32[]{:S(2)}) collective-permute-start(bf16[256,1024]{1,0:T(8,128)(2,1)S(1)} %copy-done.3), channel_id=1, source_target_pairs={{0,4},{4,0},{8,12},{12,8},{16,20},{20,16},{24,28},{28,24},{1,5},{5... | collective-permute-start | bytes 1572872 | tf_op jit(solution)/shard_map/ppermute | solution.py:246
  93.8 14.8 %collective-permute-start.19 = (bf16[512,512]{1,0:T(8,128)(2,1)S(1)}, bf16[512,512]{1,0:T(8,128)(2,1)S(1)}, u32[]{:S(2)}, u32[]{:S(2)}) collective-permute-start(bf16[512,512]{1,0:T(8,128)(2,1)S(1)} %collective-permute-done.17.refs_1_), channel_id=1, source_target_pairs={{0,16},{4,12},{8,24},{12,4},{16,0},{20,28},{24,8},{28,20},{1,17},{... | collective-permute-start | bytes 1572872 | tf_op jit(solution)/shard_map/ppermute | solution.py:249
  94.7 22.4 %collective-permute-start.37 = (bf16[512,512]{1,0:T(8,128)(2,1)S(1)}, bf16[512,512]{1,0:T(8,128)(2,1)S(1)}, u32[]{:S(2)}, u32[]{:S(2)}) collective-permute-start(bf16[512,512]{1,0:T(8,128)(2,1)S(1)} %constant_dynamic-update-slice_fusion.2.refs_0_), channel_id=1, source_target_pairs={{0,16},{4,12},{8,24},{12,4},{16,0},{20,28},{24,8},{28,20},{1,17},{... | collective-permute-start | bytes 1572872 | tf_op jit(solution)/shard_map/ppermute | solution.py:249
  107.0 10.7 %collective-permute-start.38 = (bf16[512,512]{1,0:T(8,128)(2,1)S(1)}, bf16[512,512]{1,0:T(8,128)(2,1)S(1)}, u32[]{:S(2)}, u32[]{:S(2)}) collective-permute-start(bf16[512,512]{1,0:T(8,128)(2,1)S(1)} %collective-permute-done.36.refs_1_), channel_id=1, source_target_pairs={{0,16},{4,12},{8,24},{12,4},{16,0},{20,28},{24,8},{28,20},{1,17},{... | collective-permute-start | bytes 1572872 | tf_op jit(solution)/shard_map/ppermute | solution.py:249
  114.9 9.4 %collective-permute-start.27 = (bf16[512,512]{1,0:T(8,128)(2,1)S(1)}, bf16[512,512]{1,0:T(8,128)(2,1)S(1)}, u32[]{:S(2)}, u32[]{:S(2)}) collective-permute-start(bf16[512,512]{1,0:T(8,128)(2,1)S(1)} %get-tuple-element.62), channel_id=1, source_target_pairs={{0,16},{4,12},{8,24},{12,4},{16,0},{20,28},{24,8},{28,20},{1,17},{... | collective-permute-start | bytes 1572872 | tf_op jit(solution)/shard_map/ppermute | solution.py:249
  115.5 14.3 %collective-permute-start.28 = (bf16[512,512]{1,0:T(8,128)(2,1)S(1)}, bf16[512,512]{1,0:T(8,128)(2,1)S(1)}, u32[]{:S(2)}, u32[]{:S(2)}) collective-permute-start(bf16[512,512]{1,0:T(8,128)(2,1)S(1)} %get-tuple-element.64), channel_id=1, source_target_pairs={{0,16},{4,12},{8,24},{12,4},{16,0},{20,28},{24,8},{28,20},{1,17},{... | collective-permute-start | bytes 1572872 | tf_op jit(solution)/shard_map/ppermute | solution.py:249
  124.3 13.7 %collective-permute-start.40 = (bf16[512,512]{1,0:T(8,128)(2,1)S(1)}, bf16[512,512]{1,0:T(8,128)(2,1)S(1)}, u32[]{:S(2)}, u32[]{:S(2)}) collective-permute-start(bf16[512,512]{1,0:T(8,128)(2,1)S(1)} %get-tuple-element.79), channel_id=1, source_target_pairs={{0,16},{4,12},{8,24},{12,4},{16,0},{20,28},{24,8},{28,20},{1,17},{... | collective-permute-start | bytes 1572872 | tf_op jit(solution)/shard_map/ppermute | solution.py:249
  129.9 14.9 %collective-permute-start.29 = (bf16[512,512]{1,0:T(8,128)(2,1)S(1)}, bf16[512,512]{1,0:T(8,128)(2,1)S(1)}, u32[]{:S(2)}, u32[]{:S(2)}) collective-permute-start(bf16[512,512]{1,0:T(8,128)(2,1)S(1)} %add_convert_fusion.1), channel_id=1, source_target_pairs={{0,8},{4,20},{8,0},{12,28},{16,24},{20,4},{24,16},{28,12},{1,9},{5... | collective-permute-start | bytes 1572872 | tf_op jit(solution)/shard_map/ppermute | solution.py:249
  130.1 19.2 %collective-permute-start.39 = (bf16[512,512]{1,0:T(8,128)(2,1)S(1)}, bf16[512,512]{1,0:T(8,128)(2,1)S(1)}, u32[]{:S(2)}, u32[]{:S(2)}) collective-permute-start(bf16[512,512]{1,0:T(8,128)(2,1)S(1)} %get-tuple-element.75), channel_id=1, source_target_pairs={{0,16},{4,12},{8,24},{12,4},{16,0},{20,28},{24,8},{28,20},{1,17},{... | collective-permute-start | bytes 1572872 | tf_op jit(solution)/shard_map/ppermute | solution.py:249
  138.1 14.2 %collective-permute-start.41 = (bf16[512,512]{1,0:T(8,128)(2,1)S(1)}, bf16[512,512]{1,0:T(8,128)(2,1)S(1)}, u32[]{:S(2)}, u32[]{:S(2)}) collective-permute-start(bf16[512,512]{1,0:T(8,128)(2,1)S(1)} %add_convert_fusion), channel_id=1, source_target_pairs={{0,8},{4,20},{8,0},{12,28},{16,24},{20,4},{24,16},{28,12},{1,9},{5... | collective-permute-start | bytes 1572872 | tf_op jit(solution)/shard_map/ppermute | solution.py:249
  145.0 1.6 collective-permute-start.30
  152.5 3.1 %collective-permute-start.42 = (bf16[256,512]{1,0:T(8,128)(2,1)S(1)}, bf16[256,512]{1,0:T(8,128)(2,1)S(1)}, u32[]{:S(2)}, u32[]{:S(2)}) collective-permute-start(bf16[256,512]{1,0:T(8,128)(2,1)S(1)} %get-tuple-element.89), channel_id=1, source_target_pairs={{0,4},{4,0},{8,12},{12,8},{16,20},{20,16},{24,28},{28,24},{1,5},{5... | collective-permute-start | bytes 786440 | tf_op jit(solution)/shard_map/ppermute | solution.py:246
  152.6 10.1 %collective-permute-start.31 = (bf16[256,512]{1,0:T(8,128)(2,1)S(1)}, bf16[256,512]{1,0:T(8,128)(2,1)S(1)}, u32[]{:S(2)}, u32[]{:S(2)}) collective-permute-start(bf16[256,512]{1,0:T(8,128)(2,1)S(1)} %get-tuple-element.66), channel_id=1, source_target_pairs={{0,2},{1,3},{2,0},{3,1},{4,5},{5,4},{6,7},{7,6},{8,10},{9,11},{10,... | collective-permute-start | bytes 786440 | tf_op jit(solution)/shard_map/ppermute | solution.py:253
  152.7 15.7 %collective-permute-start.32 = (bf16[256,512]{1,0:T(8,128)(2,1)S(1)}, bf16[256,512]{1,0:T(8,128)(2,1)S(1)}, u32[]{:S(2)}, u32[]{:S(2)}) collective-permute-start(bf16[256,512]{1,0:T(8,128)(2,1)S(1)} %get-tuple-element.68), channel_id=1, source_target_pairs={{0,2},{1,3},{2,0},{3,1},{4,5},{5,4},{6,7},{7,6},{8,10},{9,11},{10,... | collective-permute-start | bytes 786440 | tf_op jit(solution)/shard_map/ppermute | solution.py:253
  162.7 16.0 %collective-permute-start.44 = (bf16[256,512]{1,0:T(8,128)(2,1)S(1)}, bf16[256,512]{1,0:T(8,128)(2,1)S(1)}, u32[]{:S(2)}, u32[]{:S(2)}) collective-permute-start(bf16[256,512]{1,0:T(8,128)(2,1)S(1)} %get-tuple-element.86), channel_id=1, source_target_pairs={{0,2},{1,3},{2,0},{3,1},{4,5},{5,4},{6,7},{7,6},{8,10},{9,11},{10,... | collective-permute-start | bytes 786440 | tf_op jit(solution)/shard_map/ppermute | solution.py:253
  168.4 13.9 %collective-permute-start.33 = (bf16[256,512]{1,0:T(8,128)(2,1)S(1)}, bf16[256,512]{1,0:T(8,128)(2,1)S(1)}, u32[]{:S(2)}, u32[]{:S(2)}) collective-permute-start(bf16[256,512]{1,0:T(8,128)(2,1)S(1)} %add_convert_fusion.7), channel_id=1, source_target_pairs={{0,1},{1,0},{2,3},{3,2},{4,6},{5,7},{6,4},{7,5},{8,9},{9,8},{10,11... | collective-permute-start | bytes 786440 | tf_op jit(solution)/shard_map/ppermute | solution.py:253
  168.5 21.4 %collective-permute-start.43 = (bf16[256,512]{1,0:T(8,128)(2,1)S(1)}, bf16[256,512]{1,0:T(8,128)(2,1)S(1)}, u32[]{:S(2)}, u32[]{:S(2)}) collective-permute-start(bf16[256,512]{1,0:T(8,128)(2,1)S(1)} %get-tuple-element.83), channel_id=1, source_target_pairs={{0,2},{1,3},{2,0},{3,1},{4,5},{5,4},{6,7},{7,6},{8,10},{9,11},{10,... | collective-permute-start | bytes 786440 | tf_op jit(solution)/shard_map/ppermute | solution.py:253
  178.8 11.1 %collective-permute-start.45 = (bf16[256,512]{1,0:T(8,128)(2,1)S(1)}, bf16[256,512]{1,0:T(8,128)(2,1)S(1)}, u32[]{:S(2)}, u32[]{:S(2)}) collective-permute-start(bf16[256,512]{1,0:T(8,128)(2,1)S(1)} %add_convert_fusion.3), channel_id=1, source_target_pairs={{0,1},{1,0},{2,3},{3,2},{4,6},{5,7},{6,4},{7,5},{8,9},{9,8},{10,11... | collective-permute-start | bytes 786440 | tf_op jit(solution)/shard_map/ppermute | solution.py:253
  (6 other events, 11.2 us)
